TPU v7x, 32 devices: a whole 2x2x4 slice. The times are simulated.
32 devices in a mesh: seq: 16 (over z, x, core), tp: 2 (over y).
Axes of the slice: x: 2, y: 2, z: 4, core: 2. Of those that a mesh axis runs over, the one named last changes fastest.
Arguments:
- layer_input: bfloat16 [16384, 1024], P('seq'), may hold values from -6 to 6
- attn_gain: float32 [1024], replicated, may hold values from 0.5 to 1.5
- w_qkv: bfloat16 [1024, 3, 1024], P('seq', None, 'tp'), may hold values from -0.1875 to 0.1875
- w_out: bfloat16 [1024, 1024], P('tp', 'seq'), may hold values from -6 to 6
- mlp_gain: float32 [1024], replicated, may hold values from 0.5 to 1.5
- w_up: bfloat16 [1024, 4096], P('seq', 'tp'), may hold values from -0.1875 to 0.1875
- w_down: bfloat16 [4096, 1024], P('tp', 'seq'), may hold values from -0.09375 to 0.09375
- w_unpatch: bfloat16 [1024, 2048], P('seq'), may hold values from -0.1875 to 0.1875
- dens_in: float32 [64, 32], replicated, may hold values from -1 to 1
- dens_bias: float32 [64], replicated, may hold values from -3 to 3
- dens_out: float32 [64], replicated, may hold values from -0.75 to 0.75
- color_in: float32 [64, 32], replicated, may hold values from -1 to 1
- color_bias: float32 [64], replicated, may hold values from -3 to 3
- color_out: float32 [3, 64], replicated, may hold values from -0.75 to 0.75
- edge_ids: int32 [16, 2048], P('seq', 'tp'), may hold values from 0 to 393215
- blend_steps: int32 [16, 2048], P('seq', 'tp'), may hold values from 0 to 16
- live_count: int32 [16, 2], P('seq', 'tp'), may hold values from 256 to 1024, as said below
- color_grad: float32 [3, 16, 2048], P(None, 'seq', 'tp'), may hold values from -6 to 6
- out_grad: float32 [16384, 1024], P('seq'), may hold values from -6 to 6
Outputs:
- colors: float32 [3, 16, 2048], P(None, 'seq', 'tp')
- x_grad: float32 [16384, 1024], P(('seq', 'tp'))
- attn_gain_grad: float32 [1024], replicated
- w_qkv_grad: float32 [1024, 3, 1024], P('seq', None, 'tp')
- w_out_grad: float32 [1024, 1024], P('tp', 'seq')
- mlp_gain_grad: float32 [1024], replicated
- w_up_grad: float32 [1024, 4096], P('seq', 'tp')
- w_down_grad: float32 [4096, 1024], P('tp', 'seq')
- w_unpatch_grad: float32 [1024, 2048], P('seq')
- dens_in_grad: float32 [64, 32], replicated
- dens_bias_grad: float32 [64], replicated
- dens_out_grad: float32 [64], replicated
- color_in_grad: float32 [64, 32], replicated
- color_bias_grad: float32 [64], replicated
- color_out_grad: float32 [3, 64], replicated
Inputs may be any that keep to these rules, and one draw needn't show every extreme that they name: `live_count`: in every scene some slab uses all 1024 slots of its list.
All inputs are finite; a program needn't handle non-finite values.
Results may differ from a plain program's by a relative error of at most 0.025.
The roundings to bfloat16 on the way count: a program that leaves them out, or rounds other values in their place, can miss the bound.
Values may be sent and summed in bfloat16 or wider, within the bound.
No kernel may reach another device: no remote copies, remote signals or barrier semaphores. Data moves between devices by JAX's collectives and lax.ppermute only.
A program may use at most 512 MiB of HBM per device.

v0:
```python
import jax
import jax.numpy as jnp
from jax import lax
from jax.sharding import PartitionSpec as P

HEAD_DIM = 64
FEAT = 32
PATCH = 8
GRID = 64
TRI = 192


HIGHEST = lax.Precision.HIGHEST


def from_behind(x, axis, by):
    length = lax.axis_size(axis)
    pairs = [(i, i + by) for i in range(length) if 0 <= i + by < length]
    return lax.ppermute(x, axis, pairs)


def gelu_exact(values):
    return jax.nn.gelu(values, approximate=False)


def layer_norm(values, gain_vec):
    center = values - jnp.mean(values, axis=-1, keepdims=True)
    spread = jnp.mean(center * center, axis=-1, keepdims=True)
    return center * lax.rsqrt(spread + 1e-05) * gain_vec


def density(field_vals, dens_in, dens_bias, dens_out):
    hidden = gelu_exact(jnp.dot(dens_in, field_vals, precision=HIGHEST) + dens_bias[:, None])
    return jnp.dot(dens_out, hidden, precision=HIGHEST)


def decode(vertex_feat, vertex_dens, color_in, color_bias, color_out):
    hidden = gelu_exact(jnp.dot(color_in, vertex_feat, precision=HIGHEST) + color_bias[:, None])
    shade_rgb = jax.nn.sigmoid(jnp.dot(color_out, hidden, precision=HIGHEST))
    return jax.nn.sigmoid(vertex_dens)[None, :] * shade_rgb


def edge_ends(edge_row, slab_planes, grid_side, plane_offset):
    slab_cells = slab_planes * grid_side * grid_side
    direction = edge_row // slab_cells
    cell_index = edge_row % slab_cells
    plane_a = cell_index // (grid_side * grid_side) + plane_offset
    spot_a = cell_index % (grid_side * grid_side)
    column = spot_a // grid_side
    depth_index = spot_a % grid_side
    valid_mask = (
        (direction == 0)
        | (direction == 1) & (column < grid_side - 1)
        | (direction == 2) & (depth_index < grid_side - 1)
    )
    plane_b = jnp.where(direction == 0, plane_a + 1, plane_a)
    spot_b = jnp.where(
        valid_mask & (direction == 1),
        spot_a + grid_side,
        jnp.where(valid_mask & (direction == 2), spot_a + 1, spot_a),
    )
    return (plane_a, spot_a, plane_b, spot_b, valid_mask.astype(jnp.float32))


def to_plane(units, patch_rows):
    grid_patches = GRID // PATCH
    return (
        units.reshape(patch_rows, grid_patches, PATCH, PATCH, FEAT)
        .transpose(4, 0, 2, 1, 3)
        .reshape(FEAT, patch_rows * PATCH, GRID)
    )


def from_plane(grads, patch_rows):
    grid_patches = GRID // PATCH
    return (
        grads.reshape(FEAT, patch_rows, PATCH, grid_patches, PATCH)
        .transpose(1, 3, 2, 4, 0)
        .reshape(patch_rows * grid_patches, PATCH * PATCH * FEAT)
    )


def attend_forward(queries, key_rows, value_rows, score_scale):
    length = queries.shape[0]
    heads_here = queries.shape[1]
    block_rows = min(512, length)

    def one_block(q_block):
        scores = (
            jnp.einsum("qhd,khd->hqk", q_block, key_rows, preferred_element_type=jnp.float32)
            * score_scale
        )
        row_max = jnp.max(scores, axis=-1, keepdims=True)
        exp_scores = jnp.exp(scores - row_max)
        row_total = jnp.sum(exp_scores, axis=-1, keepdims=True)
        probs = (exp_scores / row_total).astype(jnp.bfloat16)
        block_out = jnp.einsum(
            "hqk,khd->qhd", probs, value_rows, preferred_element_type=jnp.float32
        ).astype(jnp.bfloat16)
        return (block_out, (row_max + jnp.log(row_total))[..., 0])

    blocks_out, log_total = lax.map(
        one_block, queries.reshape(length // block_rows, block_rows, heads_here, HEAD_DIM)
    )
    return (blocks_out.reshape(length, heads_here, HEAD_DIM), log_total)


def attend_backward(queries, key_rows, value_rows, grad_heads, log_total, score_scale):
    length = queries.shape[0]
    heads_here = queries.shape[1]
    block_rows = min(512, length)

    def one_block(state_acc, inputs):
        key_acc, value_acc = state_acc
        q_block, g_block, lse_block = inputs
        scores = (
            jnp.einsum("qhd,khd->hqk", q_block, key_rows, preferred_element_type=jnp.float32)
            * score_scale
        )
        probs = jnp.exp(scores - lse_block[..., None])
        grad_probs = jnp.einsum(
            "qhd,khd->hqk", g_block, value_rows, preferred_element_type=jnp.float32
        )
        inner = jnp.sum(probs * grad_probs, axis=-1, keepdims=True)
        grad_scores = (probs * (grad_probs - inner)).astype(jnp.bfloat16)
        grad_query = (
            jnp.einsum("hqk,khd->qhd", grad_scores, key_rows, preferred_element_type=jnp.float32)
            * score_scale
        )
        key_acc = (
            key_acc
            + jnp.einsum("hqk,qhd->khd", grad_scores, q_block, preferred_element_type=jnp.float32)
            * score_scale
        )
        value_acc = value_acc + jnp.einsum(
            "hqk,qhd->khd", probs.astype(jnp.bfloat16), g_block, preferred_element_type=jnp.float32
        )
        return ((key_acc, value_acc), grad_query)

    zero_rows = jnp.zeros(key_rows.shape, jnp.float32)
    shaped = (length // block_rows, block_rows, heads_here, HEAD_DIM)
    (grad_key, grad_value), grad_query = lax.scan(
        one_block,
        (zero_rows, zero_rows),
        (queries.reshape(shaped), grad_heads.reshape(shaped), log_total),
    )
    return (grad_query.reshape(length, heads_here, HEAD_DIM), grad_key, grad_value)


def shards(
    layer_input,
    attn_gain,
    w_qkv,
    w_out,
    mlp_gain,
    w_up,
    w_down,
    w_unpatch,
    dens_in,
    dens_bias,
    dens_out,
    color_in,
    color_bias,
    color_out,
    edge_ids,
    blend_steps,
    live_count,
    color_grad,
    out_grad,
):
    tp_count = lax.axis_size("tp")
    tp_index = lax.axis_index("tp")
    length, model_width = layer_input.shape
    own_rows = length // tp_count
    row_first = tp_index * own_rows
    tri_rows = TRI // tp_count
    slab_planes = GRID // tp_count
    slab_patches = slab_planes // PATCH
    grid_patches = GRID // PATCH
    plane_tokens_count = grid_patches * grid_patches
    slab_tokens = slab_patches * grid_patches
    plane_cells = GRID * GRID
    slab_cells = slab_planes * plane_cells
    score_scale = HEAD_DIM ** (-0.5)
    gathered = (
        lax.all_gather(w_qkv, "seq", axis=0, tiled=True),
        lax.all_gather(w_out, "seq", axis=1, tiled=True),
        lax.all_gather(w_up, "seq", axis=0, tiled=True),
        lax.all_gather(w_down, "seq", axis=1, tiled=True),
        lax.all_gather(w_unpatch, "seq", axis=0, tiled=True),
    )
    qkv_full, out_full, up_full, down_full, unpatch_full = gathered
    local_width = qkv_full.shape[2]
    heads_here = local_width // HEAD_DIM
    input_f32 = layer_input.astype(jnp.float32)
    normed_a = layer_norm(input_f32, attn_gain).astype(jnp.bfloat16)
    projected = jnp.dot(
        normed_a, qkv_full.reshape(model_width, 3 * local_width), preferred_element_type=jnp.float32
    )
    projected = projected.astype(jnp.bfloat16).reshape(length, 3, heads_here, HEAD_DIM)
    queries = projected[:, 0]
    key_rows = projected[:, 1]
    value_rows = projected[:, 2]
    attended, log_total = attend_forward(queries, key_rows, value_rows, score_scale)
    attended = attended.reshape(length, local_width)
    attn_own = lax.psum_scatter(
        jnp.dot(attended, out_full, preferred_element_type=jnp.float32),
        "tp",
        scatter_dimension=0,
        tiled=True,
    )
    input_own = lax.dynamic_slice_in_dim(input_f32, row_first, own_rows, 0)
    hidden_own = input_own + attn_own
    normed_b = lax.all_gather(
        layer_norm(hidden_own, mlp_gain).astype(jnp.bfloat16), "tp", axis=0, tiled=True
    )
    up_value = jnp.dot(normed_b, up_full, preferred_element_type=jnp.float32)
    activated = gelu_exact(up_value).astype(jnp.bfloat16)
    mlp_own = lax.psum_scatter(
        jnp.dot(activated, down_full, preferred_element_type=jnp.float32),
        "tp",
        scatter_dimension=0,
        tiled=True,
    )
    output_own = hidden_own + mlp_own
    plane_tokens = lax.all_gather(
        output_own[own_rows - tri_rows :].astype(jnp.bfloat16), "tp", axis=0, tiled=True
    )
    xy_tokens = lax.dynamic_slice_in_dim(plane_tokens, tp_index * slab_tokens, slab_tokens, 0)
    xz_tokens = lax.dynamic_slice_in_dim(
        plane_tokens, plane_tokens_count + tp_index * slab_tokens, slab_tokens, 0
    )
    yz_tokens = plane_tokens[2 * plane_tokens_count :]
    plane_xy = to_plane(
        jnp.dot(xy_tokens, unpatch_full, preferred_element_type=jnp.float32), slab_patches
    )
    plane_xz = to_plane(
        jnp.dot(xz_tokens, unpatch_full, preferred_element_type=jnp.float32), slab_patches
    )
    plane_yz = to_plane(
        jnp.dot(yz_tokens, unpatch_full, preferred_element_type=jnp.float32), grid_patches
    )
    field_slab = (
        plane_xy[:, :, :, None] + plane_xz[:, :, None, :] + plane_yz[:, None, :, :]
    ).reshape(FEAT, slab_cells)
    dens_slab = density(field_slab, dens_in, dens_bias, dens_out)
    next_field, next_dens = (
        from_behind(field_slab[:, :plane_cells].astype(jnp.bfloat16), "tp", -1).astype(jnp.float32),
        from_behind(dens_slab[:plane_cells].astype(jnp.bfloat16), "tp", -1).astype(jnp.float32),
    )
    field_ext = jnp.concatenate([field_slab, next_field], 1)
    dens_ext = jnp.concatenate([dens_slab, next_dens], 0)
    edge_row = edge_ids[0]
    plane_a, spot_a, plane_b, spot_b, valid_b = edge_ends(edge_row, slab_planes, GRID, 0)
    flat_a = plane_a * plane_cells + spot_a
    flat_b = plane_b * plane_cells + spot_b
    weight_b = blend_steps[0].astype(jnp.float32) / 16.0
    weight_a = 1.0 - weight_b
    weight_b = weight_b * valid_b
    live_mask = (jnp.arange(edge_row.shape[0], dtype=jnp.int32) < live_count[0, 0]).astype(
        jnp.float32
    )
    vertex_feat = (
        weight_a[None, :] * field_ext[:, flat_a] + weight_b[None, :] * field_ext[:, flat_b]
    )
    vertex_dens = weight_a * dens_ext[flat_a] + weight_b * dens_ext[flat_b]
    shaded, decode_back = jax.vjp(decode, vertex_feat, vertex_dens, color_in, color_bias, color_out)
    colors = live_mask[None, :] * shaded
    grad_feat, grad_vdens, grad_color_in, grad_color_bias, grad_color_out = decode_back(
        color_grad[:, 0, :] * live_mask[None, :]
    )
    ext_cells = slab_cells + plane_cells
    field_grad = (
        jnp.zeros((FEAT, ext_cells), jnp.float32)
        .at[:, flat_a]
        .add(weight_a[None, :] * grad_feat)
        .at[:, flat_b]
        .add(weight_b[None, :] * grad_feat)
    )
    dens_grad = (
        jnp.zeros((ext_cells,), jnp.float32)
        .at[flat_a]
        .add(weight_a * grad_vdens)
        .at[flat_b]
        .add(weight_b * grad_vdens)
    )
    has_next = (tp_index < tp_count - 1).astype(jnp.float32)
    keep_mask = jnp.concatenate(
        [jnp.ones((slab_cells,), jnp.float32), has_next * jnp.ones((plane_cells,), jnp.float32)], 0
    )
    dens_value, dens_back = jax.vjp(density, field_ext, dens_in, dens_bias, dens_out)
    grad_field, grad_dens_in, grad_dens_bias, grad_dens_out = dens_back(dens_grad * keep_mask)
    field_total = (grad_field + field_grad * keep_mask[None, :]).reshape(
        FEAT, slab_planes + 1, GRID, GRID
    )
    grad_xy = jnp.sum(field_total, axis=3)
    grad_xz = jnp.sum(field_total, axis=2)
    grad_yz = jnp.sum(field_total, axis=1)
    blank_plane = jnp.zeros((FEAT, GRID + 1, GRID), jnp.float32)
    xy_whole = lax.dynamic_update_slice_in_dim(blank_plane, grad_xy, tp_index * slab_planes, 1)[
        :, :GRID
    ]
    xz_whole = lax.dynamic_update_slice_in_dim(blank_plane, grad_xz, tp_index * slab_planes, 1)[
        :, :GRID
    ]
    grad_units = jnp.concatenate(
        [
            from_plane(xy_whole, grid_patches),
            from_plane(xz_whole, grid_patches),
            from_plane(grad_yz, grid_patches),
        ],
        0,
    )
    grad_units = lax.psum(grad_units.astype(jnp.bfloat16), "tp")
    grad_tokens = jnp.dot(grad_units, unpatch_full.T, preferred_element_type=jnp.float32)
    grad_unpatch = jnp.dot(plane_tokens.T, grad_units, preferred_element_type=jnp.float32)
    grad_output = out_grad.reshape(tp_count, own_rows, model_width)
    grad_output = (
        grad_output.at[:, own_rows - tri_rows :, :]
        .add(grad_tokens.reshape(tp_count, tri_rows, model_width))
        .reshape(length, model_width)
    )
    grad_mlp = grad_output.astype(jnp.bfloat16)
    grad_act = jnp.dot(grad_mlp, down_full.T, preferred_element_type=jnp.float32)
    grad_down = jnp.dot(activated.T, grad_mlp, preferred_element_type=jnp.float32)
    gelu_value, gelu_back = jax.vjp(gelu_exact, up_value)
    grad_up_value = gelu_back(grad_act)[0].astype(jnp.bfloat16)
    grad_up = jnp.dot(normed_b.T, grad_up_value, preferred_element_type=jnp.float32)
    grad_normed_b = lax.psum_scatter(
        jnp.dot(grad_up_value, up_full.T, preferred_element_type=jnp.float32).astype(jnp.bfloat16),
        "tp",
        scatter_dimension=0,
        tiled=True,
    ).astype(jnp.float32)
    norm_b_value, norm_b_back = jax.vjp(layer_norm, hidden_own, mlp_gain)
    grad_hidden, grad_mlp_gain = norm_b_back(grad_normed_b)
    grad_hidden = grad_hidden + lax.dynamic_slice_in_dim(grad_output, row_first, own_rows, 0)
    grad_branch = lax.all_gather(grad_hidden.astype(jnp.bfloat16), "tp", axis=0, tiled=True)
    grad_out_w = jnp.dot(attended.T, grad_branch, preferred_element_type=jnp.float32)
    grad_heads = (
        jnp.dot(grad_branch, out_full.T, preferred_element_type=jnp.float32)
        .astype(jnp.bfloat16)
        .reshape(length, heads_here, HEAD_DIM)
    )
    grad_query, grad_key, grad_value = attend_backward(
        queries, key_rows, value_rows, grad_heads, log_total, score_scale
    )
    grad_proj = (
        jnp.stack([grad_query, grad_key, grad_value], 1)
        .astype(jnp.bfloat16)
        .reshape(length, 3 * local_width)
    )
    grad_qkv = jnp.dot(normed_a.T, grad_proj, preferred_element_type=jnp.float32).reshape(
        model_width, 3, local_width
    )
    qkv_flat = qkv_full.reshape(model_width, 3 * local_width)
    grad_normed_a = lax.psum_scatter(
        jnp.dot(grad_proj, qkv_flat.T, preferred_element_type=jnp.float32).astype(jnp.bfloat16),
        "tp",
        scatter_dimension=0,
        tiled=True,
    ).astype(jnp.float32)
    norm_a_value, norm_a_back = jax.vjp(layer_norm, input_own, attn_gain)
    grad_input, grad_attn_gain = norm_a_back(grad_normed_a)
    grad_input = grad_input + grad_hidden
    weight_sums = (
        lax.psum_scatter(
            grad_qkv.astype(jnp.bfloat16), "seq", scatter_dimension=0, tiled=True
        ).astype(jnp.float32),
        lax.psum_scatter(
            grad_out_w.astype(jnp.bfloat16), "seq", scatter_dimension=1, tiled=True
        ).astype(jnp.float32),
        lax.psum_scatter(
            grad_up.astype(jnp.bfloat16), "seq", scatter_dimension=0, tiled=True
        ).astype(jnp.float32),
        lax.psum_scatter(
            grad_down.astype(jnp.bfloat16), "seq", scatter_dimension=1, tiled=True
        ).astype(jnp.float32),
        lax.psum_scatter(
            grad_unpatch.astype(jnp.bfloat16), "seq", scatter_dimension=0, tiled=True
        ).astype(jnp.float32),
    )
    small_sums = lax.psum(
        (
            grad_attn_gain,
            grad_mlp_gain,
            grad_dens_in,
            grad_dens_bias,
            grad_dens_out,
            grad_color_in,
            grad_color_bias,
            grad_color_out,
        ),
        ("seq", "tp"),
    )
    return (
        colors[:, None, :],
        grad_input,
        small_sums[0],
        weight_sums[0],
        weight_sums[1],
        small_sums[1],
        weight_sums[2],
        weight_sums[3],
        weight_sums[4],
        small_sums[2],
        small_sums[3],
        small_sums[4],
        small_sums[5],
        small_sums[6],
        small_sums[7],
    )


def solution(mesh):
    placed = (
        P("seq", None),
        P(),
        P("seq", None, "tp"),
        P("tp", "seq"),
        P(),
        P("seq", "tp"),
        P("tp", "seq"),
        P("seq", None),
        P(),
        P(),
        P(),
        P(),
        P(),
        P(),
        P("seq", "tp"),
        P("seq", "tp"),
        P("seq", "tp"),
        P(None, "seq", "tp"),
        P("seq", None),
    )
    return jax.shard_map(
        shards,
        mesh=mesh,
        in_specs=placed,
        out_specs=(
            P(None, "seq", "tp"),
            P(("seq", "tp"), None),
            P(),
            P("seq", None, "tp"),
            P("tp", "seq"),
            P(),
            P("seq", "tp"),
            P("tp", "seq"),
            P("seq", None),
            P(),
            P(),
            P(),
            P(),
            P(),
            P(),
        ),
        check_vma=False,
    )
```

profile of v0, /device:TPU:0, one launch (start us, length us, event | category | flops | bytes accessed | tf_op | source)
XLA Modules:
  0.0 1605.0 jit_solution(11579380000336815335)
XLA Ops:
  14.1 46.2 %all-gather.8.cloned.1.call-done = bf16[1024,3,512]{2,0,1:T(8,128)(2,1)} async-done(((bf16[64,3,512]{2,0,1:T(8,128)(2,1)}), bf16[1024,3,512]{2,0,1:T(8,128)(2,1)}) %all-gather.8.cloned.1.call-update) | async-done | bytes 3145744 | tf_op jit(solution)/shard_map/all_gather | solution.py:186
  65.0 7.1 convolution_convert_fusion.1
  82.0 25.8 %while.28 = (s32[]{:T(128)}, bf16[2,512,8,64]{1,3,2,0:T(8,128)(2,1)}, f32[2,8,512]{2,1,0:T(8,128)S(1)}, bf16[2,512,8,64]{1,3,2,0:T(8,128)(2,1)}, bf16[1024,8,64]...) while((s32[]{:T(128)}, bf16[2,512,8,64]{1,3,2,0:T(8,128)(2,1)}, ...), condition=%wide.region_5.6_spmd, body=%wide.region_2.5_spmd.sunk | while | flops 1111748608 | bytes 61997208 | solution.py:102
  120.1 49.8 %reduce-scatter.10.cloned.1.call-done = f32[512,1024]{1,0:T(8,128)} async-done(((f32[1024,1024]{1,0:T(8,128)}), f32[512,1024]{1,0:T(8,128)}) %reduce-scatter.10.cloned.1.call-update) | async-done | bytes 2097168 | tf_op jit(solution)/shard_map/reduce_scatter | solution.py:206
  175.9 46.9 %all-gather.14.cloned.1.call-done = bf16[1024,2048]{1,0:T(8,128)(2,1)} async-done(((bf16[64,2048]{1,0:T(8,128)(2,1)}), bf16[1024,2048]{1,0:T(8,128)(2,1)}) %all-gather.14.cloned.1.call-update) | async-done | bytes 4194320 | tf_op jit(solution)/shard_map/all_gather | solution.py:188
  222.8 33.7 %all-gather.12.cloned.1.call-done = bf16[1024,1024]{1,0:T(8,128)(2,1)} async-done(((bf16[512,1024]{1,0:T(8,128)(2,1)}), bf16[1024,1024]{1,0:T(8,128)(2,1)}) %all-gather.12.cloned.1.call-update) | async-done | bytes 2097168 | tf_op jit(solution)/shard_map/all_gather | solution.py:214
  256.5 25.9 %multiply_convert_fusion.1 = (bf16[1024,2048]{1,0:T(8,128)(2,1)}, f32[1024,2048]{1,0:T(8,128)}, f32[1024,2048]{1,0:T(8,128)}) fusion(bf16[1024,1024]{1,0:T(8,128)(2,1)} %all-gather.12.cloned.1.call-done, bf16[1024,2048]{1,0:T(8,128)(2,1)} %all-gather.14.cloned.1.call-done), kind=kOutput, calls=%fused_computation.189 | convolution fusion | flops 4431282176 | bytes 27262976 | tf_op jit(solution)/shard_map/dot_general | solution.py:217
  282.4 26.9 %all-gather.16.cloned.1.call-done = bf16[2048,1024]{0,1:T(8,128)(2,1)} async-done(((bf16[2048,64]{0,1:T(8,128)(2,1)}), bf16[2048,1024]{0,1:T(8,128)(2,1)}) %all-gather.16.cloned.1.call-update) | async-done | bytes 4194320 | tf_op jit(solution)/shard_map/all_gather | solution.py:189
  309.3 10.0 fusion.286
  332.1 40.3 %reduce-scatter.12.cloned.1.call-done = f32[512,1024]{1,0:T(8,128)} async-done(((f32[1024,1024]{1,0:T(8,128)}), f32[512,1024]{1,0:T(8,128)}) %reduce-scatter.12.cloned.1.call-update) | async-done | bytes 2097168 | tf_op jit(solution)/shard_map/reduce_scatter | solution.py:219
  373.5 7.4 all_gather.29
  380.9 44.3 %all-gather.18.cloned.1.call-done = bf16[1024,2048]{1,0:T(8,128)(2,1)} async-done(((bf16[64,2048]{1,0:T(8,128)(2,1)}), bf16[1024,2048]{1,0:T(8,128)(2,1)}) %all-gather.18.cloned.1.call-update) | async-done | bytes 4194320 | tf_op jit(solution)/shard_map/all_gather | solution.py:190
  443.1 12.3 add_add_fusion
  455.3 31.1 %add.412 = f32[32,131072]{1,0:T(8,128)} reshape(f32[32,32,64,64]{3,2,1,0:T(8,128)} %add_add_fusion) | data formatting | bytes 33554432 | tf_op jit(solution)/shard_map/add | solution.py:244
  486.4 32.7 %convolution_add_fusion.1 = f32[131072,64]{0,1:T(8,128)} fusion(f32[32,131072]{1,0:T(8,128)} %add.412, f32[64,32]{0,1:T(8,128)S(1)} %copy-done, f32[64]{0:T(128)S(1)} %copy-done.72), kind=kOutput, calls=%fused_computation.53 | convolution fusion | flops 3229614080 | bytes 50340096 | tf_op jit(solution)/shard_map/dot_general | solution.py:33
  519.2 96.5 %fusion.61 = f32[1,131072]{1,0:T(1,128)S(1)} fusion(f32[131072,64]{0,1:T(8,128)} %convolution_add_fusion.1, f32[64]{0:T(128)S(1)} %copy-done.83), kind=kOutput, calls=%fused_computation.90 | convolution fusion | flops 637534208 | bytes 34078976 | tf_op jit(solution)/shard_map/dot_general | solution.py:34
  633.9 12.6 pad_maximum_fusion
  646.5 36.2 %copy.75 = f32[32,135168]{0,1:T(8,128)} copy(f32[32,135168]{1,0:T(8,128)} %pad_maximum_fusion) | data formatting | bytes 34603008 | tf_op jit(solution)/shard_map/concatenate | solution.py:251
  682.7 10.5 gather_fusion.3
  693.3 10.5 gather_fusion.2
  708.4 43.3 %scatter_custom_fusion.2 = f32[32,135168]{0,1:T(8,128)} fusion(s32[1024]{0:T(1024)} %get-tuple-element.228, f32[]{:T(128)} %constant.125.clone.1, f32[1024,32]{1,0:T(8,128)S(1)} %copy.79, s32[1024]{0:T(1024)} %broadcast_clamp_fusion.1), kind=kCustom, calls=%fused_computation.73 | custom fusion | flops 32768 | bytes 17302016 | tf_op jit(solution)/shard_map/scatter-add | solution.py:276
  751.7 57.5 %scatter_custom_fusion.3 = f32[32,135168]{0,1:T(8,128)} fusion(f32[32,135168]{0,1:T(8,128)} %scatter_custom_fusion.2, s32[1024]{0:T(1024)} %get-tuple-element.230, f32[1024,32]{1,0:T(8,128)S(1)} %copy.80, s32[1024]{0:T(1024)} %broadcast_clamp_fusion), kind=kCustom, calls=%fused_computation.259 | custom fusion | flops 32768 | bytes 17301504 | tf_op jit(solution)/shard_map/scatter-add | solution.py:278
  809.2 41.1 %copy.81 = f32[32,135168]{1,0:T(8,128)} copy(f32[32,135168]{0,1:T(8,128)} %scatter_custom_fusion.3) | data formatting | bytes 34603008 | tf_op jit(solution)/shard_map/scatter-add | solution.py:278
  856.6 6.2 scatter_fusion
  863.7 119.9 %fusion.277 = (f32[64]{0:T(128)}, f32[64,135168]{1,0:T(8,128)}, f32[64,135168]{1,0:T(8,128)}, f32[135168,64]{0,1:T(8,128)}) fusion(f32[64]{0:T(128)S(1)} %copy-done.83, f32[135168]{0:T(1024)S(1)} %get-tuple-element.303, f32[64]{0:T(128)S(1)} %copy-done.73, f32[64,32]{0,1:T(8,128)S(1)} %copy-done, f32[32,4096]{1,0:T(8,128)S(1)} %convert_element_type.134, ...), kind=kOutput, calls=%fused_computation.438 | convolution fusion | flops 3966369792 | bytes 121660160 | tf_op jit(solution)/shard_map/jvp()/dot_general | solution.py:33
  983.7 28.8 %fusion.35 = f32[32,135168]{1,0:T(8,128)} fusion(f32[64,135168]{1,0:T(8,128)} %get-tuple-element.280, f32[64,32]{0,1:T(8,128)S(1)} %copy-done, f32[32,135168]{1,0:T(8,128)} %copy.81, f32[135168]{0:T(1024)S(1)} %copy-done.19), kind=kOutput, calls=%fused_computation.54 | convolution fusion | flops 3330539520 | bytes 69754880 | tf_op jit(solution)/shard_map/transpose(jvp())/dot_general | solution.py:33
  1012.5 35.8 %reshape.570 = f32[32,33,64,64]{3,2,1,0:T(8,128)} reshape(f32[32,135168]{1,0:T(8,128)} %fusion.35) | data formatting | bytes 34603008 | tf_op jit(solution)/shard_map/reshape | solution.py:293
  1048.3 16.0 fusion.276
  1071.9 32.1 %all-reduce.4.cloned.1.call-done = bf16[192,2048]{1,0:T(8,128)(2,1)} async-done(((bf16[192,2048]{1,0:T(8,128)(2,1)}), bf16[192,2048]{1,0:T(8,128)(2,1)}) %all-reduce.4.cloned.1.call-update) | async-done | bytes 786448 | tf_op jit(solution)/shard_map/psum | solution.py:314
  1110.2 13.4 add_convert_fusion
  1131.5 31.9 %reduce-scatter.14.cloned.1.call-done = bf16[512,1024]{1,0:T(8,128)(2,1)} async-done(((bf16[1024,1024]{1,0:T(8,128)(2,1)}), bf16[512,1024]{1,0:T(8,128)(2,1)}) %reduce-scatter.14.cloned.1.call-update) | async-done | bytes 1048592 | tf_op jit(solution)/shard_map/reduce_scatter | solution.py:329
  1171.3 9.4 convolution_convert_fusion.3
  1180.8 10.1 convolution_convert_fusion.2
  1194.3 9.8 all-gather.20.cloned.1.call-done
  1217.2 119.5 %while.29 = (s32[]{:T(128)}, f32[1024,8,64]{0,2,1:T(8,128)}, f32[1024,8,64]{0,2,1:T(8,128)}, bf16[2,512,8,64]{1,0,3,2:T(2,128)(2,1)}, bf16[2,512,8,64]{1,3,2,0:T...) while((s32[]{:T(128)}, f32[1024,8,64]{0,2,1:T(8,128)}, ...), condition=%wide.region_24.25_spmd.clone, body=%wide.region_22.24_spmd.clone.sunk | while | flops 2737827840 | bytes 175751344 | solution.py:142
  1226.1 9.6 multiply_reduce_fusion.9
  1235.7 11.0 multiply_convert_fusion.7
  1257.8 18.3 %dynamic_update_slice.30 = bf16[2,512,8,64]{1,0,3,2:T(2,128)(2,1)} dynamic-update-slice(bf16[2,512,8,64]{1,0,3,2:T(2,128)(2,1)} %get-tuple-element.457, bf16[1,512,8,64]{1,0,3,2:T(2,128)(2,1)S(1)} %copy.130, s32[]{:T(128)S(6)} %copy.153, s32[]{:T(128)} %constant.122.clone.1..sunk, s32[]{:T(128)} %constant.122.clone.1..sunk, s32[]{:T(128)} %constant.122.clone.1..sunk) | dynamic-update-slice | bytes 1048580 | tf_op jit(solution)/shard_map/while/body/jit(dynamic_update_index_in_dim)/dynamic_update_slice | solution.py:142
  1285.2 10.0 multiply_reduce_fusion.9
  1295.1 11.1 multiply_convert_fusion.7
  1318.5 18.3 %dynamic_update_slice.30 = bf16[2,512,8,64]{1,0,3,2:T(2,128)(2,1)} dynamic-update-slice(bf16[2,512,8,64]{1,0,3,2:T(2,128)(2,1)} %get-tuple-element.457, bf16[1,512,8,64]{1,0,3,2:T(2,128)(2,1)S(1)} %copy.130, s32[]{:T(128)S(6)} %copy.153, s32[]{:T(128)} %constant.122.clone.1..sunk, s32[]{:T(128)} %constant.122.clone.1..sunk, s32[]{:T(128)} %constant.122.clone.1..sunk) | dynamic-update-slice | bytes 1048580 | tf_op jit(solution)/shard_map/while/body/jit(dynamic_update_index_in_dim)/dynamic_update_slice | solution.py:142
  1347.9 7.6 convolution_convert_fusion.4
  1355.8 32.1 %fusion.275 = f32[64,32]{0,1:T(8,128)S(1)} fusion(f32[64,135168]{1,0:T(8,128)} %get-tuple-element.280, f32[32,4096]{1,0:T(8,128)S(1)} %copy-done.13, f32[32,131072]{1,0:T(8,128)} %add.412), kind=kOutput, calls=%fused_computation.436 | convolution fusion | flops 3326214144 | bytes 51912704 | tf_op jit(solution)/shard_map/transpose(jvp())/dot_general | solution.py:33
  1389.2 32.1 %fusion.176 = f32[64]{0:T(128)S(1)} fusion(f32[135168,1]{0,1:T(1,128)S(1)} %bitcast.480, f32[64,135168]{1,0:T(8,128)} %get-tuple-element.281, f32[135168,64]{0,1:T(8,128)} %get-tuple-element.319), kind=kOutput, calls=%fused_computation.248 | convolution fusion | flops 121110528 | bytes 69746944 | tf_op jit(solution)/shard_map/transpose(jvp())/dot_general | solution.py:34
  1433.1 58.6 %reduce-scatter.20.cloned.1.call-done = bf16[512,64]{0,1:T(8,128)(2,1)} async-done(((bf16[512,1024]{0,1:T(8,128)(2,1)}), bf16[512,64]{0,1:T(8,128)(2,1)}) %reduce-scatter.20.cloned.1.call-update) | async-done | bytes 65552 | tf_op jit(solution)/shard_map/reduce_scatter | solution.py:370
  1493.2 32.1 %reduce-scatter.16.cloned.1.call-done = bf16[512,1024]{1,0:T(8,128)(2,1)} async-done(((bf16[1024,1024]{1,0:T(8,128)(2,1)}), bf16[512,1024]{1,0:T(8,128)(2,1)}) %reduce-scatter.16.cloned.1.call-update) | async-done | bytes 1048592 | tf_op jit(solution)/shard_map/reduce_scatter | solution.py:357
  1530.9 41.0 %all-reduce.1 = (f32[1024]{0:T(1024)}, f32[1024]{0:T(1024)}, f32[64,32]{0,1:T(8,128)}, f32[64]{0:T(128)}, f32[64]{0:T(128)}, /*index=5*/f32[64,32]{0,1:T(8,128)}, f32[64]{0:T(128)}, f32[3,64]{1,0:T(4,128)}) all-reduce(f32[1024]{0:T(1024)S(1)} %get-tuple-element.235, ...), channel_id=1, replica_groups=mesh['seq'=16,'tp'=2] {'seq','tp'}, use_global_device_ids=true, to_apply=%region_31.32 | all-reduce | flops 6528 | bytes 52224 | tf_op jit(solution)/shard_map/psum | solution.py:383
  1576.5 19.8 %reduce-scatter.18.cloned.1.call-done = bf16[64,3,512]{2,0,1:T(8,128)(2,1)} async-done(((bf16[1024,3,512]{2,0,1:T(8,128)(2,1)}), bf16[64,3,512]{2,0,1:T(8,128)(2,1)}) %reduce-scatter.18.cloned.1.call-update) | async-done | bytes 196624 | tf_op jit(solution)/shard_map/reduce_scatter | solution.py:367
  (353 shorter events, 250.6 us)
Async XLA Ops:
  7.2 479.2 %copy-start = (f32[64,32]{0,1:T(8,128)S(1)}, f32[64,32]{0,1:T(8,128)}, u32[]{:S(2)}) copy-start(f32[64,32]{0,1:T(8,128)} %param.33) | copy-start | bytes 24580
  7.2 57.8 %copy-start.47 = (f32[1024]{0:T(1024)S(1)}, f32[1024]{0:T(1024)}, u32[]{:S(2)}) copy-start(f32[1024]{0:T(1024)} %param.26) | copy-start | bytes 12292
  7.2 53.1 %all-gather.8.cloned.1.call-start = ((), (), s32[]{:S(2)}) async-start(), calls=%async_computation.9 | async-start | bytes 3342336 | tf_op jit(solution)/shard_map/all_gather | solution.py:186
  12.2 99.6 %all-gather.10.cloned.1.call-start = ((), (), s32[]{:S(2)}) async-start(), calls=%async_computation.10 | async-start | bytes 1114112 | tf_op jit(solution)/shard_map/all_gather | solution.py:187
  13.0 157.0 %reduce-scatter.10.cloned.1.call-start = ((), (), s32[]{:S(2)}) async-start(), calls=%async_computation.11 | async-start | bytes 6291456 | tf_op jit(solution)/shard_map/reduce_scatter | solution.py:206
  13.4 58.6 %copy-start.68 = (f32[1024]{0:T(1024)}, f32[1024]{0:T(1024)S(1)}, u32[]{:S(2)}) copy-start(f32[1024]{0:T(1024)S(1)} %broadcast_multiply_fusion.2) | copy-start | bytes 12292
  14.1 57.9 %copy-start.75 = (f32[1024]{0:T(1024)}, f32[1024]{0:T(1024)S(1)}, u32[]{:S(2)}) copy-start(f32[1024]{0:T(1024)S(1)} %add_rsqrt_fusion) | copy-start | bytes 12292
  116.7 57.2 %copy-start.58 = (f32[1024]{0:T(1024)S(1)}, f32[1024]{0:T(1024)}, u32[]{:S(2)}) copy-start(f32[1024]{0:T(1024)} %param.29) | copy-start | bytes 12292
  116.7 106.1 %all-gather.14.cloned.1.call-start = ((), (), s32[]{:S(2)}) async-start(), calls=%async_computation.13 | async-start | bytes 4456448 | tf_op jit(solution)/shard_map/all_gather | solution.py:188
  117.3 139.2 %all-gather.12.cloned.1.call-start = ((), (), s32[]{:S(2)}) async-start(), calls=%async_computation.12 | async-start | bytes 3145728 | tf_op jit(solution)/shard_map/all_gather | solution.py:214
  173.1 199.3 %copy-start.4 = (f32[512,1024]{1,0:T(8,128)}, f32[512,1024]{1,0:T(8,128)S(1)}, u32[]{:S(2)}) copy-start(f32[512,1024]{1,0:T(8,128)S(1)} %get-tuple-element.293) | copy-start | bytes 6291460
  173.5 108.9 %copy-start.64 = (f32[512]{0:T(512)}, f32[512]{0:T(512)S(1)}, u32[]{:S(2)}) copy-start(f32[512]{0:T(512)S(1)} %multiply_reduce_fusion.4) | copy-start | bytes 6148
  173.9 108.5 %copy-start.62 = (f32[512]{0:T(512)}, f32[512]{0:T(512)S(1)}, u32[]{:S(2)}) copy-start(f32[512]{0:T(512)S(1)} %fusion.235) | copy-start | bytes 6148
  175.3 134.1 %all-gather.16.cloned.1.call-start = ((), (), s32[]{:S(2)}) async-start(), calls=%async_computation.14 | async-start | bytes 4456448 | tf_op jit(solution)/shard_map/all_gather | solution.py:189
  175.8 196.6 %reduce-scatter.12.cloned.1.call-start = ((), (), s32[]{:S(2)}) async-start(), calls=%async_computation.15 | async-start | bytes 6291456 | tf_op jit(solution)/shard_map/reduce_scatter | solution.py:219
  319.3 105.8 %all-gather.18.cloned.1.call-start = ((), (), s32[]{:S(2)}) async-start(), calls=%async_computation.16 | async-start | bytes 4456448 | tf_op jit(solution)/shard_map/all_gather | solution.py:190
  320.1 784.0 %all-reduce.4.cloned.1.call-start = ((), (), s32[]{:S(2)}) async-start(), calls=%async_computation.17 | async-start | bytes 1572864 | tf_op jit(solution)/shard_map/psum | solution.py:314
  320.9 51.6 %copy-start.57 = (s32[1024,1]{0,1:T(1,128)}, s32[1024,1]{0,1:T(1,128)S(1)}, u32[]{:S(2)}) copy-start(s32[1024,1]{0,1:T(1,128)S(1)} %get-tuple-element.286) | copy-start | bytes 12292
  321.0 51.5 %copy-start.40 = (s32[1024,1]{0,1:T(1,128)}, s32[1024,1]{0,1:T(1,128)S(1)}, u32[]{:S(2)}) copy-start(s32[1024,1]{0,1:T(1,128)S(1)} %compare_select_fusion) | copy-start | bytes 12292
  380.9 52.3 %copy-start.14 = (bf16[192,1024]{1,0:T(8,128)(2,1)}, bf16[192,1024]{1,0:T(8,128)(2,1)S(1)}, u32[]{:S(2)}) copy-start(bf16[192,1024]{1,0:T(8,128)(2,1)S(1)} %all_gather.29) | copy-start | bytes 1179652
  519.1 102.2 %copy-start.61 = (s32[1024]{0:T(1024)S(1)}, s32[1024]{0:T(1024)}, u32[]{:S(2)}) copy-start(s32[1024]{0:T(1024)} %broadcast_clamp_fusion.2) | copy-start | bytes 12292
  519.1 108.3 %copy-start.60 = (s32[1024]{0:T(1024)S(1)}, s32[1024]{0:T(1024)}, u32[]{:S(2)}) copy-start(s32[1024]{0:T(1024)} %broadcast_clamp_fusion.3) | copy-start | bytes 12292
  615.7 5.5 collective-permute-start
  617.0 89.9 %copy-start.53 = (f32[1024]{0:T(1024)}, f32[1024]{0:T(1024)S(1)}, u32[]{:S(2)}) copy-start(f32[1024]{0:T(1024)S(1)} %fusion.227) | copy-start | bytes 12292
  618.1 15.7 collective-permute-start.1
  633.8 73.2 %copy-start.55 = (f32[1,1024]{1,0:T(1,128)}, f32[1,1024]{1,0:T(1,128)S(1)}, u32[]{:S(2)}) copy-start(f32[1,1024]{1,0:T(1,128)S(1)} %get-tuple-element.312) | copy-start | bytes 12292
  633.8 73.9 %copy-start.49 = (f32[1,1024]{1,0:T(1,128)}, f32[1,1024]{1,0:T(1,128)S(1)}, u32[]{:S(2)}) copy-start(f32[1,1024]{1,0:T(1,128)S(1)} %get-tuple-element.311) | copy-start | bytes 12292
  633.8 73.9 %copy-start.51 = (f32[1,1024]{1,0:T(1,128)}, f32[1,1024]{1,0:T(1,128)S(1)}, u32[]{:S(2)}) copy-start(f32[1,1024]{1,0:T(1,128)S(1)} %get-tuple-element.313) | copy-start | bytes 12292
  633.9 229.9 %copy-start.12 = (f32[32,4096]{1,0:T(8,128)}, f32[32,4096]{1,0:T(8,128)S(1)}, u32[]{:S(2)}) copy-start(f32[32,4096]{1,0:T(8,128)S(1)} %convert_element_type.134) | copy-start | bytes 1572868
  646.5 57.7 %copy-start.71 = (f32[64,32]{0,1:T(8,128)S(1)}, f32[64,32]{0,1:T(8,128)}, u32[]{:S(2)}) copy-start(f32[64,32]{0,1:T(8,128)} %param.36) | copy-start | bytes 24580
  646.5 57.7 %copy-start.82 = (f32[64]{0:T(128)S(1)}, f32[64]{0:T(128)}, u32[]{:S(2)}) copy-start(f32[64]{0:T(128)} %param.37) | copy-start | bytes 772
  704.0 47.7 %copy-start.30 = (f32[1024,32]{0,1:T(8,128)}, f32[1024,32]{0,1:T(8,128)S(1)}, u32[]{:S(2)}) copy-start(f32[1024,32]{0,1:T(8,128)S(1)} %copy.76) | copy-start | bytes 393220
  809.2 47.4 %copy-start.41 = (s32[1024,1]{0,1:T(1,128)S(1)}, s32[1024,1]{0,1:T(1,128)}, u32[]{:S(2)}) copy-start(s32[1024,1]{0,1:T(1,128)} %copy-done.40) | copy-start | bytes 12292
  863.7 119.9 %copy-start.20 = (f32[135168]{0:T(1024)}, f32[135168]{0:T(1024)S(1)}, u32[]{:S(2)}) copy-start(f32[135168]{0:T(1024)S(1)} %get-tuple-element.303) | copy-start | bytes 1622020
  863.7 119.9 %copy-start.19 = (f32[135168]{0:T(1024)S(1)}, f32[135168]{0:T(1024)}, u32[]{:S(2)}) copy-start(f32[135168]{0:T(1024)} %get-tuple-element.302) | copy-start | bytes 1622020
  1071.7 91.8 %reduce-scatter.14.cloned.1.call-start = ((), (), s32[]{:S(2)}) async-start(), calls=%async_computation.18 | async-start | bytes 3145728 | tf_op jit(solution)/shard_map/reduce_scatter | solution.py:329
  1131.4 72.7 %all-gather.20.cloned.1.call-start = ((), (), s32[]{:S(2)}) async-start(), calls=%async_computation.19 | async-start | bytes 3145728 | tf_op jit(solution)/shard_map/all_gather | solution.py:338
  1170.9 250.5 %reduce-scatter.22.cloned.1.call-start = ((), (), s32[]{:S(2)}) async-start(), calls=%async_computation.23 | async-start | bytes 4456448 | tf_op jit(solution)/shard_map/reduce_scatter | solution.py:373
  1180.7 242.6 %reduce-scatter.24.cloned.1.call-start = ((), (), s32[]{:S(2)}) async-start(), calls=%async_computation.24 | async-start | bytes 4456448 | tf_op jit(solution)/shard_map/reduce_scatter | solution.py:376
  1190.9 240.4 %reduce-scatter.26.cloned.1.call-start = ((), (), s32[]{:S(2)}) async-start(), calls=%async_computation.25 | async-start | bytes 4456448 | tf_op jit(solution)/shard_map/reduce_scatter | solution.py:379
  1194.3 297.4 %reduce-scatter.20.cloned.1.call-start = ((), (), s32[]{:S(2)}) async-start(), calls=%async_computation.22 | async-start | bytes 1114112 | tf_op jit(solution)/shard_map/reduce_scatter | solution.py:370
  1217.0 308.3 %reduce-scatter.16.cloned.1.call-start = ((), (), s32[]{:S(2)}) async-start(), calls=%async_computation.20 | async-start | bytes 3145728 | tf_op jit(solution)/shard_map/reduce_scatter | solution.py:357
  1347.8 248.5 %reduce-scatter.18.cloned.1.call-start = ((), (), s32[]{:S(2)}) async-start(), calls=%async_computation.21 | async-start | bytes 3342336 | tf_op jit(solution)/shard_map/reduce_scatter | solution.py:367
  1421.3 109.5 %copy-start.70 = (f32[1024]{0:T(1024)S(1)}, f32[1024]{0:T(1024)}, u32[]{:S(2)}) copy-start(f32[1024]{0:T(1024)} %get-tuple-element.239) | copy-start | bytes 12292
  1421.3 109.5 %copy-start.79 = (f32[64]{0:T(128)S(1)}, f32[64]{0:T(128)}, u32[]{:S(2)}) copy-start(f32[64]{0:T(128)} %get-tuple-element.320) | copy-start | bytes 772
  1421.3 109.5 %copy-start.80 = (f32[64]{0:T(128)S(1)}, f32[64]{0:T(128)}, u32[]{:S(2)}) copy-start(f32[64]{0:T(128)} %get-tuple-element.279) | copy-start | bytes 772
  1421.3 150.5 %copy-start.11 = (f32[512,1024]{1,0:T(8,128)S(1)}, f32[512,1024]{1,0:T(8,128)}, u32[]{:S(2)}) copy-start(f32[512,1024]{1,0:T(8,128)} %copy-done.10) | copy-start | bytes 6291460
  1421.4 150.5 %copy-start.67 = (f32[512]{0:T(512)S(1)}, f32[512]{0:T(512)}, u32[]{:S(2)}) copy-start(f32[512]{0:T(512)} %copy-done.66) | copy-start | bytes 6148
  (59 other events, 968.1 us)
Sparse Core Ops, SparseCore 0:
  12.4 47.8 all-gather.7
  62.5 36.7 all-gather.9
  116.8 53.1 reduce-scatter.9
  172.2 50.5 all-gather.13
  224.8 31.6 all-gather.11
  258.7 50.5 all-gather.15
  319.4 52.9 reduce-scatter.11
  374.6 50.5 all-gather.17
  1071.8 32.2 all-reduce.3
  1131.6 31.8 reduce-scatter.13
  1171.0 33.1 all-gather.19
  1207.9 72.3 reduce-scatter.21
  1284.6 71.5 reduce-scatter.23
  1359.9 71.3 reduce-scatter.25
  1435.2 56.3 reduce-scatter.19
  1494.3 30.9 reduce-scatter.15
  1529.4 66.8 reduce-scatter.17
where the time goes:
time: 1620 us; the launch traced here: 1610 us
  matrix products  544 us (34%)
  waiting for transfers between devices  483 us (30%)
  local copies, waits for them, and re-layouts  272 us (17%)
  other arithmetic  236 us (15%)
  blocking collectives  48.4 us (3%)
  between operations  16.4 us (1%)
    dot_general x4, matrix products, density(): jnp.dot(dens_in, field_vals, precision=HIGHEST) + dens_bias[:, None]  214 us
    dot_general x2, matrix products, density(): return jnp.dot(dens_out, hidden, precision=HIGHEST)  129 us
    scatter-add x6, other arithmetic, shards(): field_grad = jnp.zeros((FEAT, ext_cells), jnp.float32).at[:, flat_a].add(...  111 us
    reduce_scatter x1, waiting for transfers between devices, shards(): lax.psum_scatter(grad_out_w.astype(jnp.bfloat16), 'seq', scatter_dimensio...  58.6 us
    reduce_scatter x1, waiting for transfers between devices, shards(): lax.psum_scatter(jnp.dot(attended, out_full, preferred_element_type=jnp.f...  49.8 us
    all_gather x1, waiting for transfers between devices, shards(): lax.all_gather(w_up, 'seq', axis=0, tiled=True)  46.9 us
    all_gather x1, waiting for transfers between devices, shards(): lax.all_gather(w_qkv, 'seq', axis=0, tiled=True)  46.2 us
    all_gather x1, waiting for transfers between devices, shards(): lax.all_gather(w_unpatch, 'seq', axis=0, tiled=True)  44.3 us
  transfers between devices with their start and end apart: 19, of which 15 were waited for; matrix products, arithmetic and copies ran while one was open for 23% of the time, Pallas kernels for 0%

commit v1 on v0

v1 whole, which is shorter than its diff:
```python
import functools
import math

import jax
import jax.numpy as jnp
from jax import lax
from jax.experimental import pallas as pl
from jax.experimental.pallas import tpu as pltpu
from jax.sharding import PartitionSpec as P

HEAD_DIM = 64
FEAT = 32
PATCH = 8
GRID = 64
TRI = 192
SIDE = GRID // PATCH
PLANE_TOKENS = SIDE * SIDE
SPOTS = PLANE_TOKENS * PATCH
CELLS = PATCH * FEAT

HIGHEST = lax.Precision.HIGHEST
BF16 = jnp.bfloat16
F32 = jnp.float32
NN = (((1,), (0,)), ((), ()))
NT = (((1,), (1,)), ((), ()))
TN = (((0,), (0,)), ((), ()))


def cost(flops, moved, exps=0):
    return pl.CostEstimate(flops=int(flops), bytes_accessed=int(moved), transcendentals=int(exps))


def dot(a, b, dims=NN, precision=None):
    return lax.dot_general(a, b, dims, precision=precision, preferred_element_type=F32)


def gelu_parts(x):
    density = jnp.exp(-0.5 * x * x)
    t = 1.0 / (1.0 + (0.3275911 * 2.0**-0.5) * jnp.abs(x))
    poly = ((((1.061405429 * t - 1.453152027) * t + 1.421413741) * t - 0.284496736) * t + 0.254829592) * t
    tail = 0.5 * poly * density
    cdf = jnp.where(x < 0.0, tail, 1.0 - tail)
    return x * cdf, cdf + x * (density * (1.0 / math.sqrt(2.0 * math.pi)))


def leave(*refs):
    pass


def after(x, *others):
    if not others:
        return x
    anywhere = pl.BlockSpec(memory_space=pl.ANY)
    return pl.pallas_call(
        leave,
        in_specs=[anywhere] * (1 + len(others)),
        out_specs=anywhere,
        out_shape=jax.ShapeDtypeStruct(x.shape, x.dtype),
        input_output_aliases={0: 0},
        name="after",
    )(x, *others)


def layer_norm(values, gain_vec):
    center = values - jnp.mean(values, axis=-1, keepdims=True)
    spread = jnp.mean(center * center, axis=-1, keepdims=True)
    return center * lax.rsqrt(spread + 1e-05) * gain_vec


def attend_fwd_kernel(q_ref, k_ref, v_ref, o_ref, lse_ref, *, scale, block):
    length, width = q_ref.shape
    heads = width // HEAD_DIM
    lane = lax.broadcasted_iota(jnp.int32, (1, width), 1) // HEAD_DIM
    lane_block = lax.broadcasted_iota(jnp.int32, (block, width), 1)
    keys = k_ref[...]
    values = v_ref[...]
    zero = jnp.zeros((), BF16)
    masked = [jnp.where(lane == h, keys, zero) for h in range(heads)]
    for b in range(length // block):
        rows = pl.ds(b * block, block)
        q = (q_ref[rows, :].astype(F32) * scale).astype(BF16)
        result = jnp.zeros((block, width), F32)
        stats = jnp.zeros((block, width), F32)
        for h in range(heads):
            s = dot(q, masked[h], NT)
            top = jnp.max(s, axis=1, keepdims=True)
            p = jnp.exp(s - top)
            total = jnp.sum(p, axis=1, keepdims=True)
            o = dot((p * (1.0 / total)).astype(BF16), values)
            result = jnp.where(lane == h, o, result)
            stats = jnp.where(lane_block == h, top + jnp.log(total), stats)
        o_ref[rows, :] = result.astype(BF16)
        lse_ref[0, :, pl.ds(b * block, block)] = stats.T[:8, :]


def attend_fwd(projected, local_width):
    length = projected.shape[0]
    width = 2 * HEAD_DIM
    pairs = local_width // width
    spec = lambda part: pl.BlockSpec((length, width), lambda i: (0, part * pairs + i))
    return pl.pallas_call(
        functools.partial(attend_fwd_kernel, scale=HEAD_DIM**-0.5, block=512),
        grid=(pairs,),
        in_specs=[spec(0), spec(1), spec(2)],
        out_specs=[
            pl.BlockSpec((length, width), lambda i: (0, i)),
            pl.BlockSpec((1, 8, length), lambda i: (i, 0, 0)),
        ],
        out_shape=[
            jax.ShapeDtypeStruct((length, local_width), BF16),
            jax.ShapeDtypeStruct((pairs, 8, length), F32),
        ],
        compiler_params=pltpu.CompilerParams(vmem_limit_bytes=48 * 1024 * 1024),
        cost_estimate=cost(
            12 * length * length * local_width, 8 * length * local_width, length * length * pairs * 2
        ),
        name="attend_fwd",
    )(projected, projected, projected)


def attend_bwd_kernel(
    q_ref, k_ref, v_ref, g_ref, o_ref, lse_ref, out_ref, dq_ref, dk_ref, dv_ref, *, scale, block
):
    length, width = q_ref.shape
    heads = width // HEAD_DIM
    step = pl.program_id(1)

    @pl.when(step == 0)
    def _():
        lane = lax.broadcasted_iota(jnp.int32, (1, width), 1) // HEAD_DIM
        keys = k_ref[...]
        values = v_ref[...]
        zero = jnp.zeros((), BF16)
        key_cols = keys.T
        prod = g_ref[...].astype(F32) * o_ref[...].astype(F32)
        pick = (
            lax.broadcasted_iota(jnp.int32, (8, width), 1) // HEAD_DIM
            == lax.broadcasted_iota(jnp.int32, (8, width), 0)
        ).astype(F32)
        inner = dot(pick, prod, NT, HIGHEST)
        for h in range(heads):
            k_h = jnp.where(lane == h, keys, zero)
            v_h = jnp.where(lane == h, values, zero)
            for b in range(length // block):
                rows = pl.ds(b * block, block)
                q = (q_ref[rows, :].astype(F32) * scale).astype(BF16)
                g = g_ref[rows, :]
                s = dot(k_h, q, NT)
                p = jnp.exp(s - lse_ref[0, h : h + 1, b * block : (b + 1) * block])
                dp = dot(v_h, g, NT)
                ds = (p * (dp - inner[h : h + 1, b * block : (b + 1) * block])).astype(BF16)
                dv = dot(p.astype(BF16), jnp.where(lane == h, g, zero))
                dk = dot(ds, jnp.where(lane == h, q, zero))
                if h == 0 and b == 0:
                    dv_ref[...] = dv
                    dk_ref[...] = dk
                else:
                    dv_ref[...] += dv
                    dk_ref[...] += dk
                dq_ref[h * HEAD_DIM : (h + 1) * HEAD_DIM, b * block : (b + 1) * block] = (
                    dot(key_cols[h * HEAD_DIM : (h + 1) * HEAD_DIM, :], ds) * scale
                )
        out_ref[...] = dq_ref[...].T.astype(BF16)

    @pl.when(step == 1)
    def _():
        out_ref[...] = dk_ref[...].astype(BF16)

    @pl.when(step == 2)
    def _():
        out_ref[...] = dv_ref[...].astype(BF16)


def attend_bwd(projected, grad_heads, attended, lse, local_width):
    length = projected.shape[0]
    width = 2 * HEAD_DIM
    pairs = local_width // width
    spec = lambda part: pl.BlockSpec((length, width), lambda i, j: (0, part * pairs + i))
    return pl.pallas_call(
        functools.partial(attend_bwd_kernel, scale=HEAD_DIM**-0.5, block=256),
        grid=(pairs, 3),
        in_specs=[
            spec(0),
            spec(1),
            spec(2),
            spec(0),
            spec(0),
            pl.BlockSpec((1, 8, length), lambda i, j: (i, 0, 0)),
        ],
        out_specs=pl.BlockSpec((length, width), lambda i, j: (0, j * pairs + i)),
        out_shape=jax.ShapeDtypeStruct((length, 3 * local_width), BF16),
        scratch_shapes=[
            pltpu.VMEM((width, length), F32),
            pltpu.VMEM((length, width), F32),
            pltpu.VMEM((length, width), F32),
        ],
        compiler_params=pltpu.CompilerParams(vmem_limit_bytes=48 * 1024 * 1024),
        cost_estimate=cost(
            24 * length * length * local_width, 16 * length * local_width, length * length * pairs * 2
        ),
        name="attend_bwd",
    )(projected, projected, projected, grad_heads, attended, lse)


def mlp_mid_kernel(nb_ref, gm_ref, up_ref, down_ref, act_ref, gup_ref, *, block):
    up = up_ref[...]
    down = down_ref[...]
    for b in range(nb_ref.shape[0] // block):
        rows = pl.ds(b * block, block)
        value, slope = gelu_parts(dot(nb_ref[rows, :], up))
        act_ref[rows, :] = value.astype(BF16)
        gup_ref[rows, :] = (slope * dot(gm_ref[rows, :], down)).astype(BF16)


def mlp_mid(normed, grad, up_full, down_full):
    rows, depth = normed.shape
    width = up_full.shape[1]
    cols = min(width, 512)
    block = rows
    for cand in (416, 192):
        if rows % cand == 0:
            block = cand
            break
    whole = pl.BlockSpec((rows, depth), lambda i: (0, 0))
    weight = pl.BlockSpec((depth, cols), lambda i: (0, i))
    result = pl.BlockSpec((rows, cols), lambda i: (0, i))
    return pl.pallas_call(
        functools.partial(mlp_mid_kernel, block=block),
        grid=(width // cols,),
        in_specs=[whole, whole, weight, weight],
        out_specs=[result, result],
        out_shape=[jax.ShapeDtypeStruct((rows, width), BF16)] * 2,
        compiler_params=pltpu.CompilerParams(vmem_limit_bytes=48 * 1024 * 1024),
        cost_estimate=cost(
            8 * rows * depth * width, 4 * (rows + width) * depth + 4 * rows * width, rows * width
        ),
        name="mlp_mid",
    )(normed, grad, up_full, down_full)


def mlp_tri_kernel(nb_ref, up_ref, down_ref, out_ref):
    value, _ = gelu_parts(dot(nb_ref[...], up_ref[...]))
    part = dot(value.astype(BF16), down_ref[...], NT)

    @pl.when(pl.program_id(0) == 0)
    def _():
        out_ref[...] = part

    @pl.when(pl.program_id(0) > 0)
    def _():
        out_ref[...] += part


def mlp_tri(normed, up_full, down_full):
    rows, depth = normed.shape
    width = up_full.shape[1]
    cols = min(width, 512)
    whole = pl.BlockSpec((rows, depth), lambda i: (0, 0))
    weight = pl.BlockSpec((depth, cols), lambda i: (0, i))
    return pl.pallas_call(
        mlp_tri_kernel,
        grid=(width // cols,),
        in_specs=[whole, weight, weight],
        out_specs=whole,
        out_shape=jax.ShapeDtypeStruct((rows, depth), F32),
        compiler_params=pltpu.CompilerParams(vmem_limit_bytes=32 * 1024 * 1024),
        cost_estimate=cost(4e9, 4 * width * depth, rows * width),
        name="mlp_tri",
    )(normed, up_full, down_full)


def weight_grad_kernel(place_ref, *refs, segments, pieces):
    step = pl.program_id(0)
    rest = refs[2 * sum(n for n, _, _ in segments) :]
    outs, turned = rest[:pieces], rest[pieces:]
    at = 0
    for parts, first, last in segments:
        lefts, rights = refs[at : at + parts], refs[at + parts : at + 2 * parts]
        at += 2 * parts

        @pl.when(step == first)
        def _():
            for left, spot in zip(lefts, turned):
                rows = left.shape[0]
                for j in range(left.shape[1] // 128):
                    both = left[:, j * 128 : (j + 1) * 128].T
                    for k in range(2):
                        to = pl.multiple_of(place_ref[2 * j + k] * 64, 64)
                        spot[pl.ds(to, 64), :rows] = both[k * 64 : (k + 1) * 64]

        @pl.when((step >= first) & (step <= last))
        def _():
            total = sum(
                dot(spot[:, : right.shape[0]], right[...]) for spot, right in zip(turned, rights)
            )
            for i, out in enumerate(outs):
                rows = out.shape[0]
                out[...] = total[i * rows : (i + 1) * rows].astype(BF16)


def weight_grad(place, pieces, *segments):
    specs, args, marks = [], [], []
    first = 0
    cols = min(512, *(rights[0].shape[1] for _, rights in segments))
    depth = segments[0][0][0].shape[1]
    for lefts, rights in segments:
        steps = rights[0].shape[1] // cols
        for left in lefts:
            specs.append(pl.BlockSpec(left.shape, lambda i, place: (0, 0)))
            args.append(left)
        for right in rights:
            specs.append(
                pl.BlockSpec(
                    (right.shape[0], cols),
                    lambda i, place, a=first, b=steps: (0, jnp.clip(i - a, 0, b - 1)),
                )
            )
            args.append(right)
        marks.append((len(lefts), first, first + steps - 1))
        first += steps
    parts = segments[0][0]
    result = jax.ShapeDtypeStruct((depth // pieces, first * cols), BF16)
    return pl.pallas_call(
        functools.partial(weight_grad_kernel, segments=tuple(marks), pieces=pieces),
        grid_spec=pltpu.PrefetchScalarGridSpec(
            num_scalar_prefetch=1,
            grid=(first,),
            in_specs=specs,
            out_specs=[pl.BlockSpec((depth // pieces, cols), lambda i, place: (0, i))] * pieces,
            scratch_shapes=[pltpu.VMEM((depth, left.shape[0]), BF16) for left in parts],
        ),
        out_shape=[result] * pieces,
        compiler_params=pltpu.CompilerParams(vmem_limit_bytes=40 * 1024 * 1024),
        cost_estimate=cost(
            3 * depth * first * cols * sum(left.shape[0] for left in parts), 8 * depth * first * cols
        ),
        name="weight_grad",
    )(place, *args)


def split_halves(x):
    high = x.astype(BF16)
    return high, (x - high.astype(F32)).astype(BF16)


def dot_fine(a, b):
    a_high, a_low = split_halves(a)
    b_high, b_low = split_halves(b)
    return dot(
        jnp.concatenate([a_high, a_high, a_low], axis=1),
        jnp.concatenate([b_high, b_low, b_high], axis=0),
    )


def dot_fine_lanes(a, b):
    rows, cols = a.shape[0], b.shape[0]
    both = dot(
        jnp.concatenate(split_halves(a), axis=0), jnp.concatenate(split_halves(b), axis=0), NT
    )
    return both[:rows, :cols] + both[:rows, cols:] + both[rows:, :cols]


def scene_kernel(
    own_ref,
    tokens_ref,
    w_ref,
    spot_ref,
    edge_ref,
    cot_ref,
    net_ref,
    colors_ref,
    units_ref,
    gtok_ref,
    gdi_ref,
    gdb_ref,
    gdo_ref,
    gci_ref,
    gcb_ref,
    gco_ref,
    table_ref,
    hot_ref,
    grad_ref,
    *,
    per_slab,
):
    step = pl.program_id(0)
    block = spot_ref.shape[1]
    ends = 2 * block

    @pl.when(step == 0)
    def _():
        units = dot(tokens_ref[...], w_ref[...])
        for p in range(3):
            rows = jnp.concatenate(
                [
                    units[p * PLANE_TOKENS : (p + 1) * PLANE_TOKENS, r * CELLS : (r + 1) * CELLS]
                    for r in range(PATCH)
                ],
                axis=0,
            )
            high, low = split_halves(rows.T)
            table_ref[p, :CELLS, :] = high
            table_ref[p, CELLS:, :] = low
        grad_ref[...] = jnp.zeros_like(grad_ref)
        for ref in (gdi_ref, gdb_ref, gdo_ref, gci_ref, gcb_ref, gco_ref):
            ref[...] = jnp.zeros_like(ref)

    net = net_ref[...]
    dens_in, color_in = net[:, :FEAT], net[:, FEAT : 2 * FEAT]
    color_out_t = net[:, 2 * FEAT : 2 * FEAT + 8]
    at = 2 * FEAT + 8
    dens_bias, dens_out, color_bias = net[:, at : at + 1], net[:, at + 1 : at + 2], net[:, at + 2 : at + 3]
    dens_in_t, color_in_t, color_out = dens_in.T, color_in.T, color_out_t.T
    iota = lax.broadcasted_iota(jnp.int32, (SPOTS, ends), 0)
    field = jnp.zeros((FEAT, ends), F32)
    columns = []
    for p in range(3):
        spot = jnp.concatenate([spot_ref[p : p + 1, :], spot_ref[3 + p : 4 + p, :]], axis=1)
        column = jnp.concatenate([spot_ref[6 + p : 7 + p, :], spot_ref[9 + p : 10 + p, :]], axis=1)
        columns.append(column)
        hot = jnp.where(iota == spot, 1.0, 0.0).astype(BF16)
        hot_ref[p] = hot
        found = dot(table_ref[p], hot)
        found = found[:CELLS] + found[CELLS:]
        for c in range(PATCH):
            field = field + jnp.where(column == c, found[c * FEAT : (c + 1) * FEAT], 0.0)

    w_a = edge_ref[0:1, :]
    w_b = edge_ref[1:2, :]
    inside = edge_ref[2:3, :]
    live = edge_ref[3:4, :]
    pre_d = dot_fine(dens_in, field) + dens_bias
    act_d, slope_d = gelu_parts(pre_d)
    dens = jnp.sum(act_d * dens_out, axis=0, keepdims=True)
    v_dens = w_a * dens[:, :block] + w_b * inside * dens[:, block:]
    v_feat = w_a * field[:, :block] + w_b * field[:, block:]
    pre_c = dot_fine(color_in, v_feat) + color_bias
    act_c, slope_c = gelu_parts(pre_c)
    shade = jax.nn.sigmoid(dot_fine(color_out, act_c))
    opacity = jax.nn.sigmoid(v_dens)
    colors_ref[...] = live * opacity * shade
    g_color = cot_ref[...] * live
    g_shade = g_color * opacity
    g_logit = g_shade * shade * (1.0 - shade)
    g_dens = jnp.sum(g_color * shade, axis=0, keepdims=True) * opacity * (1.0 - opacity)
    g_pre_c = dot_fine(color_out_t, g_logit) * slope_c
    g_feat = dot_fine(color_in_t, g_pre_c)
    g_dens2 = jnp.concatenate([w_a * g_dens, w_b * inside * g_dens], axis=1)
    g_pre_d = dens_out * g_dens2 * slope_d
    g_field = dot_fine(dens_in_t, g_pre_d) + jnp.concatenate(
        [w_a * g_feat, w_b * g_feat], axis=1
    )

    @pl.when(step // per_slab == own_ref[0])
    def _():
        gco_ref[...] += dot_fine_lanes(g_logit, act_c)
        gci_ref[...] += dot_fine_lanes(g_pre_c, v_feat)
        gcb_ref[...] += jnp.sum(g_pre_c, axis=1, keepdims=True)
        gdi_ref[...] += dot_fine_lanes(g_pre_d, field)
        gdb_ref[...] += jnp.sum(g_pre_d, axis=1, keepdims=True)
        gdo_ref[...] += jnp.sum(act_d * g_dens2, axis=1, keepdims=True)

    for p in range(3):
        spread = jnp.concatenate(
            [jnp.where(columns[p] == c, g_field, 0.0) for c in range(PATCH)], axis=0
        )
        grad_ref[p] += dot(hot_ref[p], spread.astype(BF16), NT)

    @pl.when(step == pl.num_programs(0) - 1)
    def _():
        for p in range(3):
            for r in range(PATCH):
                units_ref[
                    p * PLANE_TOKENS : (p + 1) * PLANE_TOKENS, r * CELLS : (r + 1) * CELLS
                ] = grad_ref[p, r * PLANE_TOKENS : (r + 1) * PLANE_TOKENS, :].astype(BF16)
        gtok_ref[...] = dot(units_ref[...], w_ref[...], NT)


def scene_pass(tokens, w_unpatch, spots, edges, cot, own, small, slab_edges):
    dens_in, dens_bias, dens_out, color_in, color_bias, color_out = small
    net = jnp.concatenate(
        [
            dens_in,
            color_in,
            jnp.pad(color_out.T, ((0, 0), (0, 8 - color_out.shape[0]))),
            dens_bias[:, None],
            dens_out[:, None],
            color_bias[:, None],
        ],
        axis=1,
    )
    net = jnp.pad(net, ((0, 0), (0, 128 - net.shape[1])))
    total = spots.shape[1]
    block = min(512, slab_edges)
    const = lambda shape: pl.BlockSpec(shape, lambda i, own: (0,) * len(shape))
    lanes = lambda rows: pl.BlockSpec((rows, block), lambda i, own: (0, i))
    dens, colr = dens_in.shape[0], color_in.shape[0]
    outs = [
        ((8, total), F32, lanes(8)),
        ((TRI, w_unpatch.shape[1]), BF16, None),
        ((TRI, w_unpatch.shape[0]), F32, None),
        ((dens, FEAT), F32, None),
        ((dens, 1), F32, None),
        ((dens, 1), F32, None),
        ((colr, FEAT), F32, None),
        ((colr, 1), F32, None),
        ((8, colr), F32, None),
    ]
    return pl.pallas_call(
        functools.partial(scene_kernel, per_slab=slab_edges // block),
        grid_spec=pltpu.PrefetchScalarGridSpec(
            num_scalar_prefetch=1,
            grid=(total // block,),
            in_specs=[
                const(tokens.shape),
                const(w_unpatch.shape),
                lanes(16),
                lanes(8),
                lanes(8),
                const((dens, 128)),
            ],
            out_specs=[s if s is not None else const(shape) for shape, _, s in outs],
            scratch_shapes=[
                pltpu.VMEM((3, 2 * CELLS, SPOTS), BF16),
                pltpu.VMEM((3, SPOTS, 2 * block), BF16),
                pltpu.VMEM((3, SPOTS, CELLS), F32),
            ],
        ),
        out_shape=[jax.ShapeDtypeStruct(shape, kind) for shape, kind, _ in outs],
        compiler_params=pltpu.CompilerParams(vmem_limit_bytes=56 * 1024 * 1024),
        cost_estimate=cost(25e9, 8 * w_unpatch.size, 1e6),
        name="scene",
    )(
        own,
        tokens,
        w_unpatch,
        spots,
        edges,
        cot,
        net,
    )


def edge_tables(edge_rows, blend_rows, live_counts, slab_planes):
    slabs, count = edge_rows.shape
    plane_cells = GRID * GRID
    slab_cells = slab_planes * plane_cells
    direction = edge_rows // slab_cells
    cell = edge_rows % slab_cells
    first = (jnp.arange(slabs, dtype=jnp.int32) * slab_planes)[:, None]
    i_a = cell // plane_cells + first
    j_a = (cell % plane_cells) // GRID
    l_a = cell % GRID
    i_b = i_a + (direction == 0)
    j_b = j_a + (direction == 1)
    l_b = l_a + (direction == 2)
    valid = (j_b < GRID) & (l_b < GRID)
    inside = valid & (i_b < GRID)

    def place(row, col, keep):
        spot = (row % PATCH) * PLANE_TOKENS + (row // PATCH) * SIDE + col // PATCH
        return jnp.where(keep, spot, -1), col % PATCH

    on = jnp.ones_like(valid)
    pairs = [
        place(i_a, j_a, on),
        place(i_a, l_a, on),
        place(j_a, l_a, on),
        place(i_b, j_b, inside),
        place(i_b, l_b, inside),
        place(j_b, l_b, inside),
    ]
    blank_i = jnp.zeros_like(edge_rows)
    spots = jnp.stack([a for a, _ in pairs] + [b for _, b in pairs] + [blank_i] * 4)
    w_b = blend_rows.astype(F32) / 16.0
    w_a = 1.0 - w_b
    live = jnp.arange(count, dtype=jnp.int32)[None, :] < live_counts
    blank = jnp.zeros_like(w_b)
    edges = jnp.stack(
        [w_a, w_b * valid.astype(F32), inside.astype(F32), live.astype(F32)] + [blank] * 4
    )
    return spots.reshape(16, slabs * count), edges.reshape(8, slabs * count)


def swap(x, axis="tp"):
    return lax.ppermute(x, axis, [(0, 1), (1, 0)])


def tp_sum(partial, *gates):
    if lax.axis_size("tp") == 2:
        return partial.astype(F32) + after(swap(partial), *gates).astype(F32)
    return lax.psum(partial.astype(F32), "tp")


def tp_parts(partial):
    count = lax.axis_size("tp")
    if count != 2:
        return partial, partial
    rows = partial.shape[0] // count
    me = lax.axis_index("tp")
    theirs = lax.dynamic_slice_in_dim(partial, (1 - me) * rows, rows, 0).astype(BF16)
    return lax.dynamic_slice_in_dim(partial, me * rows, rows, 0), theirs


def tp_sum_own(mine, theirs, *gates):
    if lax.axis_size("tp") == 2:
        return mine + after(swap(theirs), *gates).astype(F32)
    return lax.psum_scatter(mine, "tp", scatter_dimension=0, tiled=True)


def tp_rows(own):
    if lax.axis_size("tp") == 2:
        other = swap(own)
        first = lax.axis_index("tp") == 0
        return jnp.concatenate(
            [jnp.where(first, own, other), jnp.where(first, other, own)], axis=0
        )
    return lax.all_gather(own, "tp", axis=0, tiled=True)


LINE, WIDE, CORES = 4, 2, 2


def blocks_known():
    return lax.axis_size("seq") == LINE * WIDE * CORES


def own_places(blocks):
    block = jnp.arange(blocks, dtype=jnp.int32)
    if not blocks_known():
        return block
    me = lax.axis_index("seq")
    w, c = (me // CORES) % WIDE, me % CORES
    z, x, core = block // (WIDE * CORES), (block // CORES) % WIDE, block % CORES
    return ((core ^ c) * WIDE + (x ^ w)) * LINE + z


def hop(x, kind):
    pairs = []
    for i in range(LINE * WIDE * CORES):
        z, w, c = i // (WIDE * CORES), (i // CORES) % WIDE, i % CORES
        if kind == "core":
            c = 1 - c
        else:
            w = 1 - w
        pairs.append((i, (z * WIDE + w) * CORES + c))
    return lax.ppermute(x, "seq", pairs)


def along_line(x):
    step = WIDE * CORES
    groups = [[z * step + i for z in range(LINE)] for i in range(step)]
    return lax.all_to_all(x, "seq", 0, 0, axis_index_groups=groups, tiled=True)


def gather_plain(shard):
    return lax.all_gather(shard, "seq", axis=0, tiled=True)


def scatter_plain(grad):
    return lax.psum_scatter(grad, "seq", scatter_dimension=0, tiled=True)


def gather_line(shard):
    return along_line(jnp.concatenate([shard] * LINE, 0))


def assemble_kernel(place_ref, *refs):
    *parts, out_ref = refs
    for i, part in enumerate(parts):
        rows = part.shape[0]
        out_ref[pl.ds(pl.multiple_of(place_ref[i] * rows, rows), rows), :] = part[...]


def gather_rest(line, wide):
    me = lax.axis_index("seq")
    w, c = (me // CORES) % WIDE, me % CORES
    parts = [line, wide, hop(line, "core"), hop(wide, "core")]
    place = [(w ^ xr) * CORES + (c ^ cr) for cr in range(CORES) for xr in range(WIDE)]
    rows, width = line.shape[0] // LINE, line.shape[1]
    return pl.pallas_call(
        assemble_kernel,
        grid_spec=pltpu.PrefetchScalarGridSpec(
            num_scalar_prefetch=1,
            grid=(LINE,),
            in_specs=[pl.BlockSpec((rows, width), lambda i, place: (i, 0))] * len(parts),
            out_specs=pl.BlockSpec((len(parts) * rows, width), lambda i, place: (i, 0)),
        ),
        out_shape=jax.ShapeDtypeStruct((len(parts) * line.shape[0], width), line.dtype),
        cost_estimate=cost(0, 16 * line.size),
        compiler_params=pltpu.CompilerParams(vmem_limit_bytes=24 * 1024 * 1024),
        name="assemble",
    )(jnp.stack(place).astype(jnp.int32), *parts)


def add_rounded(a, b):
    return (a.astype(F32) + b.astype(F32)).astype(BF16)


def scatter_chip(near, far):
    if not blocks_known():
        return jnp.concatenate([near, far], 0)
    return add_rounded(near, hop(far, "core"))


def scatter_pair(chip):
    if not blocks_known():
        return chip
    half = chip.shape[0] // WIDE
    return add_rounded(chip[:half], hop(chip[half:], "x"))


def scatter_line(pair):
    if not blocks_known():
        return lax.psum_scatter(pair, "seq", scatter_dimension=0, tiled=True).astype(F32)
    parts = along_line(pair).reshape(LINE, -1, pair.shape[1])
    return jnp.sum(parts.astype(F32), axis=0)


def sum_by_hops(vec):
    for axis, steps in (("seq", (4, 8)), ("tp", (1,)), ("seq", (1, 2))):
        size = lax.axis_size(axis)
        if axis == "tp" and size > 2:
            steps = tuple(2**i for i in range(size.bit_length() - 1))
        if steps == (4, 8) and size > 16:
            steps = tuple(2**i for i in range(2, size.bit_length() - 1))
        for step in steps:
            vec = vec + lax.ppermute(vec, axis, [(i, i ^ step) for i in range(size)])
    return vec


def shards(
    layer_input,
    attn_gain,
    w_qkv,
    w_out,
    mlp_gain,
    w_up,
    w_down,
    w_unpatch,
    dens_in,
    dens_bias,
    dens_out,
    color_in,
    color_bias,
    color_out,
    edge_ids,
    blend_steps,
    live_count,
    color_grad,
    out_grad,
):
    tp_count = lax.axis_size("tp")
    tp_index = lax.axis_index("tp")
    length, model_width = layer_input.shape
    own_rows = length // tp_count
    own_tri = TRI // tp_count
    own_rest = own_rows - own_tri
    slab_planes = GRID // tp_count
    slab_edges = edge_ids.shape[1]

    def split_rows(x):
        blocks = x.reshape(tp_count, own_rows, x.shape[-1])
        return (
            blocks[:, own_rest:].reshape(TRI, x.shape[-1]),
            blocks[:, :own_rest].reshape(length - TRI, x.shape[-1]),
        )

    def block_rows(x):
        tri = x[:TRI].reshape(tp_count, own_tri, x.shape[-1])
        rest = x[TRI:].reshape(tp_count, own_rest, x.shape[-1])
        return jnp.concatenate([rest, tri], 1).reshape(length, x.shape[-1])

    def own_columns(x, width):
        if width == x.shape[1]:
            return x
        return lax.dynamic_slice_in_dim(x, tp_index * width, width, 1)

    def own_of(rows, count):
        return lax.dynamic_slice_in_dim(rows, tp_index * count, count, 0)

    packed = jnp.concatenate(
        [
            edge_ids.astype(F32),
            blend_steps.astype(F32),
            jnp.broadcast_to(live_count.astype(F32), edge_ids.shape),
            color_grad[:, 0],
        ],
        0,
    )
    slabs = tp_rows(packed).reshape(tp_count, packed.shape[0], slab_edges)
    spots, edges = edge_tables(
        slabs[:, 0].astype(jnp.int32), slabs[:, 1], slabs[:, 2, :1].astype(jnp.int32), slab_planes
    )
    cot = slabs[:, 3:].swapaxes(0, 1).reshape(-1, tp_count * slab_edges)
    cot = jnp.pad(cot, ((0, 8 - cot.shape[0]), (0, 0)))

    places = own_places(model_width // 64)
    in_order = jnp.arange(model_width // 64, dtype=jnp.int32)
    x_tri, x_rest = split_rows(layer_input)
    rows_in = jnp.concatenate([x_tri, x_rest], 0)
    og_tri, og_rest = split_rows(out_grad)
    gm_rest = og_rest.astype(BF16)
    og_own = own_of(og_rest, own_rest)

    local_width = w_out.shape[0]
    first = gather_plain(jnp.concatenate([w_qkv.reshape(w_qkv.shape[0], -1), w_out.T], 1))
    first = after(first, spots, edges, cot, gm_rest, rows_in)
    if blocks_known():
        line_u = gather_line(w_up)
        first = after(first, line_u)
    else:
        line_u = w_up
    down_t = gather_plain(after(w_down.T, first))
    qkv_full, out_t = first[:, : 3 * local_width], first[:, 3 * local_width :]

    normed_a = layer_norm(rows_in.astype(F32), attn_gain).astype(BF16)
    projected = dot(normed_a, qkv_full).astype(BF16)
    attended, lse = attend_fwd(projected, local_width)
    if blocks_known():
        wide_u = hop(line_u, "x")
        up_full = gather_rest(line_u, wide_u)
    else:
        wide_u = line_u
        up_full = gather_plain(w_up)
    rest_own = own_of(x_rest, own_rest).astype(F32)
    out_tri = dot(attended[:TRI], out_t, NT)
    mine, theirs = tp_parts(dot(after(attended, out_tri)[TRI:], out_t, NT))
    hidden_tri = x_tri.astype(F32) + tp_sum(out_tri, theirs)
    hidden_rest = rest_own + tp_sum_own(mine, theirs)

    normed_own = layer_norm(hidden_rest, mlp_gain).astype(BF16)
    unpatch_full = gather_plain(after(w_unpatch, hidden_tri, normed_own, wide_u))

    normed_tri = layer_norm(hidden_tri, mlp_gain).astype(BF16)
    tokens = (hidden_tri + tp_sum(mlp_tri(normed_tri, up_full, down_t).astype(BF16))).astype(BF16)
    normed_rest = tp_rows(normed_own)

    act_rest, gup_rest = mlp_mid(after(normed_rest, tokens), gm_rest, up_full, down_t)
    gnb_mine, gnb_theirs = tp_parts(dot(gup_rest, up_full, NT))
    tokens = after(tokens, gnb_theirs)

    (
        colors_all,
        grad_units,
        grad_tokens,
        g_dens_in,
        g_dens_bias,
        g_dens_out,
        g_color_in,
        g_color_bias,
        g_color_out,
    ) = scene_pass(
        tokens,
        unpatch_full,
        spots,
        edges,
        cot,
        tp_index[None].astype(jnp.int32),
        (dens_in, dens_bias, dens_out, color_in, color_bias, color_out),
        slab_edges,
    )
    colors = lax.dynamic_slice_in_dim(
        colors_all[: color_out.shape[0]], tp_index * slab_edges, slab_edges, 1
    )
    gnb_rest = tp_sum_own(gnb_mine, gnb_theirs, grad_tokens)
    go_tri = og_tri + grad_tokens
    gm_tri = go_tri.astype(BF16)
    act_tri, gup_tri = mlp_mid(normed_tri, gm_tri, up_full, down_t)
    gnb_tri = tp_sum(dot(gup_tri, up_full, NT).astype(BF16))
    grad_down = weight_grad(in_order, 1, ((gm_rest, gm_tri), (act_rest, act_tri)))[0]
    sum_down = scatter_plain(grad_down).astype(F32)
    width = grad_units.shape[1] // tp_count if tp_count == 2 else grad_units.shape[1]
    sum_unpatch = scatter_plain(dot(tokens, own_columns(grad_units, width), TN).astype(BF16))
    grad_up = weight_grad(places, 2, ((normed_rest, normed_tri), (gup_rest, gup_tri)))
    _, back_rest = jax.vjp(layer_norm, hidden_rest, mlp_gain)
    gh_rest, gain_rest = back_rest(gnb_rest)
    _, back_tri = jax.vjp(lambda h: layer_norm(h, mlp_gain), hidden_tri)
    gh_tri = back_tri(gnb_tri)[0] + go_tri
    _, back_gain = jax.vjp(lambda g: layer_norm(own_of(hidden_tri, own_tri), g), mlp_gain)
    grad_mlp_gain = gain_rest + back_gain(own_of(gnb_tri, own_tri))[0]
    gh_rest = gh_rest + og_own
    branch = jnp.concatenate([gh_tri.astype(BF16), tp_rows(gh_rest.astype(BF16))], 0)

    smalls = (
        grad_mlp_gain,
        g_dens_in,
        g_dens_bias,
        g_dens_out,
        g_color_in,
        g_color_bias,
        g_color_out[: color_out.shape[0]],
    )
    flat = sum_by_hops(jnp.concatenate([s.reshape(-1) for s in smalls]))

    chip_up = scatter_chip(*grad_up)
    grad_heads = dot(branch, out_t).astype(BF16)
    grad_heads = after(grad_heads, chip_up, grad_down, flat)
    pair_up = scatter_pair(chip_up)
    grad_proj = attend_bwd(projected, grad_heads, attended, lse, local_width)
    grad_proj = after(grad_proj, pair_up)
    sum_up = scatter_line(pair_up)
    gna = dot(grad_proj, qkv_full, NT)
    gna_sum = tp_sum_own(*tp_parts(block_rows(gna)))
    chip_last = scatter_chip(
        *weight_grad(places, 2, ((normed_a,), (grad_proj,)), ((branch,), (attended,)))
    )
    pair_last = scatter_pair(chip_last)
    sum_last = scatter_line(after(pair_last, gna_sum))
    _, back_gain_a = jax.vjp(lambda g: layer_norm(rows_in.astype(F32), g), attn_gain)
    grad_attn_gain = back_gain_a(gna)[0]
    tri_own = own_of(x_tri, own_tri).astype(F32)
    _, back_a = jax.vjp(
        lambda v: layer_norm(v, attn_gain), jnp.concatenate([rest_own, tri_own], 0)
    )
    grad_input = back_a(gna_sum)[0] + jnp.concatenate(
        [gh_rest, own_of(gh_tri, own_tri)], 0
    )
    if tp_count == 2:
        other = swap(sum_unpatch)
        low = tp_index == 0
        sum_unpatch = jnp.concatenate(
            [jnp.where(low, sum_unpatch, other), jnp.where(low, other, sum_unpatch)], 1
        )
    sum_unpatch = sum_unpatch.astype(F32)

    weight_sums = (
        sum_last[:, : 3 * local_width].reshape(w_qkv.shape),
        sum_last[:, 3 * local_width :].T,
        sum_up,
        sum_down.T,
        sum_unpatch,
    )
    small_sums = [sum_by_hops(after(grad_attn_gain, pair_last))]
    at = 0
    for s in smalls:
        small_sums.append(flat[at : at + s.size].reshape(s.shape))
        at += s.size
    for i in (3, 4, 6):
        small_sums[i] = small_sums[i].reshape(-1)
    return (
        colors[:, None, :],
        grad_input,
        small_sums[0],
        weight_sums[0],
        weight_sums[1],
        small_sums[1],
        weight_sums[2],
        weight_sums[3],
        weight_sums[4],
        small_sums[2],
        small_sums[3],
        small_sums[4],
        small_sums[5],
        small_sums[6],
        small_sums[7],
    )


def solution(mesh):
    placed = (
        P("seq", None),
        P(),
        P("seq", None, "tp"),
        P("tp", "seq"),
        P(),
        P("seq", "tp"),
        P("tp", "seq"),
        P("seq", None),
        P(),
        P(),
        P(),
        P(),
        P(),
        P(),
        P("seq", "tp"),
        P("seq", "tp"),
        P("seq", "tp"),
        P(None, "seq", "tp"),
        P("seq", None),
    )
    return jax.shard_map(
        shards,
        mesh=mesh,
        in_specs=placed,
        out_specs=(
            P(None, "seq", "tp"),
            P(("seq", "tp"), None),
            P(),
            P("seq", None, "tp"),
            P("tp", "seq"),
            P(),
            P("seq", "tp"),
            P("tp", "seq"),
            P("seq", None),
            P(),
            P(),
            P(),
            P(),
            P(),
            P(),
        ),
        check_vma=False,
    )
```

time: 1620 us -> 489 us (0.30)
  matrix products: 544 us -> 28.4 us
  waiting for transfers between devices: 483 us -> 130 us
  local copies, waits for them, and re-layouts: 272 us -> 77 us
  other arithmetic: 236 us -> 70 us
  Pallas kernels: 0 us -> 120 us
  blocking collectives: 48.4 us -> 0 us
  starting transfers between devices: 4.41 us -> 42.7 us
    dot_general x43 -> x8, matrix products: 544 us -> 28.4 us  [dot(): lax.dot_general(a, b, dims, precision=precision, preferred_element_type=F32)]
    reduce_scatter x9 -> x2, waiting for transfers between devices: 239 us -> 0.01 us  [scatter_plain(): return lax.psum_scatter(grad, 'seq', scatter_dimension=0, tiled=True)]
    all_gather x7 -> x3, waiting for transfers between devices: 208 us -> 45.7 us  [gather_plain(): return lax.all_gather(shard, 'seq', axis=0, tiled=True)]
    scatter-add x9 -> x0, other arithmetic: 125 us -> none  [the longest x6 111 us: shards(): field_grad = jnp.zeros((FEAT, ext_cells), jnp.float32).at[:, flat_a].add(...]
    pallas_call x0 -> x23, Pallas kernels: none -> 120 us  [the longest x1 29 us: attend_bwd(): pl.pallas_call(functools.partial(attend_bwd_kernel, scale=HEAD_DIM ** (-0...]
    ppermute x2 -> x27, waiting for transfers between devices: 1.85 us -> 84.2 us  [the longest x10 50.9 us: swap(): return lax.ppermute(x, axis, [(0, 1), (1, 0)])]
    scatter-add x3 -> x0, local copies, waits for them, and re-layouts: 41.1 us -> none  [shards(): field_grad = jnp.zeros((FEAT, ext_cells), jnp.float32).at[:, flat_a].add(...]
    psum x1 -> x0, blocking collectives: 41 us -> none  [shards(): lax.psum((grad_attn_gain, grad_mlp_gain, grad_dens_in, grad_dens_bias, gr...]
  transfers between devices with their start and end apart: 19 -> 35, of which waited for: 15 -> 17; matrix products, arithmetic and copies ran while one was open for 23% -> 27% of each run, Pallas kernels for 0% -> 25%
where the time goes in v1:
time: 489 us; the launch traced here: 483 us
  waiting for transfers between devices  130 us (27%)
  Pallas kernels  120 us (25%)
  local copies, waits for them, and re-layouts  77 us (16%)
  other arithmetic  70 us (14%)
  starting transfers between devices  42.7 us (9%)
  matrix products  28.4 us (6%)
  between operations  15.9 us (3%)
    ppermute x10, waiting for transfers between devices, swap(): return lax.ppermute(x, axis, [(0, 1), (1, 0)])  50.9 us
    unnamed x207, local copies, waits for them, and re-layouts  46.9 us
    all_gather x3, waiting for transfers between devices, gather_plain(): return lax.all_gather(shard, 'seq', axis=0, tiled=True)  45.7 us
    ppermute x10, waiting for transfers between devices, sum_by_hops(): vec = vec + lax.ppermute(vec, axis, [(i, i ^ step) for i in range(size)])  29.7 us
    pallas_call x1, Pallas kernels, attend_bwd(): pl.pallas_call(functools.partial(attend_bwd_kernel, scale=HEAD_DIM ** (-0...  29 us
    dot_general x8, matrix products, dot(): lax.dot_general(a, b, dims, precision=precision, preferred_element_type=F32)  28.4 us
    pallas_call x3, Pallas kernels, weight_grad(): pl.pallas_call(functools.partial(weight_grad_kernel, segments=tuple(marks...  24.9 us
    pallas_call x1, Pallas kernels, scene_pass(): pl.pallas_call(functools.partial(scene_kernel, per_slab=slab_edges // blo...  22.6 us
  transfers between devices with their start and end apart: 35, of which 17 were waited for; matrix products, arithmetic and copies ran while one was open for 27% of the time, Pallas kernels for 25%

profile of v1, /device:TPU:0, one launch (start us, length us, event | category | flops | bytes accessed | tf_op | source)
XLA Modules:
  0.0 483.5 jit_solution(7621446426168665319)
XLA Ops:
  14.0 3.0 collective-permute-start
  18.1 4.9 %all-to-all-start = ((bf16[4,64,2048]{2,1,0:T(8,128)(2,1)}), bf16[4,64,2048]{2,1,0:T(8,128)(2,1)S(1)}, u32[]{:S(2)}, u32[]{:S(2)}) async-start(bf16[4,64,2048]{2,1,0:T(8,128)(2,1)} %bitcast.12), calls=%async_computation | async-start | bytes 2097152 | tf_op jit(solution)/shard_map/all_to_all | solution.py:653
  34.8 45.6 %all-gather.4.cloned.1.call-done.refs_0_ = bf16[1024,2048]{1,0:T(8,128)(2,1)} async-done(((bf16[64,2048]{1,0:T(8,128)(2,1)}), bf16[1024,2048]{1,0:T(8,128)(2,1)}) %all-gather.4.cloned.1.call-update) | async-done | bytes 4194320 | tf_op jit(solution)/shard_map/all_gather | solution.py:657
  85.3 3.6 convolution_convert_fusion.q_ref.k_ref.v_ref
  90.3 15.5 %attend_fwd.1 = (bf16[1024,512]{1,0:T(8,128)(2,1)S(1)}, f32[4,8,1024]{2,1,0:T(8,128)S(1)}) custom-call(bf16[1024,1536]{1,0:T(8,128)(2,1)S(1)} %convolution_convert_fusion.q_ref.k_ref.v_ref, bf16[1024,1536]{1,0:T(8,128)(2,1)S(1)} %convolution_convert_fusion.q_ref.k_ref.v_ref, bf16[1024,1536]{1,0:T(8,128)(2,1)S(1)} %convolution_convert_fusion.q_ref.k_ref.v_ref), custom_call_target="tpu_custom_call" | custom-call | flops 6442450944 | bytes 4194304 | tf_op jit(solution)/shard_map/attend_fwd/pallas_call | solution.py:101
  109.9 2.6 fusion.11
  116.9 12.3 %collective-permute-done.1.refs_0_ = f32[192,1024]{1,0:T(8,128)} collective-permute-done((f32[192,1024]{1,0:T(8,128)}, f32[192,1024]{1,0:T(8,128)}, u32[]{:S(2)}, u32[]{:S(2)}) %collective-permute-start.1) | collective-permute-done | bytes 786464 | tf_op jit(solution)/shard_map/ppermute | solution.py:586
  129.1 2.5 fusion.46
  131.6 15.1 %collective-permute-done.6 = bf16[416,1024]{1,0:T(8,128)(2,1)} collective-permute-done((bf16[416,1024]{1,0:T(8,128)(2,1)}, bf16[416,1024]{1,0:T(8,128)(2,1)}, u32[]{:S(2)}, u32[]{:S(2)}) %collective-permute-start.6) | collective-permute-done | bytes 852000 | tf_op jit(solution)/shard_map/ppermute | solution.py:586
  146.7 2.1 fusion.45
  152.2 2.1 slice.159
  156.2 2.7 assemble.1.up_ref
  159.0 2.0 copy-done.7
  163.9 2.3 copy-done.8
  166.3 2.2 copy-done.27
  168.5 5.0 %mlp_tri.1 = f32[192,1024]{1,0:T(8,128)S(1)} custom-call(bf16[192,1024]{1,0:T(8,128)(2,1)S(1)} %multiply_convert_fusion.1.nb_ref.refs_1_, bf16[1024,2048]{1,0:T(8,128)(2,1)S(1)} %copy-done.8, bf16[1024,2048]{1,0:T(8,128)(2,1)S(1)} %copy-done.27), custom_call_target="tpu_custom_call" | custom-call | flops 4000000000 | bytes 8388608 | tf_op jit(solution)/shard_map/mlp_tri/pallas_call | solution.py:260
  174.2 9.5 %collective-permute-done.7 = bf16[416,1024]{1,0:T(8,128)(2,1)S(1)} collective-permute-done((bf16[416,1024]{1,0:T(8,128)(2,1)}, bf16[416,1024]{1,0:T(8,128)(2,1)S(1)}, u32[]{:S(2)}, u32[]{:S(2)}) %collective-permute-start.7) | collective-permute-done | bytes 852000 | tf_op jit(solution)/shard_map/ppermute | solution.py:586
  185.6 5.7 %collective-permute-done.5 = bf16[192,1024]{1,0:T(8,128)(2,1)S(1)} collective-permute-done((bf16[192,1024]{1,0:T(8,128)(2,1)S(1)}, bf16[192,1024]{1,0:T(8,128)(2,1)S(1)}, u32[]{:S(2)}, u32[]{:S(2)}) %collective-permute-start.5) | collective-permute-done | bytes 393248 | tf_op jit(solution)/shard_map/ppermute | solution.py:586
  195.2 13.8 %mlp_mid.2 = (bf16[832,2048]{1,0:T(8,128)(2,1)}, bf16[832,2048]{1,0:T(8,128)(2,1)}) custom-call(bf16[832,1024]{1,0:T(8,128)(2,1)S(1)} %copy-done.4, bf16[832,1024]{1,0:T(8,128)(2,1)S(1)} %copy-done.3, bf16[1024,2048]{1,0:T(8,128)(2,1)} %copy-done.7, bf16[1024,2048]{1,0:T(8,128)(2,1)} %all-gather.6.cloned.1.call-done.down_ref), custom_call_target="tpu_custom_call" | custom-call | flops 13958643712 | bytes 18612224 | tf_op jit(solution)/shard_map/mlp_mid/pallas_call | solution.py:227
  208.9 5.7 %fusion.54 = f32[832,1024]{1,0:T(8,128)S(1)} fusion(bf16[832,2048]{1,0:T(8,128)(2,1)} %get-tuple-element.35.refs_2_, bf16[1024,2048]{1,0:T(8,128)(2,1)S(1)} %copy-done.9), kind=kOutput, calls=%fused_computation.211 | convolution fusion | flops 3489660928 | bytes 11010048 | tf_op jit(solution)/shard_map/dot_general | solution.py:34
  219.0 22.6 %scene.1 = (f32[8,2048]{1,0:T(8,128)}, bf16[192,2048]{1,0:T(8,128)(2,1)}, f32[192,1024]{1,0:T(8,128)}, f32[64,32]{1,0:T(8,128)}, f32[64,1]{1,0:T(8,128)}, /*inde...) custom-call(s32[1]{0:T(128)} %bitcast.own_ref, bf16[192,1024]{1,0:T(8,128)(2,1)} %after.19.tokens_ref, ...), custom_call_target="tpu_custom_call" | custom-call | flops 24999999488 | bytes 16777216 | tf_op jit(solution)/shard_map/scene/pallas_call | solution.py:509
  241.6 3.1 convolution_convert_fusion.1
  247.2 6.2 %mlp_mid.3 = (bf16[192,2048]{1,0:T(8,128)(2,1)S(1)}, bf16[192,2048]{1,0:T(8,128)(2,1)S(1)}) custom-call(bf16[192,1024]{1,0:T(8,128)(2,1)S(1)} %copy-done.23, bf16[192,1024]{1,0:T(8,128)(2,1)S(1)} %fusion.18.gm_ref.refs_1_, bf16[1024,2048]{1,0:T(8,128)(2,1)} %copy-done.7, bf16[1024,2048]{1,0:T(8,128)(2,1)} %all-gather.6.cloned.1.call-done.down_ref), custom_call_target="tpu_custom_call" | custom-call | flops 3221225472 | bytes 10747904 | tf_op jit(solution)/shard_map/mlp_mid/pallas_call | solution.py:227
  253.4 2.3 convolution_convert_fusion.3
  256.2 8.7 %weight_grad.3 = (bf16[512,2048]{1,0:T(8,128)(2,1)S(1)}, bf16[512,2048]{1,0:T(8,128)(2,1)}) custom-call(s32[16]{0:T(128)S(1)} %fusion.33.place_ref, bf16[832,1024]{1,0:T(8,128)(2,1)S(1)} %pad_maximum_fusion.4.refs_0_, bf16[192,1024]{1,0:T(8,128)(2,1)S(1)} %copy-done.24, bf16[832,2048]{1,0:T(8,128)(2,1)S(1)} %copy-done.32, ...), custom_call_target="tpu_custom_call" | custom-call | flops 6442450944 | bytes 16777216 | tf_op jit(solution)/shard_map/weight_grad/pallas_call | solution.py:323
  277.2 3.1 fusion.44
  280.4 3.0 multiply_reduce_fusion.2
  287.8 2.6 fusion.43
  297.5 8.0 %weight_grad.4.refs_2_ = bf16[1024,2048]{1,0:T(8,128)(2,1)S(1)} custom-call(s32[16]{0:T(128)S(1)} %iota.25.place_ref, bf16[832,1024]{1,0:T(8,128)(2,1)S(1)} %copy-done.3, bf16[192,1024]{1,0:T(8,128)(2,1)S(1)} %copy-done.26, bf16[832,2048]{1,0:T(8,128)(2,1)S(1)} %copy-done.30, bf16[192,2048]{1,0:T(8,128)(2,1)S(1)} %copy-done.29), custom_call_target="tpu_custom_call" | custom-call | flops 6442450944 | bytes 16777216 | tf_op jit(solution)/shard_map/weight_grad/pallas_call | solution.py:323
  307.6 6.7 %collective-permute-done.14 = f32[5504]{0:T(1024)S(1)} collective-permute-done((f32[5504]{0:T(1024)S(1)}, f32[5504]{0:T(1024)S(1)}, u32[]{:S(2)}, u32[]{:S(2)}) %collective-permute-start.14) | collective-permute-done | bytes 22048 | tf_op jit(solution)/shard_map/ppermute | solution.py:728
  317.1 2.2 collective-permute-done.16
  322.7 3.7 convolution_convert_fusion.2.refs_0_
  326.4 2.4 add_convert_fusion.1.refs_1_
  332.4 29.0 %attend_bwd.1.refs_0_ = bf16[1024,1536]{1,0:T(8,128)(2,1)S(1)} custom-call(bf16[1024,1536]{1,0:T(8,128)(2,1)} %copy-done.31, bf16[1024,1536]{1,0:T(8,128)(2,1)} %copy-done.31, bf16[1024,1536]{1,0:T(8,128)(2,1)} %copy-done.31, bf16[1024,512]{1,0:T(8,128)(2,1)S(1)} %copy-done.21, bf16[1024,512]{1,0:T(8,128)(2,1)S(1)} %copy-done.20, ...), custom_call_target="tpu_custom_call" | custom-call | flops 12884901888 | bytes 8388608 | tf_op jit(solution)/shard_map/attend_bwd/pallas_call | solution.py:179
  363.2 2.5 collective-permute-done.17
  365.6 2.6 add_convert_fusion.3.refs_1_
  373.4 8.2 %weight_grad.5 = (bf16[512,2048]{1,0:T(8,128)(2,1)S(1)}, bf16[512,2048]{1,0:T(8,128)(2,1)}) custom-call(s32[16]{0:T(128)S(1)} %fusion.33.place_ref, bf16[1024,1024]{1,0:T(8,128)(2,1)S(1)} %copy-done.17, bf16[1024,1536]{1,0:T(8,128)(2,1)S(1)} %copy-done.12, bf16[1024,1024]{1,0:T(8,128)(2,1)S(1)} %copy-done.18, bf16[1024,512]{1,0:T(8,128)(2,1)S(1)} %copy-done.20), custom_call_target="tpu_custom_call" | custom-call | flops 6442450944 | bytes 16777216 | tf_op jit(solution)/shard_map/weight_grad/pallas_call | solution.py:323
  387.0 6.1 %fusion.5 = (f32[1024]{0:T(1024)}, f32[1024,1024]{1,0:T(8,128)S(1)}) fusion(f32[1024]{0:T(1024)S(1)} %copy-done.78, f32[1024]{0:T(1024)S(1)} %copy-done.72, bf16[832,1024]{1,0:T(8,128)(2,1)S(1)} %bitcast.81, bf16[192,1024]{1,0:T(8,128)(2,1)S(1)} %bitcast.89, bf16[1024,1536]{1,0:T(8,128)(2,1)S(1)} %copy-done.13, bf16[1024,2048]{1,0:T(8,128)(2,1)} %after.14.refs_1_), kind=kOutput, calls=%fused_computation.7 | convolution fusion | flops 3229613056 | bytes 12595200 | tf_op jit(solution)/shard_map/dot_general | solution.py:34
  398.6 4.2 all-to-all-start.2
  402.8 2.4 add_convert_fusion
  417.4 8.3 %collective-permute-done.26 = bf16[64,1024]{1,0:T(8,128)(2,1)S(1)} collective-permute-done((bf16[64,1024]{1,0:T(8,128)(2,1)}, bf16[64,1024]{1,0:T(8,128)(2,1)S(1)}, u32[]{:S(2)}, u32[]{:S(2)}) %collective-permute-start.26) | collective-permute-done | bytes 131104 | tf_op jit(solution)/shard_map/ppermute | solution.py:586
  427.5 4.0 multiply_reduce_fusion.1
  435.2 4.8 all-to-all-start.1
  442.5 2.4 fusion.40
  444.9 11.4 %collective-permute-done.21 = f32[1024]{0:T(1024)S(1)} collective-permute-done((f32[1024]{0:T(1024)}, f32[1024]{0:T(1024)S(1)}, u32[]{:S(2)}, u32[]{:S(2)}) %collective-permute-start.21) | collective-permute-done | bytes 4128 | tf_op jit(solution)/shard_map/ppermute | solution.py:728
  456.4 4.6 collective-permute-start.22
  461.0 4.1 collective-permute-done.22
  468.7 2.2 convert_reduce_fusion.1
  (404 shorter events, 138.2 us)
Async XLA Ops:
  7.2 73.2 %all-gather.4.cloned.1.call-start = ((), (), s32[]{:S(2)}) async-start(), calls=%async_computation.5 | async-start | bytes 4456448 | tf_op jit(solution)/shard_map/all_gather | solution.py:657
  14.0 16.9 %collective-permute-start = (f32[6,1024]{1,0:T(8,128)S(1)}, f32[6,1024]{1,0:T(8,128)S(1)}, u32[]{:S(2)}, u32[]{:S(2)}) collective-permute-start(f32[6,1024]{1,0:T(8,128)S(1)} %pad_maximum_fusion.8), channel_id=1, source_target_pairs={{0,1},{1,0},{2,3},{3,2},{4,5},{5,4},{6,7},{7,6},{8,9},{9,8},{10,11... | collective-permute-start | bytes 73736 | tf_op jit(solution)/shard_map/ppermute | solution.py:586
  18.1 62.4 %all-to-all-start = ((bf16[4,64,2048]{2,1,0:T(8,128)(2,1)}), bf16[4,64,2048]{2,1,0:T(8,128)(2,1)S(1)}, u32[]{:S(2)}, u32[]{:S(2)}) async-start(bf16[4,64,2048]{2,1,0:T(8,128)(2,1)} %bitcast.12), calls=%async_computation | async-start | bytes 2097152 | tf_op jit(solution)/shard_map/all_to_all | solution.py:653
  22.9 141.0 %all-gather.6.cloned.1.call-start = ((), (), s32[]{:S(2)}) async-start(), calls=%async_computation.6 | async-start | bytes 4456448 | tf_op jit(solution)/shard_map/all_gather | solution.py:657
  24.8 58.4 %copy-start.33 = (bf16[2,416,1024]{2,1,0:T(8,128)(2,1)}, bf16[2,416,1024]{2,1,0:T(8,128)(2,1)S(1)}, u32[]{:S(2)}) copy-start(bf16[2,416,1024]{2,1,0:T(8,128)(2,1)S(1)} %slice.150) | copy-start | bytes 5111812
  26.5 102.6 %copy-start.50 = (bf16[2,96,1024]{2,1,0:T(8,128)(2,1)}, bf16[2,96,1024]{2,1,0:T(8,128)(2,1)S(1)}, u32[]{:S(2)}) copy-start(bf16[2,96,1024]{2,1,0:T(8,128)(2,1)S(1)} %slice.149) | copy-start | bytes 1179652
  81.5 137.5 %all-gather.8.cloned.1.call-start = ((), (), s32[]{:S(2)}) async-start(), calls=%async_computation.7 | async-start | bytes 4456448 | tf_op jit(solution)/shard_map/all_gather | solution.py:657
  90.3 15.5 %copy-start.31 = (bf16[1024,1536]{1,0:T(8,128)(2,1)}, bf16[1024,1536]{1,0:T(8,128)(2,1)S(1)}, u32[]{:S(2)}) copy-start(bf16[1024,1536]{1,0:T(8,128)(2,1)S(1)} %convolution_convert_fusion.q_ref.k_ref.v_ref) | copy-start | bytes 9437188
  108.5 20.7 %collective-permute-start.1 = (f32[192,1024]{1,0:T(8,128)}, f32[192,1024]{1,0:T(8,128)}, u32[]{:S(2)}, u32[]{:S(2)}) collective-permute-start(f32[192,1024]{1,0:T(8,128)} %fusion.15.refs_1_), channel_id=1, source_target_pairs={{0,1},{1,0},{2,3},{3,2},{4,5},{5,4},{6,7},{7,6},{8,9},{9,8},{10,11... | collective-permute-start | bytes 2359304 | tf_op jit(solution)/shard_map/ppermute | solution.py:586
  115.4 31.3 %collective-permute-start.6 = (bf16[416,1024]{1,0:T(8,128)(2,1)}, bf16[416,1024]{1,0:T(8,128)(2,1)}, u32[]{:S(2)}, u32[]{:S(2)}) collective-permute-start(bf16[416,1024]{1,0:T(8,128)(2,1)} %dynamic-slice_convert_fusion.2.refs_1_), channel_id=1, source_target_pairs={{0,1},{1,0},{2,3},{3,2},{4,5},{5,4},{6,7},{7,6},{8,9},{9,8},{10,11... | collective-permute-start | bytes 2555912 | tf_op jit(solution)/shard_map/ppermute | solution.py:586
  116.0 34.4 %collective-permute-start.2 = (bf16[256,2048]{1,0:T(8,128)(2,1)S(1)}, bf16[256,2048]{1,0:T(8,128)(2,1)S(1)}, u32[]{:S(2)}, u32[]{:S(2)}) collective-permute-start(bf16[256,2048]{1,0:T(8,128)(2,1)S(1)} %bitcast.72), channel_id=1, source_target_pairs={{0,4},{2,6},{4,0},{6,2},{8,12},{10,14},{12,8},{14,10},{16,20},{18,... | collective-permute-start | bytes 3145736 | tf_op jit(solution)/shard_map/ppermute | solution.py:647
  129.1 17.6 %copy-start.34 = (bf16[2,416,1024]{2,1,0:T(8,128)(2,1)S(1)}, bf16[2,416,1024]{2,1,0:T(8,128)(2,1)}, u32[]{:S(2)}) copy-start(bf16[2,416,1024]{2,1,0:T(8,128)(2,1)} %copy-done.33) | copy-start | bytes 5111812
  131.6 17.5 %copy-start.67 = (f32[1024]{0:T(1024)S(1)}, f32[1024]{0:T(1024)}, u32[]{:S(2)}) copy-start(f32[1024]{0:T(1024)} %param.23) | copy-start | bytes 12292
  151.4 264.0 %reduce-scatter.5.cloned.1.call-start = ((), (), s32[]{:S(2)}) async-start(), calls=%async_computation.9 | async-start | bytes 2228224 | tf_op jit(solution)/shard_map/reduce_scatter | solution.py:661
  151.7 4.1 collective-permute-start.3
  151.7 4.5 collective-permute-start.4
  161.6 22.1 %collective-permute-start.7 = (bf16[416,1024]{1,0:T(8,128)(2,1)}, bf16[416,1024]{1,0:T(8,128)(2,1)S(1)}, u32[]{:S(2)}, u32[]{:S(2)}) collective-permute-start(bf16[416,1024]{1,0:T(8,128)(2,1)} %multiply_convert_fusion.refs_2_), channel_id=1, source_target_pairs={{0,1},{1,0},{2,3},{3,2},{4,5},{5,4},{6,7},{7,6},{8,9},{9,8},{10,11... | collective-permute-start | bytes 2555912 | tf_op jit(solution)/shard_map/ppermute | solution.py:586
  168.5 15.2 %copy-start.37 = (f32[416,1024]{1,0:T(8,128)S(1)}, f32[416,1024]{1,0:T(8,128)}, u32[]{:S(2)}) copy-start(f32[416,1024]{1,0:T(8,128)} %copy-done.36) | copy-start | bytes 5111812
  173.6 17.7 %collective-permute-start.5 = (bf16[192,1024]{1,0:T(8,128)(2,1)S(1)}, bf16[192,1024]{1,0:T(8,128)(2,1)S(1)}, u32[]{:S(2)}, u32[]{:S(2)}) collective-permute-start(bf16[192,1024]{1,0:T(8,128)(2,1)S(1)} %convert_element_type.366), channel_id=1, source_target_pairs={{0,1},{1,0},{2,3},{3,2},{4,5},{5,4},{6,7},{7,6},{8,9},{9,8},{10,11... | collective-permute-start | bytes 1179656 | tf_op jit(solution)/shard_map/ppermute | solution.py:586
  195.2 13.8 %copy-start.9 = (bf16[1024,2048]{1,0:T(8,128)(2,1)S(1)}, bf16[1024,2048]{1,0:T(8,128)(2,1)}, u32[]{:S(2)}) copy-start(bf16[1024,2048]{1,0:T(8,128)(2,1)} %copy-done.7) | copy-start | bytes 12582916
  217.5 57.3 %collective-permute-start.9 = (bf16[416,1024]{1,0:T(8,128)(2,1)}, bf16[416,1024]{1,0:T(8,128)(2,1)}, u32[]{:S(2)}, u32[]{:S(2)}) collective-permute-start(bf16[416,1024]{1,0:T(8,128)(2,1)} %dynamic-slice_convert_fusion.1.refs_1_), channel_id=1, source_target_pairs={{0,1},{1,0},{2,3},{3,2},{4,5},{5,4},{6,7},{7,6},{8,9},{9,8},{10,11... | collective-permute-start | bytes 2555912 | tf_op jit(solution)/shard_map/ppermute | solution.py:586
  219.0 22.6 %copy-start.59 = (bf16[192,1024]{1,0:T(8,128)(2,1)S(1)}, bf16[192,1024]{1,0:T(8,128)(2,1)}, u32[]{:S(2)}) copy-start(bf16[192,1024]{1,0:T(8,128)(2,1)} %after.19.tokens_ref) | copy-start | bytes 1179652
  244.7 226.8 %reduce-scatter.3.cloned.1.call-start = ((), (), s32[]{:S(2)}) async-start(), calls=%async_computation.8 | async-start | bytes 4456448 | tf_op jit(solution)/shard_map/reduce_scatter | solution.py:661
  255.7 19.1 %collective-permute-start.8 = (bf16[192,1024]{1,0:T(8,128)(2,1)}, bf16[192,1024]{1,0:T(8,128)(2,1)}, u32[]{:S(2)}, u32[]{:S(2)}) collective-permute-start(bf16[192,1024]{1,0:T(8,128)(2,1)} %convolution_convert_fusion.3), channel_id=1, source_target_pairs={{0,1},{1,0},{2,3},{3,2},{4,5},{5,4},{6,7},{7,6},{8,9},{9,8},{10,11... | collective-permute-start | bytes 1179656 | tf_op jit(solution)/shard_map/ppermute | solution.py:586
  266.3 60.1 %collective-permute-start.11 = (bf16[512,2048]{1,0:T(8,128)(2,1)}, bf16[512,2048]{1,0:T(8,128)(2,1)}, u32[]{:S(2)}, u32[]{:S(2)}) collective-permute-start(bf16[512,2048]{1,0:T(8,128)(2,1)} %get-tuple-element.40), channel_id=1, source_target_pairs={{0,2},{2,0},{4,6},{6,4},{8,10},{10,8},{12,14},{14,12},{16,18},{18,... | collective-permute-start | bytes 6291464 | tf_op jit(solution)/shard_map/ppermute | solution.py:647
  285.5 4.9 %collective-permute-start.12 = (f32[5504]{0:T(1024)}, f32[5504]{0:T(1024)S(1)}, u32[]{:S(2)}, u32[]{:S(2)}) collective-permute-start(f32[5504]{0:T(1024)} %concatenate.49), channel_id=1, source_target_pairs={{0,8},{2,10},{4,12},{6,14},{8,0},{10,2},{12,4},{14,6},{16,24},{18,... | collective-permute-start | bytes 66056 | tf_op jit(solution)/shard_map/ppermute | solution.py:728
  290.5 5.5 %collective-permute-start.13 = (f32[5504]{0:T(1024)S(1)}, f32[5504]{0:T(1024)S(1)}, u32[]{:S(2)}, u32[]{:S(2)}) collective-permute-start(f32[5504]{0:T(1024)S(1)} %add.1026), channel_id=1, source_target_pairs={{0,16},{2,18},{4,20},{6,22},{8,24},{10,26},{12,28},{14,30},{16,0},... | collective-permute-start | bytes 66056 | tf_op jit(solution)/shard_map/ppermute | solution.py:728
  293.1 26.9 %collective-permute-start.10 = (bf16[416,1024]{1,0:T(8,128)(2,1)S(1)}, bf16[416,1024]{1,0:T(8,128)(2,1)}, u32[]{:S(2)}, u32[]{:S(2)}) collective-permute-start(bf16[416,1024]{1,0:T(8,128)(2,1)S(1)} %get-tuple-element.92), channel_id=1, source_target_pairs={{0,1},{1,0},{2,3},{3,2},{4,5},{5,4},{6,7},{7,6},{8,9},{9,8},{10,11... | collective-permute-start | bytes 2555912 | tf_op jit(solution)/shard_map/ppermute | solution.py:586
  296.0 18.3 %collective-permute-start.14 = (f32[5504]{0:T(1024)S(1)}, f32[5504]{0:T(1024)S(1)}, u32[]{:S(2)}, u32[]{:S(2)}) collective-permute-start(f32[5504]{0:T(1024)S(1)} %add.1027), channel_id=1, source_target_pairs={{0,1},{1,0},{2,3},{3,2},{4,5},{5,4},{6,7},{7,6},{8,9},{9,8},{10,11... | collective-permute-start | bytes 66056 | tf_op jit(solution)/shard_map/ppermute | solution.py:728
  314.3 1.2 collective-permute-start.15
  315.5 3.8 collective-permute-start.16
  330.0 35.7 %collective-permute-start.17 = (bf16[256,2048]{1,0:T(8,128)(2,1)}, bf16[256,2048]{1,0:T(8,128)(2,1)}, u32[]{:S(2)}, u32[]{:S(2)}) collective-permute-start(bf16[256,2048]{1,0:T(8,128)(2,1)} %slice.161), channel_id=1, source_target_pairs={{0,4},{2,6},{4,0},{6,2},{8,12},{10,14},{12,8},{14,10},{16,20},{18,... | collective-permute-start | bytes 3145736 | tf_op jit(solution)/shard_map/ppermute | solution.py:647
  332.4 33.2 %copy-start.49 = (bf16[512,2048]{1,0:T(8,128)(2,1)S(1)}, bf16[512,2048]{1,0:T(8,128)(2,1)}, u32[]{:S(2)}) copy-start(bf16[512,2048]{1,0:T(8,128)(2,1)} %copy-done.48) | copy-start | bytes 6291460
  381.6 21.2 %collective-permute-start.19 = (bf16[512,2048]{1,0:T(8,128)(2,1)}, bf16[512,2048]{1,0:T(8,128)(2,1)}, u32[]{:S(2)}, u32[]{:S(2)}) collective-permute-start(bf16[512,2048]{1,0:T(8,128)(2,1)} %get-tuple-element.51), channel_id=1, source_target_pairs={{0,2},{2,0},{4,6},{6,4},{8,10},{10,8},{12,14},{14,12},{16,18},{18,... | collective-permute-start | bytes 6291464 | tf_op jit(solution)/shard_map/ppermute | solution.py:647
  397.1 30.3 %collective-permute-start.18 = (bf16[512,1024]{1,0:T(8,128)(2,1)}, bf16[512,1024]{1,0:T(8,128)(2,1)}, u32[]{:S(2)}, u32[]{:S(2)}) collective-permute-start(bf16[512,1024]{1,0:T(8,128)(2,1)} %dynamic-slice_convert_fusion), channel_id=1, source_target_pairs={{0,1},{1,0},{2,3},{3,2},{4,5},{5,4},{6,7},{7,6},{8,9},{9,8},{10,11... | collective-permute-start | bytes 3145736 | tf_op jit(solution)/shard_map/ppermute | solution.py:586
  398.6 36.6 %all-to-all-start.2 = ((bf16[4,64,2048]{2,1,0:T(8,128)(2,1)}), bf16[4,64,2048]{2,1,0:T(8,128)(2,1)}, u32[]{:S(2)}, u32[]{:S(2)}) async-start(bf16[4,64,2048]{2,1,0:T(8,128)(2,1)} %bitcast.29), calls=%async_computation.2 | async-start | bytes 2097152 | tf_op jit(solution)/shard_map/all_to_all | solution.py:653
  406.6 20.8 %copy-start.45 = (f32[416,1024]{1,0:T(8,128)S(1)}, f32[416,1024]{1,0:T(8,128)}, u32[]{:S(2)}) copy-start(f32[416,1024]{1,0:T(8,128)} %copy-done.44) | copy-start | bytes 5111812
  406.6 20.8 %copy-start.70 = (f32[1024]{0:T(1024)S(1)}, f32[1024]{0:T(1024)}, u32[]{:S(2)}) copy-start(f32[1024]{0:T(1024)} %param.20) | copy-start | bytes 12292
  406.7 25.4 %collective-permute-start.20 = (bf16[256,2048]{1,0:T(8,128)(2,1)S(1)}, bf16[256,2048]{1,0:T(8,128)(2,1)}, u32[]{:S(2)}, u32[]{:S(2)}) collective-permute-start(bf16[256,2048]{1,0:T(8,128)(2,1)S(1)} %slice.165), channel_id=1, source_target_pairs={{0,4},{2,6},{4,0},{6,2},{8,12},{10,14},{12,8},{14,10},{16,20},{18,... | collective-permute-start | bytes 3145736 | tf_op jit(solution)/shard_map/ppermute | solution.py:647
  415.5 10.2 %collective-permute-start.26 = (bf16[64,1024]{1,0:T(8,128)(2,1)}, bf16[64,1024]{1,0:T(8,128)(2,1)S(1)}, u32[]{:S(2)}, u32[]{:S(2)}) collective-permute-start(bf16[64,1024]{1,0:T(8,128)(2,1)} %reduce-scatter.5.cloned.1.call-done), channel_id=1, source_target_pairs={{0,1},{1,0},{2,3},{3,2},{4,5},{5,4},{6,7},{7,6},{8,9},{9,8},{10,11... | collective-permute-start | bytes 393224 | tf_op jit(solution)/shard_map/ppermute | solution.py:586
  435.2 40.0 %all-to-all-start.1 = ((bf16[4,64,2048]{2,1,0:T(8,128)(2,1)}), bf16[4,64,2048]{2,1,0:T(8,128)(2,1)S(1)}, u32[]{:S(2)}, u32[]{:S(2)}) async-start(bf16[4,64,2048]{2,1,0:T(8,128)(2,1)} %bitcast.93), calls=%async_computation.1 | async-start | bytes 2097152 | tf_op jit(solution)/shard_map/all_to_all | solution.py:653
  440.5 15.8 %collective-permute-start.21 = (f32[1024]{0:T(1024)}, f32[1024]{0:T(1024)S(1)}, u32[]{:S(2)}, u32[]{:S(2)}) collective-permute-start(f32[1024]{0:T(1024)} %after.24), channel_id=1, source_target_pairs={{0,8},{2,10},{4,12},{6,14},{8,0},{10,2},{12,4},{14,6},{16,24},{18,... | collective-permute-start | bytes 12296 | tf_op jit(solution)/shard_map/ppermute | solution.py:728
  442.5 13.8 %copy-start.76 = (f32[1024]{0:T(1024)S(1)}, f32[1024]{0:T(1024)}, u32[]{:S(2)}) copy-start(f32[1024]{0:T(1024)} %after.24) | copy-start | bytes 12292
  442.5 23.1 %copy-start.58 = (f32[416,1024]{1,0:T(8,128)S(1)}, f32[416,1024]{1,0:T(8,128)}, u32[]{:S(2)}) copy-start(f32[416,1024]{1,0:T(8,128)} %get-tuple-element.93) | copy-start | bytes 5111812
  456.4 8.7 %collective-permute-start.22 = (f32[1024]{0:T(1024)S(1)}, f32[1024]{0:T(1024)S(1)}, u32[]{:S(2)}, u32[]{:S(2)}) collective-permute-start(f32[1024]{0:T(1024)S(1)} %add.1040), channel_id=1, source_target_pairs={{0,16},{2,18},{4,20},{6,22},{8,24},{10,26},{12,28},{14,30},{16,0},... | collective-permute-start | bytes 12296 | tf_op jit(solution)/shard_map/ppermute | solution.py:728
  465.1 3.6 collective-permute-start.23
  468.7 2.2 collective-permute-start.24
  470.9 3.6 collective-permute-start.25
  (82 other events, 315.1 us)
Sparse Core Ops, SparseCore 0:
  13.3 67.1 all-gather.3
  83.2 51.2 all-gather.5
  151.6 49.0 all-gather.7
  244.8 59.2 reduce-scatter.4
  308.2 83.0 reduce-scatter.2

commit v2 on v1

--- a/solution.py
+++ b/solution.py
@@ -230,7 +230,7 @@
         in_specs=[whole, whole, weight, weight],
         out_specs=[result, result],
         out_shape=[jax.ShapeDtypeStruct((rows, width), BF16)] * 2,
-        compiler_params=pltpu.CompilerParams(vmem_limit_bytes=48 * 1024 * 1024),
+        compiler_params=pltpu.CompilerParams(vmem_limit_bytes=60 * 1024 * 1024),
         cost_estimate=cost(
             8 * rows * depth * width, 4 * (rows + width) * depth + 4 * rows * width, rows * width
         ),
@@ -263,7 +263,7 @@
         in_specs=[whole, weight, weight],
         out_specs=whole,
         out_shape=jax.ShapeDtypeStruct((rows, depth), F32),
-        compiler_params=pltpu.CompilerParams(vmem_limit_bytes=32 * 1024 * 1024),
+        compiler_params=pltpu.CompilerParams(vmem_limit_bytes=60 * 1024 * 1024),
         cost_estimate=cost(4e9, 4 * width * depth, rows * width),
         name="mlp_tri",
     )(normed, up_full, down_full)
@@ -298,7 +298,7 @@
                 out[...] = total[i * rows : (i + 1) * rows].astype(BF16)
 
 
-def weight_grad(place, pieces, *segments):
+def weight_grad(place, pieces, *segments, room=40):
     specs, args, marks = [], [], []
     first = 0
     cols = min(512, *(rights[0].shape[1] for _, rights in segments))
@@ -330,7 +330,7 @@
             scratch_shapes=[pltpu.VMEM((depth, left.shape[0]), BF16) for left in parts],
         ),
         out_shape=[result] * pieces,
-        compiler_params=pltpu.CompilerParams(vmem_limit_bytes=40 * 1024 * 1024),
+        compiler_params=pltpu.CompilerParams(vmem_limit_bytes=room * 1024 * 1024),
         cost_estimate=cost(
             3 * depth * first * cols * sum(left.shape[0] for left in parts), 8 * depth * first * cols
         ),
@@ -527,7 +527,7 @@
             ],
         ),
         out_shape=[jax.ShapeDtypeStruct(shape, kind) for shape, kind, _ in outs],
-        compiler_params=pltpu.CompilerParams(vmem_limit_bytes=56 * 1024 * 1024),
+        compiler_params=pltpu.CompilerParams(vmem_limit_bytes=60 * 1024 * 1024),
         cost_estimate=cost(25e9, 8 * w_unpatch.size, 1e6),
         name="scene",
     )(
@@ -717,12 +717,12 @@
     return jnp.sum(parts.astype(F32), axis=0)
 
 
-def sum_by_hops(vec):
-    for axis, steps in (("seq", (4, 8)), ("tp", (1,)), ("seq", (1, 2))):
+def hop_sums(vec, plan):
+    for axis, steps in plan:
         size = lax.axis_size(axis)
-        if axis == "tp" and size > 2:
+        if axis == "tp":
             steps = tuple(2**i for i in range(size.bit_length() - 1))
-        if steps == (4, 8) and size > 16:
+        if steps == (4, 8):
             steps = tuple(2**i for i in range(2, size.bit_length() - 1))
         for step in steps:
             vec = vec + lax.ppermute(vec, axis, [(i, i ^ step) for i in range(size)])
@@ -833,10 +833,10 @@
     unpatch_full = gather_plain(after(w_unpatch, hidden_tri, normed_own, wide_u))
 
     normed_tri = layer_norm(hidden_tri, mlp_gain).astype(BF16)
-    tokens = (hidden_tri + tp_sum(mlp_tri(normed_tri, up_full, down_t).astype(BF16))).astype(BF16)
+    tokens = (hidden_tri + tp_sum(mlp_tri(normed_tri, up_full, down_t))).astype(BF16)
     normed_rest = tp_rows(normed_own)
 
-    act_rest, gup_rest = mlp_mid(after(normed_rest, tokens), gm_rest, up_full, down_t)
+    act_rest, gup_rest = mlp_mid(normed_rest, gm_rest, up_full, down_t)
     gnb_mine, gnb_theirs = tp_parts(dot(gup_rest, up_full, NT))
     tokens = after(tokens, gnb_theirs)
 
@@ -882,7 +882,47 @@
     gh_rest = gh_rest + og_own
     branch = jnp.concatenate([gh_tri.astype(BF16), tp_rows(gh_rest.astype(BF16))], 0)
 
+    chip_up = scatter_chip(*grad_up)
+    grad_heads = dot(branch, out_t).astype(BF16)
+    grad_heads = after(grad_heads, chip_up, grad_down)
+    pair_up = scatter_pair(chip_up)
+    grad_proj = attend_bwd(projected, grad_heads, attended, lse, local_width)
+    grad_proj = after(grad_proj, pair_up)
+    sum_up = scatter_line(pair_up)
+    chip_last = scatter_chip(
+        *weight_grad(places, 2, ((normed_a,), (grad_proj,)), ((branch,), (attended,)), room=60)
+    )
+    pair_last = scatter_pair(chip_last)
+    gna = dot(after(grad_proj, chip_last), qkv_full, NT)
+    gna_mine, gna_theirs = tp_parts(block_rows(gna))
+    gna_sum = tp_sum_own(gna_mine, gna_theirs)
+    sum_last = scatter_line(pair_last)
+    _, back_gain_a = jax.vjp(lambda g: layer_norm(rows_in.astype(F32), g), attn_gain)
+    grad_attn_gain = back_gain_a(gna)[0]
+    tri_own = own_of(x_tri, own_tri).astype(F32)
+    _, back_a = jax.vjp(
+        lambda v: layer_norm(v, attn_gain), jnp.concatenate([rest_own, tri_own], 0)
+    )
+    grad_input = back_a(gna_sum)[0] + jnp.concatenate(
+        [gh_rest, own_of(gh_tri, own_tri)], 0
+    )
+    if tp_count == 2:
+        other = swap(sum_unpatch)
+        low = tp_index == 0
+        sum_unpatch = jnp.concatenate(
+            [jnp.where(low, sum_unpatch, other), jnp.where(low, other, sum_unpatch)], 1
+        )
+    sum_unpatch = sum_unpatch.astype(F32)
+
+    weight_sums = (
+        sum_last[:, : 3 * local_width].reshape(w_qkv.shape),
+        sum_last[:, 3 * local_width :].T,
+        sum_up,
+        sum_down.T,
+        sum_unpatch,
+    )
     smalls = (
+        grad_attn_gain,
         grad_mlp_gain,
         g_dens_in,
         g_dens_bias,
@@ -891,47 +931,10 @@
         g_color_bias,
         g_color_out[: color_out.shape[0]],
     )
-    flat = sum_by_hops(jnp.concatenate([s.reshape(-1) for s in smalls]))
-
-    chip_up = scatter_chip(*grad_up)
-    grad_heads = dot(branch, out_t).astype(BF16)
-    grad_heads = after(grad_heads, chip_up, grad_down, flat)
-    pair_up = scatter_pair(chip_up)
-    grad_proj = attend_bwd(projected, grad_heads, attended, lse, local_width)
-    grad_proj = after(grad_proj, pair_up)
-    sum_up = scatter_line(pair_up)
-    gna = dot(grad_proj, qkv_full, NT)
-    gna_sum = tp_sum_own(*tp_parts(block_rows(gna)))
-    chip_last = scatter_chip(
-        *weight_grad(places, 2, ((normed_a,), (grad_proj,)), ((branch,), (attended,)))
-    )
-    pair_last = scatter_pair(chip_last)
-    sum_last = scatter_line(after(pair_last, gna_sum))
-    _, back_gain_a = jax.vjp(lambda g: layer_norm(rows_in.astype(F32), g), attn_gain)
-    grad_attn_gain = back_gain_a(gna)[0]
-    tri_own = own_of(x_tri, own_tri).astype(F32)
-    _, back_a = jax.vjp(
-        lambda v: layer_norm(v, attn_gain), jnp.concatenate([rest_own, tri_own], 0)
-    )
-    grad_input = back_a(gna_sum)[0] + jnp.concatenate(
-        [gh_rest, own_of(gh_tri, own_tri)], 0
-    )
-    if tp_count == 2:
-        other = swap(sum_unpatch)
-        low = tp_index == 0
-        sum_unpatch = jnp.concatenate(
-            [jnp.where(low, sum_unpatch, other), jnp.where(low, other, sum_unpatch)], 1
-        )
-    sum_unpatch = sum_unpatch.astype(F32)
-
-    weight_sums = (
-        sum_last[:, : 3 * local_width].reshape(w_qkv.shape),
-        sum_last[:, 3 * local_width :].T,
-        sum_up,
-        sum_down.T,
-        sum_unpatch,
-    )
-    small_sums = [sum_by_hops(after(grad_attn_gain, pair_last))]
+    flat = jnp.concatenate([s.reshape(-1) for s in smalls])
+    flat = after(hop_sums(after(flat, gna_theirs), (("seq", (4, 8)), ("seq", (1,)))), pair_last)
+    flat = hop_sums(flat, (("tp", (1,)), ("seq", (2,))))
+    small_sums = []
     at = 0
     for s in smalls:
         small_sums.append(flat[at : at + s.size].reshape(s.shape))

time: 489 us -> 442 us (0.904)
  waiting for transfers between devices: 130 us -> 100 us
  local copies, waits for them, and re-layouts: 77 us -> 51.8 us
  Pallas kernels: 120 us -> 128 us
    ppermute x10 -> x5, waiting for transfers between devices: 29.7 us -> 3.3 us  [hop_sums(): vec = vec + lax.ppermute(vec, axis, [(i, i ^ step) for i in range(size)])]
    unnamed x207 -> x181, local copies, waits for them, and re-layouts: 46.9 us -> 27.2 us
    ppermute x10 -> x5, starting transfers between devices: 12.5 us -> 11.5 us  [hop_sums(): vec = vec + lax.ppermute(vec, axis, [(i, i ^ step) for i in range(size)])]
  transfers between devices with their start and end apart: 35 -> 30, of which waited for: 17 -> 9; matrix products, arithmetic and copies ran while one was open for 27% -> 28% of each run, Pallas kernels for 25% -> 29%
where the time goes in v2:
time: 442 us; the launch traced here: 437 us
  Pallas kernels  128 us (29%)
  waiting for transfers between devices  100 us (23%)
  other arithmetic  66 us (15%)
  local copies, waits for them, and re-layouts  51.8 us (12%)
  starting transfers between devices  43.1 us (10%)
  matrix products  32.6 us (7%)
  between operations  15.9 us (4%)
    ppermute x10, waiting for transfers between devices, swap(): return lax.ppermute(x, axis, [(0, 1), (1, 0)])  46.3 us
    all_gather x3, waiting for transfers between devices, gather_plain(): return lax.all_gather(shard, 'seq', axis=0, tiled=True)  45.7 us
    dot_general x8, matrix products, dot(): lax.dot_general(a, b, dims, precision=precision, preferred_element_type=F32)  32.6 us
    pallas_call x1, Pallas kernels, attend_bwd(): pl.pallas_call(functools.partial(attend_bwd_kernel, scale=HEAD_DIM ** (-0...  28.8 us
    pallas_call x3, Pallas kernels, weight_grad(): pl.pallas_call(functools.partial(weight_grad_kernel, segments=tuple(marks...  28.3 us
    unnamed x181, local copies, waits for them, and re-layouts  27.2 us
    pallas_call x1, Pallas kernels, scene_pass(): pl.pallas_call(functools.partial(scene_kernel, per_slab=slab_edges // blo...  22.6 us
    pallas_call x2, Pallas kernels, mlp_mid(): pl.pallas_call(functools.partial(mlp_mid_kernel, block=block), grid=(widt...  21.5 us
  transfers between devices with their start and end apart: 30, of which 9 were waited for; matrix products, arithmetic and copies ran while one was open for 28% of the time, Pallas kernels for 29%

profile of v2, /device:TPU:0, one launch (start us, length us, event | category | flops | bytes accessed | tf_op | source)
XLA Modules:
  0.0 437.4 jit_solution(13155642569421284359)
XLA Ops:
  14.0 3.0 collective-permute-start
  18.1 4.9 %all-to-all-start = ((bf16[4,64,2048]{2,1,0:T(8,128)(2,1)}), bf16[4,64,2048]{2,1,0:T(8,128)(2,1)S(1)}, u32[]{:S(2)}, u32[]{:S(2)}) async-start(bf16[4,64,2048]{2,1,0:T(8,128)(2,1)} %bitcast.12), calls=%async_computation | async-start | bytes 2097152 | tf_op jit(solution)/shard_map/all_to_all | solution.py:653
  34.8 45.7 %all-gather.4.cloned.1.call-done.refs_0_ = bf16[1024,2048]{1,0:T(8,128)(2,1)} async-done(((bf16[64,2048]{1,0:T(8,128)(2,1)}), bf16[1024,2048]{1,0:T(8,128)(2,1)}) %all-gather.4.cloned.1.call-update) | async-done | bytes 4194320 | tf_op jit(solution)/shard_map/all_gather | solution.py:657
  85.1 3.6 convolution_convert_fusion.q_ref.k_ref.v_ref
  88.8 15.5 %attend_fwd.1 = (bf16[1024,512]{1,0:T(8,128)(2,1)S(1)}, f32[4,8,1024]{2,1,0:T(8,128)S(1)}) custom-call(bf16[1024,1536]{1,0:T(8,128)(2,1)S(1)} %convolution_convert_fusion.q_ref.k_ref.v_ref, bf16[1024,1536]{1,0:T(8,128)(2,1)S(1)} %convolution_convert_fusion.q_ref.k_ref.v_ref, bf16[1024,1536]{1,0:T(8,128)(2,1)S(1)} %convolution_convert_fusion.q_ref.k_ref.v_ref), custom_call_target="tpu_custom_call" | custom-call | flops 6442450944 | bytes 4194304 | tf_op jit(solution)/shard_map/attend_fwd/pallas_call | solution.py:101
  108.2 2.7 fusion.11
  114.8 12.6 %collective-permute-done.1.refs_0_ = f32[192,1024]{1,0:T(8,128)} collective-permute-done((f32[192,1024]{1,0:T(8,128)}, f32[192,1024]{1,0:T(8,128)}, u32[]{:S(2)}, u32[]{:S(2)}) %collective-permute-start.1) | collective-permute-done | bytes 786464 | tf_op jit(solution)/shard_map/ppermute | solution.py:586
  127.4 2.6 fusion.46
  130.1 14.9 %collective-permute-done.6 = bf16[416,1024]{1,0:T(8,128)(2,1)} collective-permute-done((bf16[416,1024]{1,0:T(8,128)(2,1)}, bf16[416,1024]{1,0:T(8,128)(2,1)}, u32[]{:S(2)}, u32[]{:S(2)}) %collective-permute-start.6) | collective-permute-done | bytes 852000 | tf_op jit(solution)/shard_map/ppermute | solution.py:586
  145.0 2.1 fusion.45
  152.0 2.1 slice.163
  155.5 3.6 assemble.1.up_ref
  160.2 11.4 %collective-permute-done.7 = bf16[416,1024]{1,0:T(8,128)(2,1)} collective-permute-done((bf16[416,1024]{1,0:T(8,128)(2,1)}, bf16[416,1024]{1,0:T(8,128)(2,1)}, u32[]{:S(2)}, u32[]{:S(2)}) %collective-permute-start.7) | collective-permute-done | bytes 852000 | tf_op jit(solution)/shard_map/ppermute | solution.py:586
  174.7 7.7 %mlp_tri.1 = f32[192,1024]{1,0:T(8,128)} custom-call(bf16[192,1024]{1,0:T(8,128)(2,1)} %multiply_convert_fusion.1.nb_ref.refs_1_, bf16[1024,2048]{1,0:T(8,128)(2,1)} %copy-done.7, bf16[1024,2048]{1,0:T(8,128)(2,1)} %all-gather.6.cloned.1.call-done.down_ref), custom_call_target="tpu_custom_call" | custom-call | flops 4000000000 | bytes 8388608 | tf_op jit(solution)/shard_map/mlp_tri/pallas_call | solution.py:260
  184.0 14.6 %mlp_mid.2 = (bf16[832,2048]{1,0:T(8,128)(2,1)}, bf16[832,2048]{1,0:T(8,128)(2,1)}) custom-call(bf16[832,1024]{1,0:T(8,128)(2,1)} %pad_maximum_fusion.4.nb_ref.refs_0_, bf16[832,1024]{1,0:T(8,128)(2,1)} %bitcast_convert_fusion.refs_4_.gm_ref.refs_0_, bf16[1024,2048]{1,0:T(8,128)(2,1)} %copy-done.7, bf16[1024,2048]{1,0:T(8,128)(2,1)} %all-gather.6.cloned.1.call-done.down_ref), custom_call_target="tpu_custom_call" | custom-call | flops 13958643712 | bytes 18612224 | tf_op jit(solution)/shard_map/mlp_mid/pallas_call | solution.py:227
  198.6 6.5 %fusion.55 = f32[832,1024]{1,0:T(8,128)S(1)} fusion(bf16[832,2048]{1,0:T(8,128)(2,1)} %get-tuple-element.35.refs_2_, bf16[1024,2048]{1,0:T(8,128)(2,1)} %copy-done.7), kind=kOutput, calls=%fused_computation.212 | convolution fusion | flops 3489660928 | bytes 11010048 | tf_op jit(solution)/shard_map/dot_general | solution.py:34
  208.7 2.1 add_convert_fusion.4.refs_0_
  210.7 22.6 %scene.1 = (f32[8,2048]{1,0:T(8,128)}, bf16[192,2048]{1,0:T(8,128)(2,1)}, f32[192,1024]{1,0:T(8,128)}, f32[64,32]{1,0:T(8,128)}, f32[64,1]{1,0:T(8,128)}, /*inde...) custom-call(s32[1]{0:T(128)} %bitcast.own_ref, bf16[192,1024]{1,0:T(8,128)(2,1)} %after.18.tokens_ref, ...), custom_call_target="tpu_custom_call" | custom-call | flops 24999999488 | bytes 16777216 | tf_op jit(solution)/shard_map/scene/pallas_call | solution.py:509
  233.3 3.1 convolution_convert_fusion.1
  236.5 2.5 multiply_reduce_fusion.2
  239.2 2.1 fusion.43
  241.5 1.9 fusion.42
  245.6 6.9 %mlp_mid.3 = (bf16[192,2048]{1,0:T(8,128)(2,1)}, bf16[192,2048]{1,0:T(8,128)(2,1)}) custom-call(bf16[192,1024]{1,0:T(8,128)(2,1)} %multiply_convert_fusion.1.nb_ref.refs_1_, bf16[192,1024]{1,0:T(8,128)(2,1)} %fusion.18.gm_ref.refs_1_, bf16[1024,2048]{1,0:T(8,128)(2,1)} %copy-done.7, bf16[1024,2048]{1,0:T(8,128)(2,1)} %all-gather.6.cloned.1.call-done.down_ref), custom_call_target="tpu_custom_call" | custom-call | flops 3221225472 | bytes 10747904 | tf_op jit(solution)/shard_map/mlp_mid/pallas_call | solution.py:227
  252.5 4.9 %convolution_convert_fusion.3 = bf16[192,1024]{1,0:T(8,128)(2,1)} fusion(bf16[192,2048]{1,0:T(8,128)(2,1)} %get-tuple-element.38.refs_3_, bf16[1024,2048]{1,0:T(8,128)(2,1)} %copy-done.7), kind=kOutput, calls=%fused_computation.42 | convolution fusion | flops 805502976 | bytes 5373952 | tf_op jit(solution)/shard_map/dot_general | solution.py:34
  258.2 2.3 copy-done.18
  260.6 8.7 %weight_grad.3 = (bf16[512,2048]{1,0:T(8,128)(2,1)S(1)}, bf16[512,2048]{1,0:T(8,128)(2,1)}) custom-call(s32[16]{0:T(128)S(1)} %fusion.33.place_ref, bf16[832,1024]{1,0:T(8,128)(2,1)S(1)} %copy-done.8, bf16[192,1024]{1,0:T(8,128)(2,1)S(1)} %copy-done.11, bf16[832,2048]{1,0:T(8,128)(2,1)S(1)} %copy-done.18, bf16[192,2048]{1,0:T(8,128)(2,1)S(1)} %copy-done.14), custom_call_target="tpu_custom_call" | custom-call | flops 6442450944 | bytes 16777216 | tf_op jit(solution)/shard_map/weight_grad/pallas_call | solution.py:323
  269.2 8.0 %weight_grad.4.refs_2_ = bf16[1024,2048]{1,0:T(8,128)(2,1)S(1)} custom-call(s32[16]{0:T(128)S(1)} %iota.25.place_ref, bf16[832,1024]{1,0:T(8,128)(2,1)S(1)} %copy-done.4, bf16[192,1024]{1,0:T(8,128)(2,1)S(1)} %copy-done.12, bf16[832,2048]{1,0:T(8,128)(2,1)S(1)} %copy-done.16, bf16[192,2048]{1,0:T(8,128)(2,1)S(1)} %copy-done.15), custom_call_target="tpu_custom_call" | custom-call | flops 6442450944 | bytes 16777216 | tf_op jit(solution)/shard_map/weight_grad/pallas_call | solution.py:323
  277.3 2.0 copy-done
  281.1 2.4 fusion.44
  287.6 3.5 convolution_convert_fusion.2.refs_0_
  291.1 2.4 add_convert_fusion.1.refs_1_
  296.2 28.8 %attend_bwd.1.refs_0_ = bf16[1024,1536]{1,0:T(8,128)(2,1)S(1)} custom-call(bf16[1024,1536]{1,0:T(8,128)(2,1)} %copy-done.17, bf16[1024,1536]{1,0:T(8,128)(2,1)} %copy-done.17, bf16[1024,1536]{1,0:T(8,128)(2,1)} %copy-done.17, bf16[1024,512]{1,0:T(8,128)(2,1)S(1)} %copy-done.10, bf16[1024,512]{1,0:T(8,128)(2,1)S(1)} %get-tuple-element.34.o_ref.refs_3_, ...), custom_call_target="tpu_custom_call" | custom-call | flops 12884901888 | bytes 8388608 | tf_op jit(solution)/shard_map/attend_bwd/pallas_call | solution.py:179
  328.1 11.7 %weight_grad.5 = (bf16[512,2048]{1,0:T(8,128)(2,1)}, bf16[512,2048]{1,0:T(8,128)(2,1)}) custom-call(s32[16]{0:T(128)} %copy-done.13, bf16[1024,1024]{1,0:T(8,128)(2,1)} %copy-done.52, bf16[1024,1536]{1,0:T(8,128)(2,1)} %after.22.refs_1_.refs_0_, bf16[1024,1024]{1,0:T(8,128)(2,1)} %pad_maximum_fusion.2.refs_2_, bf16[1024,512]{1,0:T(8,128)(2,1)} %copy-done.9), custom_call_target="tpu_custom_call" | custom-call | flops 6442450944 | bytes 16777216 | tf_op jit(solution)/shard_map/weight_grad/pallas_call | solution.py:323
  349.6 4.5 %all-to-all-start.2 = ((bf16[4,64,2048]{2,1,0:T(8,128)(2,1)}), bf16[4,64,2048]{2,1,0:T(8,128)(2,1)}, u32[]{:S(2)}, u32[]{:S(2)}) async-start(bf16[4,64,2048]{2,1,0:T(8,128)(2,1)} %bitcast.94), calls=%async_computation.2 | async-start | bytes 2097152 | tf_op jit(solution)/shard_map/all_to_all | solution.py:653
  355.7 3.1 add_convert_fusion.refs_1_
  362.8 6.9 %fusion.5 = (f32[1024]{0:T(1024)}, f32[1024,1024]{1,0:T(8,128)S(1)}) fusion(f32[1024]{0:T(1024)S(1)} %copy-done.71, f32[1024]{0:T(1024)S(1)} %copy-done.63, bf16[832,1024]{1,0:T(8,128)(2,1)S(1)} %bitcast.81, bf16[192,1024]{1,0:T(8,128)(2,1)S(1)} %bitcast.92, bf16[1024,1536]{1,0:T(8,128)(2,1)} %after.23, bf16[1024,2048]{1,0:T(8,128)(2,1)} %after.14.refs_1_), kind=kOutput, calls=%fused_computation.7 | convolution fusion | flops 3229613056 | bytes 12595200 | tf_op jit(solution)/shard_map/dot_general | solution.py:34
  373.9 2.0 copy-done.33
  377.0 2.1 collective-permute-start.15
  379.2 2.0 collective-permute-done.15
  382.0 7.0 %collective-permute-start.16 = (f32[6528]{0:T(1024)S(1)}, f32[6528]{0:T(1024)S(1)}, u32[]{:S(2)}, u32[]{:S(2)}) collective-permute-start(f32[6528]{0:T(1024)S(1)} %add.1019), channel_id=1, source_target_pairs={{0,16},{2,18},{4,20},{6,22},{8,24},{10,26},{12,28},{14,30},{16,0},... | collective-permute-start | bytes 78344 | tf_op jit(solution)/shard_map/ppermute | solution.py:728
  390.9 2.2 convert_reduce_fusion.1
  393.7 2.6 add_convert_fusion.2.refs_1_
  396.3 6.2 %all-to-all-start.1 = ((bf16[4,64,2048]{2,1,0:T(8,128)(2,1)}), bf16[4,64,2048]{2,1,0:T(8,128)(2,1)S(1)}, u32[]{:S(2)}, u32[]{:S(2)}) async-start(bf16[4,64,2048]{2,1,0:T(8,128)(2,1)} %bitcast.27), calls=%async_computation.1 | async-start | bytes 2097152 | tf_op jit(solution)/shard_map/all_to_all | solution.py:653
  404.4 7.2 %collective-permute-done.14 = bf16[512,1024]{1,0:T(8,128)(2,1)} collective-permute-done((bf16[512,1024]{1,0:T(8,128)(2,1)}, bf16[512,1024]{1,0:T(8,128)(2,1)}, u32[]{:S(2)}, u32[]{:S(2)}) %collective-permute-start.14) | collective-permute-done | bytes 1048608 | tf_op jit(solution)/shard_map/ppermute | solution.py:586
  411.6 2.6 multiply_reduce_fusion.1
  414.3 2.2 fusion.40
  416.6 2.3 collective-permute-start.20
  424.2 4.8 %all-to-all-done.1 = bf16[4,64,2048]{2,1,0:T(8,128)(2,1)S(1)} async-done(((bf16[4,64,2048]{2,1,0:T(8,128)(2,1)}), bf16[4,64,2048]{2,1,0:T(8,128)(2,1)S(1)}, u32[]{:S(2)}, u32[]{:S(2)}) %all-to-all-start.1) | async-done | bytes 1048608 | tf_op jit(solution)/shard_map/all_to_all | solution.py:653
  (362 shorter events, 94.4 us)
Async XLA Ops:
  7.2 73.2 %all-gather.4.cloned.1.call-start = ((), (), s32[]{:S(2)}) async-start(), calls=%async_computation.5 | async-start | bytes 4456448 | tf_op jit(solution)/shard_map/all_gather | solution.py:657
  14.0 16.9 %collective-permute-start = (f32[6,1024]{1,0:T(8,128)S(1)}, f32[6,1024]{1,0:T(8,128)S(1)}, u32[]{:S(2)}, u32[]{:S(2)}) collective-permute-start(f32[6,1024]{1,0:T(8,128)S(1)} %pad_maximum_fusion.8), channel_id=1, source_target_pairs={{0,1},{1,0},{2,3},{3,2},{4,5},{5,4},{6,7},{7,6},{8,9},{9,8},{10,11... | collective-permute-start | bytes 73736 | tf_op jit(solution)/shard_map/ppermute | solution.py:586
  18.1 62.3 %all-to-all-start = ((bf16[4,64,2048]{2,1,0:T(8,128)(2,1)}), bf16[4,64,2048]{2,1,0:T(8,128)(2,1)S(1)}, u32[]{:S(2)}, u32[]{:S(2)}) async-start(bf16[4,64,2048]{2,1,0:T(8,128)(2,1)} %bitcast.12), calls=%async_computation | async-start | bytes 2097152 | tf_op jit(solution)/shard_map/all_to_all | solution.py:653
  23.0 151.7 %all-gather.6.cloned.1.call-start = ((), (), s32[]{:S(2)}) async-start(), calls=%async_computation.6 | async-start | bytes 4456448 | tf_op jit(solution)/shard_map/all_gather | solution.py:657
  24.8 58.1 %copy-start.19 = (bf16[2,416,1024]{2,1,0:T(8,128)(2,1)}, bf16[2,416,1024]{2,1,0:T(8,128)(2,1)S(1)}, u32[]{:S(2)}) copy-start(bf16[2,416,1024]{2,1,0:T(8,128)(2,1)S(1)} %slice.154) | copy-start | bytes 5111812
  26.6 56.4 %copy-start.39 = (bf16[2,96,1024]{2,1,0:T(8,128)(2,1)}, bf16[2,96,1024]{2,1,0:T(8,128)(2,1)S(1)}, u32[]{:S(2)}) copy-start(bf16[2,96,1024]{2,1,0:T(8,128)(2,1)S(1)} %slice.153) | copy-start | bytes 1179652
  81.5 129.2 %all-gather.8.cloned.1.call-start = ((), (), s32[]{:S(2)}) async-start(), calls=%async_computation.7 | async-start | bytes 4456448 | tf_op jit(solution)/shard_map/all_gather | solution.py:657
  88.8 15.5 %copy-start.17 = (bf16[1024,1536]{1,0:T(8,128)(2,1)}, bf16[1024,1536]{1,0:T(8,128)(2,1)S(1)}, u32[]{:S(2)}) copy-start(bf16[1024,1536]{1,0:T(8,128)(2,1)S(1)} %convolution_convert_fusion.q_ref.k_ref.v_ref) | copy-start | bytes 9437188
  104.3 190.7 %copy-start.9 = (bf16[1024,512]{1,0:T(8,128)(2,1)}, bf16[1024,512]{1,0:T(8,128)(2,1)S(1)}, u32[]{:S(2)}) copy-start(bf16[1024,512]{1,0:T(8,128)(2,1)S(1)} %get-tuple-element.34.o_ref.refs_3_) | copy-start | bytes 3145732
  106.7 20.7 %collective-permute-start.1 = (f32[192,1024]{1,0:T(8,128)}, f32[192,1024]{1,0:T(8,128)}, u32[]{:S(2)}, u32[]{:S(2)}) collective-permute-start(f32[192,1024]{1,0:T(8,128)} %fusion.15.refs_1_), channel_id=1, source_target_pairs={{0,1},{1,0},{2,3},{3,2},{4,5},{5,4},{6,7},{7,6},{8,9},{9,8},{10,11... | collective-permute-start | bytes 2359304 | tf_op jit(solution)/shard_map/ppermute | solution.py:586
  113.7 31.3 %collective-permute-start.6 = (bf16[416,1024]{1,0:T(8,128)(2,1)}, bf16[416,1024]{1,0:T(8,128)(2,1)}, u32[]{:S(2)}, u32[]{:S(2)}) collective-permute-start(bf16[416,1024]{1,0:T(8,128)(2,1)} %dynamic-slice_convert_fusion.2.refs_1_), channel_id=1, source_target_pairs={{0,1},{1,0},{2,3},{3,2},{4,5},{5,4},{6,7},{7,6},{8,9},{9,8},{10,11... | collective-permute-start | bytes 2555912 | tf_op jit(solution)/shard_map/ppermute | solution.py:586
  114.2 34.4 %collective-permute-start.2 = (bf16[256,2048]{1,0:T(8,128)(2,1)S(1)}, bf16[256,2048]{1,0:T(8,128)(2,1)S(1)}, u32[]{:S(2)}, u32[]{:S(2)}) collective-permute-start(bf16[256,2048]{1,0:T(8,128)(2,1)S(1)} %bitcast.72), channel_id=1, source_target_pairs={{0,4},{2,6},{4,0},{6,2},{8,12},{10,14},{12,8},{14,10},{16,20},{18,... | collective-permute-start | bytes 3145736 | tf_op jit(solution)/shard_map/ppermute | solution.py:647
  127.4 17.6 %copy-start.20 = (bf16[2,416,1024]{2,1,0:T(8,128)(2,1)S(1)}, bf16[2,416,1024]{2,1,0:T(8,128)(2,1)}, u32[]{:S(2)}) copy-start(bf16[2,416,1024]{2,1,0:T(8,128)(2,1)} %copy-done.19) | copy-start | bytes 5111812
  130.1 17.4 %copy-start.58 = (f32[1024]{0:T(1024)S(1)}, f32[1024]{0:T(1024)}, u32[]{:S(2)}) copy-start(f32[1024]{0:T(1024)} %param.23) | copy-start | bytes 12292
  149.7 204.4 %reduce-scatter.5.cloned.1.call-start = ((), (), s32[]{:S(2)}) async-start(), calls=%async_computation.9 | async-start | bytes 2228224 | tf_op jit(solution)/shard_map/reduce_scatter | solution.py:661
  149.8 5.7 %collective-permute-start.3 = (bf16[256,2048]{1,0:T(8,128)(2,1)S(1)}, bf16[256,2048]{1,0:T(8,128)(2,1)}, u32[]{:S(2)}, u32[]{:S(2)}) collective-permute-start(bf16[256,2048]{1,0:T(8,128)(2,1)S(1)} %bitcast.73), channel_id=1, source_target_pairs={{0,2},{2,0},{4,6},{6,4},{8,10},{10,8},{12,14},{14,12},{16,18},{18,... | collective-permute-start | bytes 3145736 | tf_op jit(solution)/shard_map/ppermute | solution.py:647
  149.9 5.6 %collective-permute-start.4 = (bf16[256,2048]{1,0:T(8,128)(2,1)}, bf16[256,2048]{1,0:T(8,128)(2,1)}, u32[]{:S(2)}, u32[]{:S(2)}) collective-permute-start(bf16[256,2048]{1,0:T(8,128)(2,1)} %copy-done.5), channel_id=1, source_target_pairs={{0,2},{2,0},{4,6},{6,4},{8,10},{10,8},{12,14},{14,12},{16,18},{18,... | collective-permute-start | bytes 3145736 | tf_op jit(solution)/shard_map/ppermute | solution.py:647
  150.4 107.8 %copy-start.13 = (s32[16]{0:T(128)}, s32[16]{0:T(128)S(1)}, u32[]{:S(2)}) copy-start(s32[16]{0:T(128)S(1)} %fusion.33.place_ref) | copy-start | bytes 196
  150.4 21.3 %collective-permute-start.7 = (bf16[416,1024]{1,0:T(8,128)(2,1)}, bf16[416,1024]{1,0:T(8,128)(2,1)}, u32[]{:S(2)}, u32[]{:S(2)}) collective-permute-start(bf16[416,1024]{1,0:T(8,128)(2,1)} %multiply_convert_fusion.refs_2_), channel_id=1, source_target_pairs={{0,1},{1,0},{2,3},{3,2},{4,5},{5,4},{6,7},{7,6},{8,9},{9,8},{10,11... | collective-permute-start | bytes 2555912 | tf_op jit(solution)/shard_map/ppermute | solution.py:586
  159.0 14.3 %copy-start.7 = (bf16[1024,2048]{1,0:T(8,128)(2,1)}, bf16[1024,2048]{1,0:T(8,128)(2,1)S(1)}, u32[]{:S(2)}) copy-start(bf16[1024,2048]{1,0:T(8,128)(2,1)S(1)} %assemble.1.up_ref) | copy-start | bytes 12582916
  159.0 12.6 %copy-start.23 = (f32[416,1024]{1,0:T(8,128)S(1)}, f32[416,1024]{1,0:T(8,128)}, u32[]{:S(2)}) copy-start(f32[416,1024]{1,0:T(8,128)} %copy-done.22) | copy-start | bytes 5111812
  182.3 26.1 %collective-permute-start.5 = (f32[192,1024]{1,0:T(8,128)}, f32[192,1024]{1,0:T(8,128)}, u32[]{:S(2)}, u32[]{:S(2)}) collective-permute-start(f32[192,1024]{1,0:T(8,128)} %mlp_tri.1), channel_id=1, source_target_pairs={{0,1},{1,0},{2,3},{3,2},{4,5},{5,4},{6,7},{7,6},{8,9},{9,8},{10,11... | collective-permute-start | bytes 2359304 | tf_op jit(solution)/shard_map/ppermute | solution.py:586
  208.0 28.4 %collective-permute-start.9 = (bf16[416,1024]{1,0:T(8,128)(2,1)}, bf16[416,1024]{1,0:T(8,128)(2,1)}, u32[]{:S(2)}, u32[]{:S(2)}) collective-permute-start(bf16[416,1024]{1,0:T(8,128)(2,1)} %dynamic-slice_convert_fusion.1.refs_1_), channel_id=1, source_target_pairs={{0,1},{1,0},{2,3},{3,2},{4,5},{5,4},{6,7},{7,6},{8,9},{9,8},{10,11... | collective-permute-start | bytes 2555912 | tf_op jit(solution)/shard_map/ppermute | solution.py:586
  210.7 22.6 %copy-start.51 = (bf16[192,1024]{1,0:T(8,128)(2,1)S(1)}, bf16[192,1024]{1,0:T(8,128)(2,1)}, u32[]{:S(2)}) copy-start(bf16[192,1024]{1,0:T(8,128)(2,1)} %after.18.tokens_ref) | copy-start | bytes 1179652
  236.4 166.2 %reduce-scatter.3.cloned.1.call-start = ((), (), s32[]{:S(2)}) async-start(), calls=%async_computation.8 | async-start | bytes 4456448 | tf_op jit(solution)/shard_map/reduce_scatter | solution.py:661
  243.4 41.2 %collective-permute-start.10 = (bf16[416,1024]{1,0:T(8,128)(2,1)}, bf16[416,1024]{1,0:T(8,128)(2,1)}, u32[]{:S(2)}, u32[]{:S(2)}) collective-permute-start(bf16[416,1024]{1,0:T(8,128)(2,1)} %get-tuple-element.91), channel_id=1, source_target_pairs={{0,1},{1,0},{2,3},{3,2},{4,5},{5,4},{6,7},{7,6},{8,9},{9,8},{10,11... | collective-permute-start | bytes 2555912 | tf_op jit(solution)/shard_map/ppermute | solution.py:586
  257.4 21.9 %collective-permute-start.8 = (bf16[192,1024]{1,0:T(8,128)(2,1)}, bf16[192,1024]{1,0:T(8,128)(2,1)}, u32[]{:S(2)}, u32[]{:S(2)}) collective-permute-start(bf16[192,1024]{1,0:T(8,128)(2,1)} %convolution_convert_fusion.3), channel_id=1, source_target_pairs={{0,1},{1,0},{2,3},{3,2},{4,5},{5,4},{6,7},{7,6},{8,9},{9,8},{10,11... | collective-permute-start | bytes 1179656 | tf_op jit(solution)/shard_map/ppermute | solution.py:586
  269.2 21.9 %collective-permute-start.11 = (bf16[512,2048]{1,0:T(8,128)(2,1)}, bf16[512,2048]{1,0:T(8,128)(2,1)}, u32[]{:S(2)}, u32[]{:S(2)}) collective-permute-start(bf16[512,2048]{1,0:T(8,128)(2,1)} %get-tuple-element.40), channel_id=1, source_target_pairs={{0,2},{2,0},{4,6},{6,4},{8,10},{10,8},{12,14},{14,12},{16,18},{18,... | collective-permute-start | bytes 6291464 | tf_op jit(solution)/shard_map/ppermute | solution.py:647
  294.9 31.8 %collective-permute-start.12 = (bf16[256,2048]{1,0:T(8,128)(2,1)S(1)}, bf16[256,2048]{1,0:T(8,128)(2,1)S(1)}, u32[]{:S(2)}, u32[]{:S(2)}) collective-permute-start(bf16[256,2048]{1,0:T(8,128)(2,1)S(1)} %slice.165), channel_id=1, source_target_pairs={{0,4},{2,6},{4,0},{6,2},{8,12},{10,14},{12,8},{14,10},{16,20},{18,... | collective-permute-start | bytes 3145736 | tf_op jit(solution)/shard_map/ppermute | solution.py:647
  296.2 30.5 %copy-start.38 = (bf16[512,2048]{1,0:T(8,128)(2,1)S(1)}, bf16[512,2048]{1,0:T(8,128)(2,1)}, u32[]{:S(2)}) copy-start(bf16[512,2048]{1,0:T(8,128)(2,1)} %copy-done.37) | copy-start | bytes 6291460
  328.1 12.1 %copy-start.40 = (bf16[2,96,1024]{2,1,0:T(8,128)(2,1)S(1)}, bf16[2,96,1024]{2,1,0:T(8,128)(2,1)}, u32[]{:S(2)}) copy-start(bf16[2,96,1024]{2,1,0:T(8,128)(2,1)} %copy-done.39) | copy-start | bytes 1179652
  328.1 12.2 %copy-start.21 = (bf16[2,416,1024]{2,1,0:T(8,128)(2,1)S(1)}, bf16[2,416,1024]{2,1,0:T(8,128)(2,1)}, u32[]{:S(2)}) copy-start(bf16[2,416,1024]{2,1,0:T(8,128)(2,1)} %copy-done.19) | copy-start | bytes 5111812
  339.7 15.9 %collective-permute-start.13 = (bf16[512,2048]{1,0:T(8,128)(2,1)}, bf16[512,2048]{1,0:T(8,128)(2,1)}, u32[]{:S(2)}, u32[]{:S(2)}) collective-permute-start(bf16[512,2048]{1,0:T(8,128)(2,1)} %get-tuple-element.45), channel_id=1, source_target_pairs={{0,2},{2,0},{4,6},{6,4},{8,10},{10,8},{12,14},{14,12},{16,18},{18,... | collective-permute-start | bytes 6291464 | tf_op jit(solution)/shard_map/ppermute | solution.py:647
  349.6 41.2 %all-to-all-start.2 = ((bf16[4,64,2048]{2,1,0:T(8,128)(2,1)}), bf16[4,64,2048]{2,1,0:T(8,128)(2,1)}, u32[]{:S(2)}, u32[]{:S(2)}) async-start(bf16[4,64,2048]{2,1,0:T(8,128)(2,1)} %bitcast.94), calls=%async_computation.2 | async-start | bytes 2097152 | tf_op jit(solution)/shard_map/all_to_all | solution.py:653
  354.2 25.0 %collective-permute-start.21 = (bf16[64,1024]{1,0:T(8,128)(2,1)}, bf16[64,1024]{1,0:T(8,128)(2,1)S(1)}, u32[]{:S(2)}, u32[]{:S(2)}) collective-permute-start(bf16[64,1024]{1,0:T(8,128)(2,1)} %reduce-scatter.5.cloned.1.call-done), channel_id=1, source_target_pairs={{0,1},{1,0},{2,3},{3,2},{4,5},{5,4},{6,7},{7,6},{8,9},{9,8},{10,11... | collective-permute-start | bytes 393224 | tf_op jit(solution)/shard_map/ppermute | solution.py:586
  361.2 32.5 %collective-permute-start.18 = (bf16[256,2048]{1,0:T(8,128)(2,1)}, bf16[256,2048]{1,0:T(8,128)(2,1)}, u32[]{:S(2)}, u32[]{:S(2)}) collective-permute-start(bf16[256,2048]{1,0:T(8,128)(2,1)} %slice.169), channel_id=1, source_target_pairs={{0,4},{2,6},{4,0},{6,2},{8,12},{10,14},{12,8},{14,10},{16,20},{18,... | collective-permute-start | bytes 3145736 | tf_op jit(solution)/shard_map/ppermute | solution.py:647
  377.0 16.7 %copy-start.36 = (bf16[512,2048]{1,0:T(8,128)(2,1)S(1)}, bf16[512,2048]{1,0:T(8,128)(2,1)}, u32[]{:S(2)}) copy-start(bf16[512,2048]{1,0:T(8,128)(2,1)} %copy-done.35) | copy-start | bytes 6291460
  377.0 4.2 collective-permute-start.15
  382.0 8.8 %collective-permute-start.16 = (f32[6528]{0:T(1024)S(1)}, f32[6528]{0:T(1024)S(1)}, u32[]{:S(2)}, u32[]{:S(2)}) collective-permute-start(f32[6528]{0:T(1024)S(1)} %add.1019), channel_id=1, source_target_pairs={{0,16},{2,18},{4,20},{6,22},{8,24},{10,26},{12,28},{14,30},{16,0},... | collective-permute-start | bytes 78344 | tf_op jit(solution)/shard_map/ppermute | solution.py:728
  389.8 21.8 %collective-permute-start.14 = (bf16[512,1024]{1,0:T(8,128)(2,1)}, bf16[512,1024]{1,0:T(8,128)(2,1)}, u32[]{:S(2)}, u32[]{:S(2)}) collective-permute-start(bf16[512,1024]{1,0:T(8,128)(2,1)} %dynamic-slice_convert_fusion.refs_1_), channel_id=1, source_target_pairs={{0,1},{1,0},{2,3},{3,2},{4,5},{5,4},{6,7},{7,6},{8,9},{9,8},{10,11... | collective-permute-start | bytes 3145736 | tf_op jit(solution)/shard_map/ppermute | solution.py:586
  390.8 2.2 collective-permute-start.17
  396.3 15.3 %copy-start.30 = (f32[416,1024]{1,0:T(8,128)S(1)}, f32[416,1024]{1,0:T(8,128)}, u32[]{:S(2)}) copy-start(f32[416,1024]{1,0:T(8,128)} %copy-done.29) | copy-start | bytes 5111812
  396.3 15.3 %copy-start.47 = (f32[96,1024]{1,0:T(8,128)S(1)}, f32[96,1024]{1,0:T(8,128)}, u32[]{:S(2)}) copy-start(f32[96,1024]{1,0:T(8,128)} %copy-done.46) | copy-start | bytes 1179652
  396.3 15.3 %copy-start.61 = (f32[1024]{0:T(1024)S(1)}, f32[1024]{0:T(1024)}, u32[]{:S(2)}) copy-start(f32[1024]{0:T(1024)} %param.20) | copy-start | bytes 12292
  396.3 15.3 %copy-start.69 = (f32[512]{0:T(512)S(1)}, f32[512]{0:T(512)}, u32[]{:S(2)}) copy-start(f32[512]{0:T(512)} %broadcast_multiply_fusion.1) | copy-start | bytes 6148
  396.3 32.6 %all-to-all-start.1 = ((bf16[4,64,2048]{2,1,0:T(8,128)(2,1)}), bf16[4,64,2048]{2,1,0:T(8,128)(2,1)S(1)}, u32[]{:S(2)}, u32[]{:S(2)}) async-start(bf16[4,64,2048]{2,1,0:T(8,128)(2,1)} %bitcast.27), calls=%async_computation.1 | async-start | bytes 2097152 | tf_op jit(solution)/shard_map/all_to_all | solution.py:653
  402.6 14.0 %collective-permute-start.19 = (f32[6528]{0:T(1024)}, f32[6528]{0:T(1024)S(1)}, u32[]{:S(2)}, u32[]{:S(2)}) collective-permute-start(f32[6528]{0:T(1024)} %after.25), channel_id=1, source_target_pairs={{0,1},{1,0},{2,3},{3,2},{4,5},{5,4},{6,7},{7,6},{8,9},{9,8},{10,11... | collective-permute-start | bytes 78344 | tf_op jit(solution)/shard_map/ppermute | solution.py:728
  416.6 4.2 collective-permute-start.20
  (65 other events, 247.6 us)
Sparse Core Ops, SparseCore 0:
  13.3 67.1 all-gather.3
  83.2 53.2 all-gather.5
  149.9 49.2 all-gather.7
  236.5 59.7 reduce-scatter.4
  300.6 78.4 reduce-scatter.2

commit v3 on v2

--- a/solution.py
+++ b/solution.py
@@ -202,7 +202,7 @@
     )(projected, projected, projected, grad_heads, attended, lse)
 
 
-def mlp_mid_kernel(nb_ref, gm_ref, up_ref, down_ref, act_ref, gup_ref, *, block):
+def mlp_mid_kernel(nb_ref, gm_ref, up_ref, down_ref, act_ref, gup_ref, *back, block):
     up = up_ref[...]
     down = down_ref[...]
     for b in range(nb_ref.shape[0] // block):
@@ -210,9 +210,19 @@
         value, slope = gelu_parts(dot(nb_ref[rows, :], up))
         act_ref[rows, :] = value.astype(BF16)
         gup_ref[rows, :] = (slope * dot(gm_ref[rows, :], down)).astype(BF16)
-
-
-def mlp_mid(normed, grad, up_full, down_full):
+    for back_ref in back:
+        part = dot(gup_ref[...], up, NT)
+
+        @pl.when(pl.program_id(0) == 0)
+        def _():
+            back_ref[...] = part
+
+        @pl.when(pl.program_id(0) > 0)
+        def _():
+            back_ref[...] += part
+
+
+def mlp_mid(normed, grad, up_full, down_full, back=False):
     rows, depth = normed.shape
     width = up_full.shape[1]
     cols = min(width, 512)
@@ -228,8 +238,9 @@
         functools.partial(mlp_mid_kernel, block=block),
         grid=(width // cols,),
         in_specs=[whole, whole, weight, weight],
-        out_specs=[result, result],
-        out_shape=[jax.ShapeDtypeStruct((rows, width), BF16)] * 2,
+        out_specs=[result, result] + [whole] * back,
+        out_shape=[jax.ShapeDtypeStruct((rows, width), BF16)] * 2
+        + [jax.ShapeDtypeStruct((rows, depth), F32)] * back,
         compiler_params=pltpu.CompilerParams(vmem_limit_bytes=60 * 1024 * 1024),
         cost_estimate=cost(
             8 * rows * depth * width, 4 * (rows + width) * depth + 4 * rows * width, rows * width
@@ -866,12 +877,12 @@
     gnb_rest = tp_sum_own(gnb_mine, gnb_theirs, grad_tokens)
     go_tri = og_tri + grad_tokens
     gm_tri = go_tri.astype(BF16)
-    act_tri, gup_tri = mlp_mid(normed_tri, gm_tri, up_full, down_t)
-    gnb_tri = tp_sum(dot(gup_tri, up_full, NT).astype(BF16))
+    act_tri, gup_tri, back_part = mlp_mid(normed_tri, gm_tri, up_full, down_t, back=True)
+    gnb_tri = tp_sum(back_part.astype(BF16))
     grad_down = weight_grad(in_order, 1, ((gm_rest, gm_tri), (act_rest, act_tri)))[0]
     sum_down = scatter_plain(grad_down).astype(F32)
     width = grad_units.shape[1] // tp_count if tp_count == 2 else grad_units.shape[1]
-    sum_unpatch = scatter_plain(dot(tokens, own_columns(grad_units, width), TN).astype(BF16))
+    sum_unpatch = scatter_plain(dot(tokens, own_columns(grad_units, width), TN))
     grad_up = weight_grad(places, 2, ((normed_rest, normed_tri), (gup_rest, gup_tri)))
     _, back_rest = jax.vjp(layer_norm, hidden_rest, mlp_gain)
     gh_rest, gain_rest = back_rest(gnb_rest)

time: 442 us -> 455 us (1.029)
  waiting for transfers between devices: 100 us -> 122 us
  matrix products: 32.6 us -> 27.8 us
    ppermute x10, waiting for transfers between devices: 46.3 us -> 56.5 us  [swap(): return lax.ppermute(x, axis, [(0, 1), (1, 0)])]
    ppermute x5, waiting for transfers between devices: 3.3 us -> 9.54 us  [hop_sums(): vec = vec + lax.ppermute(vec, axis, [(i, i ^ step) for i in range(size)])]
    dot_general x8 -> x7, matrix products: 32.6 us -> 27.8 us  [dot(): lax.dot_general(a, b, dims, precision=precision, preferred_element_type=F32)]
    unnamed x181 -> x179, local copies, waits for them, and re-layouts: 27.2 us -> 29.4 us
  transfers between devices with their start and end apart: 30 -> 30, of which waited for: 9 -> 10; matrix products, arithmetic and copies ran while one was open for 28% -> 24% of each run, Pallas kernels for 29% -> 24%
where the time goes in v3:
time: 455 us; the launch traced here: 450 us
  Pallas kernels  129 us (28%)
  waiting for transfers between devices  122 us (27%)
  other arithmetic  65 us (14%)
  local copies, waits for them, and re-layouts  51 us (11%)
  starting transfers between devices  39.3 us (9%)
  matrix products  27.8 us (6%)
  between operations  15.9 us (3%)
    ppermute x10, waiting for transfers between devices, swap(): return lax.ppermute(x, axis, [(0, 1), (1, 0)])  56.5 us
    all_gather x3, waiting for transfers between devices, gather_plain(): return lax.all_gather(shard, 'seq', axis=0, tiled=True)  45.7 us
    unnamed x179, local copies, waits for them, and re-layouts  29.4 us
    pallas_call x1, Pallas kernels, attend_bwd(): pl.pallas_call(functools.partial(attend_bwd_kernel, scale=HEAD_DIM ** (-0...  29.1 us
    pallas_call x3, Pallas kernels, weight_grad(): pl.pallas_call(functools.partial(weight_grad_kernel, segments=tuple(marks...  28.1 us
    dot_general x7, matrix products, dot(): lax.dot_general(a, b, dims, precision=precision, preferred_element_type=F32)  27.8 us
    pallas_call x2, Pallas kernels, mlp_mid(): pl.pallas_call(functools.partial(mlp_mid_kernel, block=block), grid=(widt...  22.9 us
    pallas_call x1, Pallas kernels, scene_pass(): pl.pallas_call(functools.partial(scene_kernel, per_slab=slab_edges // blo...  22.6 us
  transfers between devices with their start and end apart: 30, of which 10 were waited for; matrix products, arithmetic and copies ran while one was open for 24% of the time, Pallas kernels for 24%

profile of v3, /device:TPU:0, one launch (start us, length us, event | category | flops | bytes accessed | tf_op | source)
XLA Modules:
  0.0 449.9 jit_solution(13158431676051105859)
XLA Ops:
  14.0 3.0 collective-permute-start
  18.1 4.9 %all-to-all-start = ((bf16[4,64,2048]{2,1,0:T(8,128)(2,1)}), bf16[4,64,2048]{2,1,0:T(8,128)(2,1)S(1)}, u32[]{:S(2)}, u32[]{:S(2)}) async-start(bf16[4,64,2048]{2,1,0:T(8,128)(2,1)} %bitcast.12), calls=%async_computation | async-start | bytes 2097152 | tf_op jit(solution)/shard_map/all_to_all | solution.py:664
  34.8 45.7 %all-gather.4.cloned.1.call-done.refs_0_ = bf16[1024,2048]{1,0:T(8,128)(2,1)} async-done(((bf16[64,2048]{1,0:T(8,128)(2,1)}), bf16[1024,2048]{1,0:T(8,128)(2,1)}) %all-gather.4.cloned.1.call-update) | async-done | bytes 4194320 | tf_op jit(solution)/shard_map/all_gather | solution.py:668
  85.1 3.6 convolution_convert_fusion.q_ref.k_ref.v_ref
  88.8 15.5 %attend_fwd.1 = (bf16[1024,512]{1,0:T(8,128)(2,1)S(1)}, f32[4,8,1024]{2,1,0:T(8,128)S(1)}) custom-call(bf16[1024,1536]{1,0:T(8,128)(2,1)S(1)} %convolution_convert_fusion.q_ref.k_ref.v_ref, bf16[1024,1536]{1,0:T(8,128)(2,1)S(1)} %convolution_convert_fusion.q_ref.k_ref.v_ref, bf16[1024,1536]{1,0:T(8,128)(2,1)S(1)} %convolution_convert_fusion.q_ref.k_ref.v_ref), custom_call_target="tpu_custom_call" | custom-call | flops 6442450944 | bytes 4194304 | tf_op jit(solution)/shard_map/attend_fwd/pallas_call | solution.py:101
  108.2 2.7 fusion.11
  114.7 12.7 %collective-permute-done.1.refs_0_ = f32[192,1024]{1,0:T(8,128)} collective-permute-done((f32[192,1024]{1,0:T(8,128)}, f32[192,1024]{1,0:T(8,128)}, u32[]{:S(2)}, u32[]{:S(2)}) %collective-permute-start.1) | collective-permute-done | bytes 786464 | tf_op jit(solution)/shard_map/ppermute | solution.py:597
  127.4 2.7 fusion.47
  130.1 14.9 %collective-permute-done.6 = bf16[416,1024]{1,0:T(8,128)(2,1)} collective-permute-done((bf16[416,1024]{1,0:T(8,128)(2,1)}, bf16[416,1024]{1,0:T(8,128)(2,1)}, u32[]{:S(2)}, u32[]{:S(2)}) %collective-permute-start.6) | collective-permute-done | bytes 852000 | tf_op jit(solution)/shard_map/ppermute | solution.py:597
  145.0 2.1 fusion.46
  155.5 3.3 assemble.1.up_ref
  160.0 11.5 %collective-permute-done.7 = bf16[416,1024]{1,0:T(8,128)(2,1)} collective-permute-done((bf16[416,1024]{1,0:T(8,128)(2,1)}, bf16[416,1024]{1,0:T(8,128)(2,1)}, u32[]{:S(2)}, u32[]{:S(2)}) %collective-permute-start.7) | collective-permute-done | bytes 852000 | tf_op jit(solution)/shard_map/ppermute | solution.py:597
  174.5 7.5 %mlp_tri.1 = f32[192,1024]{1,0:T(8,128)} custom-call(bf16[192,1024]{1,0:T(8,128)(2,1)} %multiply_convert_fusion.1.nb_ref.refs_1_, bf16[1024,2048]{1,0:T(8,128)(2,1)} %copy-done.7, bf16[1024,2048]{1,0:T(8,128)(2,1)} %all-gather.6.cloned.1.call-done.down_ref), custom_call_target="tpu_custom_call" | custom-call | flops 4000000000 | bytes 8388608 | tf_op jit(solution)/shard_map/mlp_tri/pallas_call | solution.py:271
  182.1 1.8 collective-permute-start.5
  183.9 14.6 %mlp_mid.2 = (bf16[832,2048]{1,0:T(8,128)(2,1)}, bf16[832,2048]{1,0:T(8,128)(2,1)}) custom-call(bf16[832,1024]{1,0:T(8,128)(2,1)} %pad_maximum_fusion.4.nb_ref.refs_0_, bf16[832,1024]{1,0:T(8,128)(2,1)} %bitcast_convert_fusion.refs_4_.gm_ref.refs_0_, bf16[1024,2048]{1,0:T(8,128)(2,1)} %copy-done.7, bf16[1024,2048]{1,0:T(8,128)(2,1)} %all-gather.6.cloned.1.call-done.down_ref), custom_call_target="tpu_custom_call" | custom-call | flops 13958643712 | bytes 18612224 | tf_op jit(solution)/shard_map/mlp_mid/pallas_call | solution.py:237
  198.5 6.5 %fusion.56 = f32[832,1024]{1,0:T(8,128)S(1)} fusion(bf16[832,2048]{1,0:T(8,128)(2,1)} %get-tuple-element.36.refs_2_, bf16[1024,2048]{1,0:T(8,128)(2,1)} %copy-done.7), kind=kOutput, calls=%fused_computation.211 | convolution fusion | flops 3489660928 | bytes 11010048 | tf_op jit(solution)/shard_map/dot_general | solution.py:34
  208.6 2.1 add_convert_fusion.4.refs_0_
  210.6 22.6 %scene.1 = (f32[8,2048]{1,0:T(8,128)}, bf16[192,2048]{1,0:T(8,128)(2,1)}, f32[192,1024]{1,0:T(8,128)}, f32[64,32]{1,0:T(8,128)}, f32[64,1]{1,0:T(8,128)}, /*inde...) custom-call(s32[1]{0:T(128)} %bitcast.own_ref, bf16[192,1024]{1,0:T(8,128)(2,1)} %after.18.tokens_ref, ...), custom_call_target="tpu_custom_call" | custom-call | flops 24999999488 | bytes 16777216 | tf_op jit(solution)/shard_map/scene/pallas_call | solution.py:520
  233.2 3.7 fusion.17
  237.4 2.1 slice.163
  239.5 17.3 %collective-permute-done.9.refs_0_ = bf16[416,1024]{1,0:T(8,128)(2,1)} collective-permute-done((bf16[416,1024]{1,0:T(8,128)(2,1)}, bf16[416,1024]{1,0:T(8,128)(2,1)}, u32[]{:S(2)}, u32[]{:S(2)}) %collective-permute-start.9) | collective-permute-done | bytes 852000 | tf_op jit(solution)/shard_map/ppermute | solution.py:597
  256.8 2.5 multiply_reduce_fusion.2
  259.6 2.0 fusion.44
  265.1 8.3 %mlp_mid.3 = (bf16[192,2048]{1,0:T(8,128)(2,1)}, bf16[192,2048]{1,0:T(8,128)(2,1)}, f32[192,1024]{1,0:T(8,128)}) custom-call(bf16[192,1024]{1,0:T(8,128)(2,1)} %multiply_convert_fusion.1.nb_ref.refs_1_, bf16[192,1024]{1,0:T(8,128)(2,1)} %fusion.19.gm_ref.refs_1_, bf16[1024,2048]{1,0:T(8,128)(2,1)} %copy-done.7, ...), custom_call_target="tpu_custom_call" | custom-call | flops 3221225472 | bytes 10747904 | tf_op jit(solution)/shard_map/mlp_mid/pallas_call | solution.py:237
  273.4 1.9 convert_element_type.357
  279.3 2.0 copy-done.18
  281.3 8.7 %weight_grad.3 = (bf16[512,2048]{1,0:T(8,128)(2,1)S(1)}, bf16[512,2048]{1,0:T(8,128)(2,1)}) custom-call(s32[16]{0:T(128)S(1)} %fusion.34.place_ref, bf16[832,1024]{1,0:T(8,128)(2,1)S(1)} %copy-done.8, bf16[192,1024]{1,0:T(8,128)(2,1)S(1)} %copy-done.11, bf16[832,2048]{1,0:T(8,128)(2,1)S(1)} %copy-done.18, bf16[192,2048]{1,0:T(8,128)(2,1)S(1)} %copy-done.15), custom_call_target="tpu_custom_call" | custom-call | flops 6442450944 | bytes 16777216 | tf_op jit(solution)/shard_map/weight_grad/pallas_call | solution.py:334
  290.0 8.0 %weight_grad.4.refs_2_ = bf16[1024,2048]{1,0:T(8,128)(2,1)S(1)} custom-call(s32[16]{0:T(128)S(1)} %iota.25.place_ref, bf16[832,1024]{1,0:T(8,128)(2,1)S(1)} %copy-done.4, bf16[192,1024]{1,0:T(8,128)(2,1)S(1)} %copy-done.12, bf16[832,2048]{1,0:T(8,128)(2,1)S(1)} %copy-done.16, bf16[192,2048]{1,0:T(8,128)(2,1)S(1)} %copy-done.14), custom_call_target="tpu_custom_call" | custom-call | flops 6442450944 | bytes 16777216 | tf_op jit(solution)/shard_map/weight_grad/pallas_call | solution.py:334
  298.0 2.0 copy-done
  300.1 1.9 multiply_reduce_fusion.5
  302.1 2.3 fusion.45
  308.5 3.5 convolution_convert_fusion.1.refs_0_
  312.0 2.4 add_convert_fusion.1.refs_1_
  317.8 29.1 %attend_bwd.1.refs_0_ = bf16[1024,1536]{1,0:T(8,128)(2,1)S(1)} custom-call(bf16[1024,1536]{1,0:T(8,128)(2,1)} %copy-done.17, bf16[1024,1536]{1,0:T(8,128)(2,1)} %copy-done.17, bf16[1024,1536]{1,0:T(8,128)(2,1)} %copy-done.17, bf16[1024,512]{1,0:T(8,128)(2,1)S(1)} %copy-done.10, bf16[1024,512]{1,0:T(8,128)(2,1)S(1)} %get-tuple-element.35.o_ref.refs_3_, ...), custom_call_target="tpu_custom_call" | custom-call | flops 12884901888 | bytes 8388608 | tf_op jit(solution)/shard_map/attend_bwd/pallas_call | solution.py:179
  349.9 11.4 %weight_grad.5 = (bf16[512,2048]{1,0:T(8,128)(2,1)}, bf16[512,2048]{1,0:T(8,128)(2,1)}) custom-call(s32[16]{0:T(128)} %copy-done.13, bf16[1024,1024]{1,0:T(8,128)(2,1)} %copy-done.52, bf16[1024,1536]{1,0:T(8,128)(2,1)} %after.22.refs_1_.refs_0_, bf16[1024,1024]{1,0:T(8,128)(2,1)} %pad_maximum_fusion.2.refs_2_, bf16[1024,512]{1,0:T(8,128)(2,1)} %copy-done.9), custom_call_target="tpu_custom_call" | custom-call | flops 6442450944 | bytes 16777216 | tf_op jit(solution)/shard_map/weight_grad/pallas_call | solution.py:334
  364.4 4.5 %all-to-all-start.2 = ((bf16[4,64,2048]{2,1,0:T(8,128)(2,1)}), bf16[4,64,2048]{2,1,0:T(8,128)(2,1)}, u32[]{:S(2)}, u32[]{:S(2)}) async-start(bf16[4,64,2048]{2,1,0:T(8,128)(2,1)} %bitcast.92), calls=%async_computation.2 | async-start | bytes 2097152 | tf_op jit(solution)/shard_map/all_to_all | solution.py:664
  369.0 3.0 add_convert_fusion.refs_1_
  375.5 6.4 %fusion.5 = (f32[1024]{0:T(1024)S(1)}, f32[1024,1024]{1,0:T(8,128)S(1)}) fusion(f32[1024]{0:T(1024)S(1)} %copy-done.70, f32[1024]{0:T(1024)S(1)} %copy-done.63, bf16[832,1024]{1,0:T(8,128)(2,1)S(1)} %bitcast.79, bf16[192,1024]{1,0:T(8,128)(2,1)S(1)} %bitcast.90, bf16[1024,1536]{1,0:T(8,128)(2,1)} %after.23, bf16[1024,2048]{1,0:T(8,128)(2,1)} %after.14.refs_1_), kind=kOutput, calls=%fused_computation.7 | convolution fusion | flops 3229613056 | bytes 12595200 | tf_op jit(solution)/shard_map/dot_general | solution.py:34
  385.9 2.0 collective-permute-start.15
  388.5 5.8 %collective-permute-done.15 = f32[6528]{0:T(1024)S(1)} collective-permute-done((f32[6528]{0:T(1024)}, f32[6528]{0:T(1024)S(1)}, u32[]{:S(2)}, u32[]{:S(2)}) %collective-permute-start.15) | collective-permute-done | bytes 26144 | tf_op jit(solution)/shard_map/ppermute | solution.py:739
  395.0 4.6 %collective-permute-start.16 = (f32[6528]{0:T(1024)S(1)}, f32[6528]{0:T(1024)S(1)}, u32[]{:S(2)}, u32[]{:S(2)}) collective-permute-start(f32[6528]{0:T(1024)S(1)} %add.1019), channel_id=1, source_target_pairs={{0,16},{2,18},{4,20},{6,22},{8,24},{10,26},{12,28},{14,30},{16,0},... | collective-permute-start | bytes 78344 | tf_op jit(solution)/shard_map/ppermute | solution.py:739
  400.7 2.9 collective-permute-done.16
  403.7 2.2 convert_reduce_fusion.1
  406.5 2.6 add_convert_fusion.2.refs_1_
  409.1 4.4 all-to-all-start.1
  415.6 2.7 multiply_reduce_fusion.1
  420.1 2.8 fusion.41
  431.3 9.0 %all-to-all-done.1 = bf16[4,64,2048]{2,1,0:T(8,128)(2,1)} async-done(((bf16[4,64,2048]{2,1,0:T(8,128)(2,1)}), bf16[4,64,2048]{2,1,0:T(8,128)(2,1)}, u32[]{:S(2)}, u32[]{:S(2)}) %all-to-all-start.1) | async-done | bytes 1048608 | tf_op jit(solution)/shard_map/all_to_all | solution.py:664
  (360 shorter events, 94.3 us)
Async XLA Ops:
  7.2 9.8 %copy-start.56 = (bf16[64,2048]{1,0:T(8,128)(2,1)S(1)}, bf16[64,2048]{1,0:T(8,128)(2,1)}, u32[]{:S(2)}) copy-start(bf16[64,2048]{1,0:T(8,128)(2,1)} %param.24) | copy-start | bytes 786436
  7.2 73.2 %all-gather.4.cloned.1.call-start = ((), (), s32[]{:S(2)}) async-start(), calls=%async_computation.5 | async-start | bytes 4456448 | tf_op jit(solution)/shard_map/all_gather | solution.py:668
  14.0 16.9 %collective-permute-start = (f32[6,1024]{1,0:T(8,128)S(1)}, f32[6,1024]{1,0:T(8,128)S(1)}, u32[]{:S(2)}, u32[]{:S(2)}) collective-permute-start(f32[6,1024]{1,0:T(8,128)S(1)} %pad_maximum_fusion.9), channel_id=1, source_target_pairs={{0,1},{1,0},{2,3},{3,2},{4,5},{5,4},{6,7},{7,6},{8,9},{9,8},{10,11... | collective-permute-start | bytes 73736 | tf_op jit(solution)/shard_map/ppermute | solution.py:597
  18.1 62.3 %all-to-all-start = ((bf16[4,64,2048]{2,1,0:T(8,128)(2,1)}), bf16[4,64,2048]{2,1,0:T(8,128)(2,1)S(1)}, u32[]{:S(2)}, u32[]{:S(2)}) async-start(bf16[4,64,2048]{2,1,0:T(8,128)(2,1)} %bitcast.12), calls=%async_computation | async-start | bytes 2097152 | tf_op jit(solution)/shard_map/all_to_all | solution.py:664
  23.0 151.5 %all-gather.6.cloned.1.call-start = ((), (), s32[]{:S(2)}) async-start(), calls=%async_computation.6 | async-start | bytes 4456448 | tf_op jit(solution)/shard_map/all_gather | solution.py:668
  24.8 58.1 %copy-start.19 = (bf16[2,416,1024]{2,1,0:T(8,128)(2,1)}, bf16[2,416,1024]{2,1,0:T(8,128)(2,1)S(1)}, u32[]{:S(2)}) copy-start(bf16[2,416,1024]{2,1,0:T(8,128)(2,1)S(1)} %slice.154) | copy-start | bytes 5111812
  26.6 56.4 %copy-start.38 = (bf16[2,96,1024]{2,1,0:T(8,128)(2,1)}, bf16[2,96,1024]{2,1,0:T(8,128)(2,1)S(1)}, u32[]{:S(2)}) copy-start(bf16[2,96,1024]{2,1,0:T(8,128)(2,1)S(1)} %slice.153) | copy-start | bytes 1179652
  81.5 129.1 %all-gather.8.cloned.1.call-start = ((), (), s32[]{:S(2)}) async-start(), calls=%async_computation.7 | async-start | bytes 4456448 | tf_op jit(solution)/shard_map/all_gather | solution.py:668
  88.8 15.5 %copy-start.17 = (bf16[1024,1536]{1,0:T(8,128)(2,1)}, bf16[1024,1536]{1,0:T(8,128)(2,1)S(1)}, u32[]{:S(2)}) copy-start(bf16[1024,1536]{1,0:T(8,128)(2,1)S(1)} %convolution_convert_fusion.q_ref.k_ref.v_ref) | copy-start | bytes 9437188
  104.3 212.2 %copy-start.9 = (bf16[1024,512]{1,0:T(8,128)(2,1)}, bf16[1024,512]{1,0:T(8,128)(2,1)S(1)}, u32[]{:S(2)}) copy-start(bf16[1024,512]{1,0:T(8,128)(2,1)S(1)} %get-tuple-element.35.o_ref.refs_3_) | copy-start | bytes 3145732
  106.7 20.7 %collective-permute-start.1 = (f32[192,1024]{1,0:T(8,128)}, f32[192,1024]{1,0:T(8,128)}, u32[]{:S(2)}, u32[]{:S(2)}) collective-permute-start(f32[192,1024]{1,0:T(8,128)} %fusion.15.refs_1_), channel_id=1, source_target_pairs={{0,1},{1,0},{2,3},{3,2},{4,5},{5,4},{6,7},{7,6},{8,9},{9,8},{10,11... | collective-permute-start | bytes 2359304 | tf_op jit(solution)/shard_map/ppermute | solution.py:597
  113.6 31.4 %collective-permute-start.6 = (bf16[416,1024]{1,0:T(8,128)(2,1)}, bf16[416,1024]{1,0:T(8,128)(2,1)}, u32[]{:S(2)}, u32[]{:S(2)}) collective-permute-start(bf16[416,1024]{1,0:T(8,128)(2,1)} %dynamic-slice_convert_fusion.2.refs_1_), channel_id=1, source_target_pairs={{0,1},{1,0},{2,3},{3,2},{4,5},{5,4},{6,7},{7,6},{8,9},{9,8},{10,11... | collective-permute-start | bytes 2555912 | tf_op jit(solution)/shard_map/ppermute | solution.py:597
  114.1 34.5 %collective-permute-start.2 = (bf16[256,2048]{1,0:T(8,128)(2,1)S(1)}, bf16[256,2048]{1,0:T(8,128)(2,1)S(1)}, u32[]{:S(2)}, u32[]{:S(2)}) collective-permute-start(bf16[256,2048]{1,0:T(8,128)(2,1)S(1)} %bitcast.70), channel_id=1, source_target_pairs={{0,4},{2,6},{4,0},{6,2},{8,12},{10,14},{12,8},{14,10},{16,20},{18,... | collective-permute-start | bytes 3145736 | tf_op jit(solution)/shard_map/ppermute | solution.py:658
  127.4 17.6 %copy-start.20 = (bf16[2,416,1024]{2,1,0:T(8,128)(2,1)S(1)}, bf16[2,416,1024]{2,1,0:T(8,128)(2,1)}, u32[]{:S(2)}) copy-start(bf16[2,416,1024]{2,1,0:T(8,128)(2,1)} %copy-done.19) | copy-start | bytes 5111812
  130.1 17.3 %copy-start.59 = (f32[1024]{0:T(1024)S(1)}, f32[1024]{0:T(1024)}, u32[]{:S(2)}) copy-start(f32[1024]{0:T(1024)} %param.23) | copy-start | bytes 12292
  149.7 265.4 %reduce-scatter.5.cloned.1.call-start = ((), (), s32[]{:S(2)}) async-start(), calls=%async_computation.9 | async-start | bytes 4456448 | tf_op jit(solution)/shard_map/reduce_scatter | solution.py:672
  149.7 3.4 collective-permute-start.3
  149.8 4.5 collective-permute-start.4
  150.3 21.2 %collective-permute-start.7 = (bf16[416,1024]{1,0:T(8,128)(2,1)}, bf16[416,1024]{1,0:T(8,128)(2,1)}, u32[]{:S(2)}, u32[]{:S(2)}) collective-permute-start(bf16[416,1024]{1,0:T(8,128)(2,1)} %multiply_convert_fusion.refs_2_), channel_id=1, source_target_pairs={{0,1},{1,0},{2,3},{3,2},{4,5},{5,4},{6,7},{7,6},{8,9},{9,8},{10,11... | collective-permute-start | bytes 2555912 | tf_op jit(solution)/shard_map/ppermute | solution.py:597
  158.8 14.4 %copy-start.7 = (bf16[1024,2048]{1,0:T(8,128)(2,1)}, bf16[1024,2048]{1,0:T(8,128)(2,1)S(1)}, u32[]{:S(2)}) copy-start(bf16[1024,2048]{1,0:T(8,128)(2,1)S(1)} %assemble.1.up_ref) | copy-start | bytes 12582916
  158.8 12.7 %copy-start.23 = (f32[416,1024]{1,0:T(8,128)S(1)}, f32[416,1024]{1,0:T(8,128)}, u32[]{:S(2)}) copy-start(f32[416,1024]{1,0:T(8,128)} %copy-done.22) | copy-start | bytes 5111812
  182.1 25.9 %collective-permute-start.5 = (f32[192,1024]{1,0:T(8,128)}, f32[192,1024]{1,0:T(8,128)}, u32[]{:S(2)}, u32[]{:S(2)}) collective-permute-start(f32[192,1024]{1,0:T(8,128)} %mlp_tri.1), channel_id=1, source_target_pairs={{0,1},{1,0},{2,3},{3,2},{4,5},{5,4},{6,7},{7,6},{8,9},{9,8},{10,11... | collective-permute-start | bytes 2359304 | tf_op jit(solution)/shard_map/ppermute | solution.py:597
  210.6 22.6 %copy-start.48 = (bf16[192,1024]{1,0:T(8,128)(2,1)S(1)}, bf16[192,1024]{1,0:T(8,128)(2,1)}, u32[]{:S(2)}) copy-start(bf16[192,1024]{1,0:T(8,128)(2,1)} %after.18.tokens_ref) | copy-start | bytes 1179652
  237.0 181.3 %reduce-scatter.3.cloned.1.call-start = ((), (), s32[]{:S(2)}) async-start(), calls=%async_computation.8 | async-start | bytes 4456448 | tf_op jit(solution)/shard_map/reduce_scatter | solution.py:672
  237.0 19.8 %collective-permute-start.9 = (bf16[416,1024]{1,0:T(8,128)(2,1)}, bf16[416,1024]{1,0:T(8,128)(2,1)}, u32[]{:S(2)}, u32[]{:S(2)}) collective-permute-start(bf16[416,1024]{1,0:T(8,128)(2,1)} %dynamic-slice_convert_fusion.1.refs_1_), channel_id=1, source_target_pairs={{0,1},{1,0},{2,3},{3,2},{4,5},{5,4},{6,7},{7,6},{8,9},{9,8},{10,11... | collective-permute-start | bytes 2555912 | tf_op jit(solution)/shard_map/ppermute | solution.py:597
  239.5 37.2 %copy-start.13 = (s32[16]{0:T(128)}, s32[16]{0:T(128)S(1)}, u32[]{:S(2)}) copy-start(s32[16]{0:T(128)S(1)} %fusion.34.place_ref) | copy-start | bytes 196
  263.5 41.9 %collective-permute-start.10 = (bf16[416,1024]{1,0:T(8,128)(2,1)}, bf16[416,1024]{1,0:T(8,128)(2,1)}, u32[]{:S(2)}, u32[]{:S(2)}) collective-permute-start(bf16[416,1024]{1,0:T(8,128)(2,1)} %get-tuple-element.93), channel_id=1, source_target_pairs={{0,1},{1,0},{2,3},{3,2},{4,5},{5,4},{6,7},{7,6},{8,9},{9,8},{10,11... | collective-permute-start | bytes 2555912 | tf_op jit(solution)/shard_map/ppermute | solution.py:597
  265.1 11.6 %copy-start.11 = (bf16[192,1024]{1,0:T(8,128)(2,1)S(1)}, bf16[192,1024]{1,0:T(8,128)(2,1)}, u32[]{:S(2)}) copy-start(bf16[192,1024]{1,0:T(8,128)(2,1)} %multiply_convert_fusion.1.nb_ref.refs_1_) | copy-start | bytes 1179652
  275.3 24.8 %collective-permute-start.8 = (bf16[192,1024]{1,0:T(8,128)(2,1)}, bf16[192,1024]{1,0:T(8,128)(2,1)}, u32[]{:S(2)}, u32[]{:S(2)}) collective-permute-start(bf16[192,1024]{1,0:T(8,128)(2,1)} %convert_element_type.357), channel_id=1, source_target_pairs={{0,1},{1,0},{2,3},{3,2},{4,5},{5,4},{6,7},{7,6},{8,9},{9,8},{10,11... | collective-permute-start | bytes 1179656 | tf_op jit(solution)/shard_map/ppermute | solution.py:597
  281.3 8.7 %copy-start.14 = (bf16[192,2048]{1,0:T(8,128)(2,1)S(1)}, bf16[192,2048]{1,0:T(8,128)(2,1)}, u32[]{:S(2)}) copy-start(bf16[192,2048]{1,0:T(8,128)(2,1)} %get-tuple-element.44.refs_3_) | copy-start | bytes 2359300
  281.3 8.7 %copy-start.16 = (bf16[832,2048]{1,0:T(8,128)(2,1)S(1)}, bf16[832,2048]{1,0:T(8,128)(2,1)}, u32[]{:S(2)}) copy-start(bf16[832,2048]{1,0:T(8,128)(2,1)} %get-tuple-element.43.refs_2_) | copy-start | bytes 10223620
  290.0 22.0 %collective-permute-start.11 = (bf16[512,2048]{1,0:T(8,128)(2,1)}, bf16[512,2048]{1,0:T(8,128)(2,1)}, u32[]{:S(2)}, u32[]{:S(2)}) collective-permute-start(bf16[512,2048]{1,0:T(8,128)(2,1)} %get-tuple-element.42), channel_id=1, source_target_pairs={{0,2},{2,0},{4,6},{6,4},{8,10},{10,8},{12,14},{14,12},{16,18},{18,... | collective-permute-start | bytes 6291464 | tf_op jit(solution)/shard_map/ppermute | solution.py:658
  315.8 32.8 %collective-permute-start.12 = (bf16[256,2048]{1,0:T(8,128)(2,1)S(1)}, bf16[256,2048]{1,0:T(8,128)(2,1)S(1)}, u32[]{:S(2)}, u32[]{:S(2)}) collective-permute-start(bf16[256,2048]{1,0:T(8,128)(2,1)S(1)} %slice.165), channel_id=1, source_target_pairs={{0,4},{2,6},{4,0},{6,2},{8,12},{10,14},{12,8},{14,10},{16,20},{18,... | collective-permute-start | bytes 3145736 | tf_op jit(solution)/shard_map/ppermute | solution.py:658
  317.8 30.8 %copy-start.37 = (bf16[512,2048]{1,0:T(8,128)(2,1)S(1)}, bf16[512,2048]{1,0:T(8,128)(2,1)}, u32[]{:S(2)}) copy-start(bf16[512,2048]{1,0:T(8,128)(2,1)} %copy-done.36) | copy-start | bytes 6291460
  349.9 11.6 %copy-start.39 = (bf16[2,96,1024]{2,1,0:T(8,128)(2,1)S(1)}, bf16[2,96,1024]{2,1,0:T(8,128)(2,1)}, u32[]{:S(2)}) copy-start(bf16[2,96,1024]{2,1,0:T(8,128)(2,1)} %copy-done.38) | copy-start | bytes 1179652
  349.9 11.7 %copy-start.21 = (bf16[2,416,1024]{2,1,0:T(8,128)(2,1)S(1)}, bf16[2,416,1024]{2,1,0:T(8,128)(2,1)}, u32[]{:S(2)}) copy-start(bf16[2,416,1024]{2,1,0:T(8,128)(2,1)} %copy-done.19) | copy-start | bytes 5111812
  361.3 7.6 %collective-permute-start.13 = (bf16[512,2048]{1,0:T(8,128)(2,1)}, bf16[512,2048]{1,0:T(8,128)(2,1)}, u32[]{:S(2)}, u32[]{:S(2)}) collective-permute-start(bf16[512,2048]{1,0:T(8,128)(2,1)} %get-tuple-element.47), channel_id=1, source_target_pairs={{0,2},{2,0},{4,6},{6,4},{8,10},{10,8},{12,14},{14,12},{16,18},{18,... | collective-permute-start | bytes 6291464 | tf_op jit(solution)/shard_map/ppermute | solution.py:658
  364.4 39.2 %all-to-all-start.2 = ((bf16[4,64,2048]{2,1,0:T(8,128)(2,1)}), bf16[4,64,2048]{2,1,0:T(8,128)(2,1)}, u32[]{:S(2)}, u32[]{:S(2)}) async-start(bf16[4,64,2048]{2,1,0:T(8,128)(2,1)} %bitcast.92), calls=%async_computation.2 | async-start | bytes 2097152 | tf_op jit(solution)/shard_map/all_to_all | solution.py:664
  374.4 32.1 %collective-permute-start.18 = (bf16[256,2048]{1,0:T(8,128)(2,1)}, bf16[256,2048]{1,0:T(8,128)(2,1)}, u32[]{:S(2)}, u32[]{:S(2)}) collective-permute-start(bf16[256,2048]{1,0:T(8,128)(2,1)} %slice.169), channel_id=1, source_target_pairs={{0,4},{2,6},{4,0},{6,2},{8,12},{10,14},{12,8},{14,10},{16,20},{18,... | collective-permute-start | bytes 3145736 | tf_op jit(solution)/shard_map/ppermute | solution.py:658
  383.9 31.7 %collective-permute-start.14 = (bf16[512,1024]{1,0:T(8,128)(2,1)}, bf16[512,1024]{1,0:T(8,128)(2,1)}, u32[]{:S(2)}, u32[]{:S(2)}) collective-permute-start(bf16[512,1024]{1,0:T(8,128)(2,1)} %dynamic-slice_convert_fusion.refs_1_), channel_id=1, source_target_pairs={{0,1},{1,0},{2,3},{3,2},{4,5},{5,4},{6,7},{7,6},{8,9},{9,8},{10,11... | collective-permute-start | bytes 3145736 | tf_op jit(solution)/shard_map/ppermute | solution.py:597
  385.2 21.3 %copy-start.35 = (bf16[512,2048]{1,0:T(8,128)(2,1)S(1)}, bf16[512,2048]{1,0:T(8,128)(2,1)}, u32[]{:S(2)}) copy-start(bf16[512,2048]{1,0:T(8,128)(2,1)} %copy-done.34) | copy-start | bytes 6291460
  385.9 8.4 %collective-permute-start.15 = (f32[6528]{0:T(1024)}, f32[6528]{0:T(1024)S(1)}, u32[]{:S(2)}, u32[]{:S(2)}) collective-permute-start(f32[6528]{0:T(1024)} %after.24), channel_id=1, source_target_pairs={{0,8},{2,10},{4,12},{6,14},{8,0},{10,2},{12,4},{14,6},{16,24},{18,... | collective-permute-start | bytes 78344 | tf_op jit(solution)/shard_map/ppermute | solution.py:739
  395.0 8.6 %collective-permute-start.16 = (f32[6528]{0:T(1024)S(1)}, f32[6528]{0:T(1024)S(1)}, u32[]{:S(2)}, u32[]{:S(2)}) collective-permute-start(f32[6528]{0:T(1024)S(1)} %add.1019), channel_id=1, source_target_pairs={{0,16},{2,18},{4,20},{6,22},{8,24},{10,26},{12,28},{14,30},{16,0},... | collective-permute-start | bytes 78344 | tf_op jit(solution)/shard_map/ppermute | solution.py:739
  403.6 2.2 collective-permute-start.17
  409.1 31.1 %all-to-all-start.1 = ((bf16[4,64,2048]{2,1,0:T(8,128)(2,1)}), bf16[4,64,2048]{2,1,0:T(8,128)(2,1)}, u32[]{:S(2)}, u32[]{:S(2)}) async-start(bf16[4,64,2048]{2,1,0:T(8,128)(2,1)} %bitcast.27), calls=%async_computation.1 | async-start | bytes 2097152 | tf_op jit(solution)/shard_map/all_to_all | solution.py:664
  413.5 9.4 %collective-permute-start.19 = (f32[6528]{0:T(1024)}, f32[6528]{0:T(1024)S(1)}, u32[]{:S(2)}, u32[]{:S(2)}) collective-permute-start(f32[6528]{0:T(1024)} %after.25), channel_id=1, source_target_pairs={{0,1},{1,0},{2,3},{3,2},{4,5},{5,4},{6,7},{7,6},{8,9},{9,8},{10,11... | collective-permute-start | bytes 78344 | tf_op jit(solution)/shard_map/ppermute | solution.py:739
  415.1 15.3 %collective-permute-start.21 = (f32[64,1024]{1,0:T(8,128)}, f32[64,1024]{1,0:T(8,128)S(1)}, u32[]{:S(2)}, u32[]{:S(2)}) collective-permute-start(f32[64,1024]{1,0:T(8,128)} %reduce-scatter.5.cloned.1.call-done), channel_id=1, source_target_pairs={{0,1},{1,0},{2,3},{3,2},{4,5},{5,4},{6,7},{7,6},{8,9},{9,8},{10,11... | collective-permute-start | bytes 786440 | tf_op jit(solution)/shard_map/ppermute | solution.py:597
  423.0 3.9 collective-permute-start.20
  (64 other events, 176.0 us)
Sparse Core Ops, SparseCore 0:
  13.3 67.1 all-gather.3
  83.2 53.2 all-gather.5
  149.8 49.0 all-gather.7
  237.1 70.0 reduce-scatter.4
  311.4 78.4 reduce-scatter.2
